TPU v7x, 128 devices: a whole 4x4x4 slice. The times are simulated.
128 devices in a mesh: dp: 4 (over x), expert: 32 (over y, z, core).
Axes of the slice: x: 4, y: 4, z: 4, core: 2. Of those that a mesh axis runs over, the one named last changes fastest.
Arguments:
- tokens: bfloat16 [16384, 2048], P(('dp', 'expert')), may hold values from -6 to 6
- cotangent: bfloat16 [16384, 2048], P(('dp', 'expert')), may hold values from -6 to 6
- expert_ids: int32 [16384, 8], P(('dp', 'expert')), may hold values from 0 to 63, all different within a row; in each aligned block of 128 rows (0 to 127, 128 to 255, ...) at most 24 rows name the same one
- gate_weights: bfloat16 [16384, 8], P(('dp', 'expert')), may hold values from 0.019897461 to 0.25
- token_counts: int32 [128], P(('dp', 'expert')), may hold values from 64 to 128, as said below
- gate_proj: bfloat16 [64, 2048, 768], P('expert'), may hold values from -0.125 to 0.125
- up_proj: bfloat16 [64, 2048, 768], P('expert'), may hold values from -0.125 to 0.125
- down_proj: bfloat16 [64, 768, 2048], P('expert'), may hold values from -0.21875 to 0.21875
Outputs:
- combined: bfloat16 [16384, 2048], P(('dp', 'expert'))
- tokens_grad: bfloat16 [16384, 2048], P(('dp', 'expert'))
- gates_grad: bfloat16 [16384, 8], P(('dp', 'expert'))
- gate_proj_grad: bfloat16 [64, 2048, 768], P('expert', 'dp')
- up_proj_grad: bfloat16 [64, 2048, 768], P('expert', 'dp')
- down_proj_grad: bfloat16 [64, 768, 2048], P('expert', None, 'dp')
Inputs may be any that keep to these rules, and one draw needn't show every extreme that they name: `expert_ids`: each token names 8 different experts. Within the 128 rows of one device no expert is named by more than 24 rows, a bound that some block reaches. `token_counts`: rows of a device at positions below its count are live, the rest are padding. Some device is full and some holds exactly 64 live rows.
All inputs are finite; a program needn't handle non-finite values.
Results may differ from a plain program's by a relative error of at most 0.013.
Values may be sent and summed in bfloat16 or wider, within the bound.
No kernel may reach another device: no remote copies, remote signals or barrier semaphores. Data moves between devices by JAX's collectives and lax.ppermute only.
A program may use at most 192 MiB of HBM per device.

v0:
```python
import jax
import jax.numpy as jnp
from jax import lax
from jax.sharding import PartitionSpec as P


def silu_parts(pre_gate):
    sigmoid_val = jax.nn.sigmoid(pre_gate)
    return (pre_gate * sigmoid_val, sigmoid_val * (1.0 + pre_gate * (1.0 - sigmoid_val)))


def forward_rows(row_block, gate_mat, up_mat, down_mat):
    pre_gate = jnp.dot(row_block, gate_mat, preferred_element_type=jnp.float32)
    pre_up = jnp.dot(row_block, up_mat, preferred_element_type=jnp.float32)
    activation, derivative = silu_parts(pre_gate)
    hidden = (activation * pre_up).astype(jnp.bfloat16)
    output = jnp.dot(hidden, down_mat, preferred_element_type=jnp.float32).astype(jnp.bfloat16)
    return (pre_gate, pre_up, hidden, output)


def backward_local(pre_gate, pre_up, scaled, gate_mat, up_mat, down_mat):
    contract_last = (((1,), (1,)), ((), ()))
    grad_hidden = lax.dot_general(
        scaled, down_mat, contract_last, preferred_element_type=jnp.float32
    )
    activation, derivative = silu_parts(pre_gate)
    grad_pregate = (grad_hidden * pre_up * derivative).astype(jnp.bfloat16)
    grad_preup = (grad_hidden * activation).astype(jnp.bfloat16)
    input_part = lax.dot_general(
        grad_pregate, gate_mat, contract_last, preferred_element_type=jnp.float32
    )
    input_part = input_part + lax.dot_general(
        grad_preup, up_mat, contract_last, preferred_element_type=jnp.float32
    )
    return (input_part.astype(jnp.bfloat16), grad_pregate, grad_preup)


def weight_grads(packed_tokens, all_pregate, all_preup, all_hidden, all_scaled):
    contract_first = (((0,), (0,)), ((), ()))
    grad_gate = lax.dot_general(
        packed_tokens, all_pregate, contract_first, preferred_element_type=jnp.float32
    )
    grad_up = lax.dot_general(
        packed_tokens, all_preup, contract_first, preferred_element_type=jnp.float32
    )
    grad_down = lax.dot_general(
        all_hidden, all_scaled, contract_first, preferred_element_type=jnp.float32
    )
    return (grad_gate, grad_up, grad_down)


def with_blank(values):
    return jnp.concatenate([values, jnp.zeros((1,) + values.shape[1:], values.dtype)], axis=0)


def place_rows(target_array, piece_rows, first_row):
    return lax.dynamic_update_slice_in_dim(target_array, piece_rows, first_row, 0)


def take_rows(source_array, first_row, block_rows):
    return lax.dynamic_slice_in_dim(source_array, first_row, block_rows, 0)


def slot_layout(expert_ids, live_count, experts_total, capacity):
    tok_dev, per_token = expert_ids.shape
    position = lax.broadcasted_iota(jnp.int32, (tok_dev, per_token), 0).reshape(-1)
    is_live = position < live_count
    flat_ids = expert_ids.reshape(-1)
    labels = jnp.arange(experts_total, dtype=jnp.int32)
    onehot = ((flat_ids[:, None] == labels[None, :]) & is_live[:, None]).astype(jnp.int32)
    running = jnp.cumsum(onehot, axis=0)
    ranking = jnp.sum(running * onehot, axis=1) - 1
    return jnp.where(is_live, flat_ids * capacity + ranking, experts_total * capacity)


def pack_plan(arrived, capacity, packed_len):
    sources = arrived.shape[0]
    offsets = jnp.cumsum(arrived) - arrived
    arrived_total = jnp.sum(arrived)
    packed_place = jnp.arange(packed_len, dtype=jnp.int32)
    source = jnp.sum((packed_place[:, None] >= offsets[None, 1:]).astype(jnp.int32), axis=1)
    first_place = jnp.take(offsets, source)
    gather_at = jnp.where(
        packed_place < arrived_total,
        source * capacity + packed_place - first_place,
        sources * capacity,
    )
    column = jnp.arange(capacity, dtype=jnp.int32)
    return_at = jnp.where(
        column[None, :] < arrived[:, None], offsets[:, None] + column[None, :], packed_len
    )
    return (gather_at, return_at.reshape(-1), arrived_total)


def forward_pass(packed_tokens, arrived_total, gate_mat, up_mat, down_mat):
    block_rows = 256
    packed_len, model_dim = packed_tokens.shape
    hidden_dim = gate_mat.shape[1]
    blocks = (arrived_total + block_rows - 1) // block_rows

    def forward_one_block(block_index, carried):
        outputs, pre_gates, pre_ups = carried
        first_row = block_index * block_rows
        row_block = take_rows(packed_tokens, first_row, block_rows)
        pre_gate, pre_up, hidden, output = forward_rows(row_block, gate_mat, up_mat, down_mat)
        return (
            place_rows(outputs, output, first_row),
            place_rows(pre_gates, pre_gate, first_row),
            place_rows(pre_ups, pre_up, first_row),
        )

    start_carry = (
        jnp.zeros((packed_len, model_dim), jnp.bfloat16),
        jnp.zeros((packed_len, hidden_dim), jnp.float32),
        jnp.zeros((packed_len, hidden_dim), jnp.float32),
    )
    return lax.fori_loop(0, blocks, forward_one_block, start_carry)


def backward_pass(
    packed_tokens, pre_gates, pre_ups, packed_scaled, arrived_total, gate_mat, up_mat, down_mat
):
    block_rows = 256
    packed_len, model_dim = packed_tokens.shape
    hidden_dim = gate_mat.shape[1]
    blocks = (arrived_total + block_rows - 1) // block_rows

    def backward_one_block(block_index, carried):
        input_parts, all_pregate, all_preup, all_hidden = carried
        first_row = block_index * block_rows
        pre_gate = take_rows(pre_gates, first_row, block_rows)
        pre_up = take_rows(pre_ups, first_row, block_rows)
        scaled = take_rows(packed_scaled, first_row, block_rows)
        activation, derivative = silu_parts(pre_gate)
        hidden = (activation * pre_up).astype(jnp.bfloat16)
        input_part, grad_pregate, grad_preup = backward_local(
            pre_gate, pre_up, scaled, gate_mat, up_mat, down_mat
        )
        return (
            place_rows(input_parts, input_part, first_row),
            place_rows(all_pregate, grad_pregate, first_row),
            place_rows(all_preup, grad_preup, first_row),
            place_rows(all_hidden, hidden, first_row),
        )

    start_carry = (
        jnp.zeros((packed_len, model_dim), jnp.bfloat16),
        jnp.zeros((packed_len, hidden_dim), jnp.bfloat16),
        jnp.zeros((packed_len, hidden_dim), jnp.bfloat16),
        jnp.zeros((packed_len, hidden_dim), jnp.bfloat16),
    )
    input_parts, all_pregate, all_preup, all_hidden = lax.fori_loop(
        0, blocks, backward_one_block, start_carry
    )
    grad_gate, grad_up, grad_down = weight_grads(
        packed_tokens, all_pregate, all_preup, all_hidden, packed_scaled
    )
    return (input_parts, grad_gate, grad_up, grad_down)


def local(tokens, cotangent, expert_ids, gate_weights, token_counts, gate_proj, up_proj, down_proj):
    block_rows = 256
    group_size = lax.axis_size("expert")
    local_experts, model_dim, hidden_dim = gate_proj.shape
    tok_dev, per_token = expert_ids.shape
    experts_total = group_size * local_experts
    capacity = 3 * tok_dev * per_token // (2 * experts_total)
    slots_total = experts_total * capacity
    packed_len = -(-(group_size * capacity) // block_rows) * block_rows
    pair_count = tok_dev * per_token
    target = slot_layout(expert_ids, token_counts[0], experts_total, capacity)
    pair_of_slot = (
        jnp.full((slots_total + 1,), pair_count, jnp.int32)
        .at[target]
        .set(jnp.arange(pair_count, dtype=jnp.int32))[:slots_total]
    )
    token_of_slot = pair_of_slot // per_token
    slot_tokens = with_blank(tokens)[token_of_slot].reshape(
        group_size, local_experts, capacity, model_dim
    )
    slot_gates = with_blank(gate_weights.reshape(-1))[pair_of_slot].reshape(
        group_size, local_experts, capacity
    )

    def collect(returned):
        flat_rows = with_blank(returned.reshape((slots_total,) + returned.shape[3:]))
        return flat_rows[target].reshape((tok_dev, per_token) + returned.shape[3:])

    def unpack(packed, return_at):
        return with_blank(packed)[return_at].reshape((group_size, capacity) + packed.shape[1:])

    def pack(arrived_rows, gather_at):
        return with_blank(arrived_rows.reshape((group_size * capacity,) + arrived_rows.shape[2:]))[
            gather_at
        ]

    gradient_sets = []
    got_tokens, got_gates = (
        lax.all_to_all(slot_tokens, "expert", split_axis=0, concat_axis=0, tiled=True),
        lax.all_to_all(slot_gates, "expert", split_axis=0, concat_axis=0, tiled=True),
    )
    pack_plans = []
    saved_rows = []
    slot_outputs = []
    for local_index in range(local_experts):
        arrived = jnp.sum((got_gates[:, local_index] > 0).astype(jnp.int32), axis=1)
        gather_at, return_at, arrived_total = pack_plan(arrived, capacity, packed_len)
        packed_tokens = pack(got_tokens[:, local_index], gather_at)
        outputs, pre_gates, pre_ups = forward_pass(
            packed_tokens,
            arrived_total,
            gate_proj[local_index],
            up_proj[local_index],
            down_proj[local_index],
        )
        pack_plans.append((gather_at, return_at, arrived_total))
        saved_rows.append((packed_tokens, pre_gates, pre_ups))
        slot_outputs.append(unpack(outputs, return_at))
    back_outputs = lax.all_to_all(
        jnp.stack(slot_outputs, axis=1), "expert", split_axis=0, concat_axis=0, tiled=True
    )
    pair_outputs = collect(back_outputs)
    gates_grad = jnp.einsum(
        "tkd,td->tk", pair_outputs, cotangent, preferred_element_type=jnp.float32
    ).astype(jnp.bfloat16)
    scaled_pairs = (
        gate_weights.astype(jnp.float32)[:, :, None] * cotangent.astype(jnp.float32)[:, None, :]
    ).astype(jnp.bfloat16)
    slot_scaled = with_blank(scaled_pairs.reshape(pair_count, model_dim))[pair_of_slot].reshape(
        group_size, local_experts, capacity, model_dim
    )
    got_scaled = lax.all_to_all(slot_scaled, "expert", split_axis=0, concat_axis=0, tiled=True)
    slot_parts = []
    for local_index in range(local_experts):
        gather_at, return_at, arrived_total = pack_plans[local_index]
        packed_tokens, pre_gates, pre_ups = saved_rows[local_index]
        input_parts, acc_gate, acc_up, acc_down = backward_pass(
            packed_tokens,
            pre_gates,
            pre_ups,
            pack(got_scaled[:, local_index], gather_at),
            arrived_total,
            gate_proj[local_index],
            up_proj[local_index],
            down_proj[local_index],
        )
        slot_parts.append(unpack(input_parts, return_at))
        gradient_sets.append((acc_gate, acc_up, acc_down))
    back_parts = lax.all_to_all(
        jnp.stack(slot_parts, axis=1), "expert", split_axis=0, concat_axis=0, tiled=True
    )
    pair_parts = collect(back_parts)
    combined = jnp.einsum(
        "tk,tkd->td", gate_weights, pair_outputs, preferred_element_type=jnp.float32
    ).astype(jnp.bfloat16)
    tokens_grad = jnp.sum(pair_parts, axis=1, dtype=jnp.float32).astype(jnp.bfloat16)
    stack_gate = jnp.stack([gradients[0] for gradients in gradient_sets]).astype(jnp.bfloat16)
    stack_up = jnp.stack([gradients[1] for gradients in gradient_sets]).astype(jnp.bfloat16)
    stack_down = jnp.stack([gradients[2] for gradients in gradient_sets]).astype(jnp.bfloat16)
    reduced_gate, reduced_up, reduced_down = (
        lax.psum_scatter(stack_gate, "dp", scatter_dimension=1, tiled=True).astype(jnp.float32),
        lax.psum_scatter(stack_up, "dp", scatter_dimension=1, tiled=True).astype(jnp.float32),
        lax.psum_scatter(stack_down, "dp", scatter_dimension=2, tiled=True).astype(jnp.float32),
    )
    return (
        combined,
        tokens_grad,
        gates_grad,
        reduced_gate.astype(jnp.bfloat16),
        reduced_up.astype(jnp.bfloat16),
        reduced_down.astype(jnp.bfloat16),
    )


def solution(mesh):
    placed = (
        P(("dp", "expert"), None),
        P(("dp", "expert"), None),
        P(("dp", "expert"), None),
        P(("dp", "expert"), None),
        P(("dp", "expert")),
        P("expert", None, None),
        P("expert", None, None),
        P("expert", None, None),
    )
    return jax.shard_map(
        local,
        mesh=mesh,
        in_specs=placed,
        out_specs=(
            P(("dp", "expert"), None),
            P(("dp", "expert"), None),
            P(("dp", "expert"), None),
            P("expert", "dp", None),
            P("expert", "dp", None),
            P("expert", None, "dp"),
        ),
        check_vma=False,
    )
```

profile of v0, /device:TPU:32, one launch (start us, length us, event | category | flops | bytes accessed | tf_op | source)
XLA Modules:
  0.0 704.4 jit_solution(5811447026581188775)
XLA Ops:
  9.8 18.0 %reduce-window.24 = s32[64,8,128]{2,1,0:T(8,128)S(1)} reduce-window(s32[64,8,128]{2,1,0:T(8,128)S(1)} %fusion.48, s32[]{:T(128)} %constant.119.clone.1), window={size=1x1x128 pad=0_0x0_0x127_0}, to_apply=%region_0.0 | reduce-window | flops 8323072 | bytes 524292 | tf_op jit(solution)/shard_map/reduce-window
  28.7 4.3 scatter_custom_fusion
  34.0 9.5 %gather_fusion = bf16[1536]{0:T(1024)(128)(2,1)S(1)} fusion(bf16[1025]{0:T(1024)(128)(2,1)S(1)} %pad_maximum_fusion.5, s32[2048]{0:T(1024)S(1)} %get-tuple-element.440), kind=kCustom, calls=%fused_computation | custom fusion | bytes 12288 | tf_op jit(solution)/shard_map/gather | solution.py:181
  44.2 8.2 %all-to-all-start = ((bf16[32,2,24]{2,1,0:T(2,128)(2,1)}), bf16[32,2,24]{2,1,0:T(2,128)(2,1)S(1)}, u32[]{:S(2)}, u32[]{:S(2)}) async-start(bf16[32,2,24]{2,1,0:T(2,128)(2,1)} %reshape.292), calls=%async_computation | async-start | bytes 32768 | tf_op jit(solution)/shard_map/all_to_all | solution.py:200
  53.5 2.3 concatenate.46
  55.8 15.4 %gather_fusion.7 = bf16[1536,2048]{1,0:T(8,128)(2,1)} fusion(bf16[1025,2048]{1,0:T(8,128)(2,1)} %concatenate.46, s32[2048]{0:T(1024)S(1)} %get-tuple-element.440), kind=kCustom, calls=%fused_computation.7 | custom fusion | bytes 12589056 | tf_op jit(solution)/shard_map/gather | solution.py:229
  71.3 7.6 %all-to-all-start.3 = ((bf16[32,2,24,2048]{3,2,1,0:T(8,128)(2,1)}), bf16[32,2,24,2048]{3,2,1,0:T(8,128)(2,1)}, u32[]{:S(2)}, u32[]{:S(2)}) async-start(bf16[32,2,24,2048]{3,2,1,0:T(8,128)(2,1)} %bitcast.209), calls=%async_computation.3 | async-start | bytes 12582912 | tf_op jit(solution)/shard_map/all_to_all | solution.py:232
  78.9 7.1 %gather_fusion.1 = bf16[1536,2048]{1,0:T(8,128)(2,1)} fusion(bf16[129,2048]{1,0:T(8,128)(2,1)S(1)} %concatenate.40, s32[2048]{0:T(1024)S(1)} %get-tuple-element.439), kind=kCustom, calls=%fused_computation.1 | custom fusion | bytes 12589056 | tf_op jit(solution)/shard_map/gather | solution.py:178
  86.0 80.4 %all-to-all-done.3 = bf16[32,2,24,2048]{3,2,1,0:T(8,128)(2,1)} async-done(((bf16[32,2,24,2048]{3,2,1,0:T(8,128)(2,1)}), bf16[32,2,24,2048]{3,2,1,0:T(8,128)(2,1)}, u32[]{:S(2)}, u32[]{:S(2)}) %all-to-all-start.3) | async-done | bytes 6291488 | tf_op jit(solution)/shard_map/all_to_all | solution.py:232
  166.4 5.0 all-to-all-start.1
  171.7 6.6 slice_bitcast_fusion.3
  178.2 8.6 %slice_bitcast_fusion.4 = (bf16[2048,768]{1,0:T(8,128)(2,1)}, bf16[2048,768]{1,0:T(8,128)(2,1)S(1)}, bf16[2048,768]{1,0:T(8,128)(2,1)}, bf16[2048,768]{1,0:T(8,128)(2,1)}) fusion(bf16[2,2048,768]{2,1,0:T(8,128)(2,1)} %param.24, bf16[2,2048,768]{2,1,0:T(8,128)(2,1)} %param.23), kind=kLoop, calls=%fused_computation.90 | loop fusion | bytes 25165824 | tf_op jit(solution)/shard_map/squeeze | solution.py:213
  192.2 20.6 %compare_select_fusion.7 = s32[768]{0:T(1024)S(1)} fusion(s32[768]{0:T(1024)S(1)} %convert_reduce_fusion.1, s32[]{:T(128)} %bitcast.39, s32[]{:T(128)} %bitcast.38, s32[]{:T(128)} %bitcast.37, s32[]{:T(128)} %bitcast.36, s32[]{:T(128)} %bitcast.35, s32[]{:T(128)} %bitcast.34, s32[]{:T(128)} %bitcast.33, s32[]{:T(128)} %bitcast.32, s32[]{:T(128)} %bitcast.31, ...), kind=kLoop, calls=%fused_computation.132 | loop fusion | flops 59136 | bytes 6276 | tf_op jit(solution)/shard_map/select_n | solution.py:193
  214.3 20.6 %compare_select_fusion.6 = s32[768]{0:T(1024)S(1)} fusion(s32[768]{0:T(1024)S(1)} %convert_reduce_fusion, s32[]{:T(128)} %bitcast.78, s32[]{:T(128)} %bitcast.77, s32[]{:T(128)} %bitcast.76, s32[]{:T(128)} %bitcast.75, s32[]{:T(128)} %bitcast.74, s32[]{:T(128)} %bitcast.73, s32[]{:T(128)} %bitcast.72, s32[]{:T(128)} %bitcast.71, s32[]{:T(128)} %bitcast.70, ...), kind=kLoop, calls=%fused_computation.131 | loop fusion | flops 59136 | bytes 6276 | tf_op jit(solution)/shard_map/select_n | solution.py:193
  235.0 5.4 fusion.67
  242.3 9.4 %gather_fusion.8 = bf16[768,2048]{1,0:T(8,128)(2,1)} fusion(bf16[769,2048]{1,0:T(8,128)(2,1)} %concatenate.47, s32[1024]{0:T(1024)S(1)} %pad_clamp_fusion.5), kind=kCustom, calls=%fused_computation.8 | custom fusion | bytes 6294528 | tf_op jit(solution)/shard_map/gather | solution.py:193
  251.7 7.2 %all-to-all-done.1 = bf16[32,2,24,2048]{3,2,1,0:T(8,128)(2,1)} async-done(((bf16[32,2,24,2048]{3,2,1,0:T(8,128)(2,1)}), bf16[32,2,24,2048]{3,2,1,0:T(8,128)(2,1)}, u32[]{:S(2)}, u32[]{:S(2)}) %all-to-all-start.1) | async-done | bytes 6291488 | tf_op jit(solution)/shard_map/all_to_all | solution.py:199
  259.0 5.5 fusion.68
  266.4 9.4 %gather_fusion.2 = bf16[768,2048]{1,0:T(8,128)(2,1)} fusion(bf16[769,2048]{1,0:T(8,128)(2,1)} %concatenate.41, s32[1024]{0:T(1024)S(1)} %pad_clamp_fusion.5), kind=kCustom, calls=%fused_computation.2 | custom fusion | bytes 6294528 | tf_op jit(solution)/shard_map/gather | solution.py:193
  281.0 19.4 %while.60 = (s32[]{:T(128)}, bf16[768,2048]{1,0:T(8,128)(2,1)}, f32[768,768]{1,0:T(8,128)}, f32[768,768]{1,0:T(8,128)}, s32[]{:T(128)}, /*index=5*/bf16[768,2048...) while((s32[]{:T(128)}, bf16[768,2048]{1,0:T(8,128)(2,1)}, ...), condition=%wide.region_9.11_spmd, body=%wide.region_8.10_spmd.sunk | while | flops 2417623040 | bytes 42469604 | solution.py:117
  281.4 4.2 constant_dynamic-update-slice_fusion.14
  285.6 3.3 constant_dynamic-update-slice_fusion.15
  290.9 4.2 constant_dynamic-update-slice_fusion.14
  295.1 3.3 constant_dynamic-update-slice_fusion.15
  305.8 18.0 %while.62 = (s32[]{:T(128)}, bf16[768,2048]{1,0:T(8,128)(2,1)}, bf16[768,768]{1,0:T(8,128)(2,1)}, bf16[768,768]{1,0:T(8,128)(2,1)}, bf16[768,768]{1,0:T(8,128)(2...) while((s32[]{:T(128)}, bf16[768,2048]{1,0:T(8,128)(2,1)}, ...), condition=%wide.region_17.19_spmd, body=%wide.region_16.18_spmd.sunk | while | flops 2419916800 | bytes 45221116 | solution.py:152
  305.9 5.1 constant_dynamic-update-slice_fusion.18
  314.8 5.0 constant_dynamic-update-slice_fusion.18
  323.8 6.7 fusion.41
  330.5 2.1 concatenate.49
  332.6 9.4 %gather_fusion.10 = bf16[768,2048]{1,0:T(8,128)(2,1)} fusion(bf16[769,2048]{1,0:T(8,128)(2,1)} %concatenate.49, s32[1024]{0:T(1024)S(1)} %pad_clamp_fusion.3), kind=kCustom, calls=%fused_computation.10 | custom fusion | bytes 6294528 | tf_op jit(solution)/shard_map/gather | solution.py:193
  342.1 4.0 concatenate.43
  346.1 9.4 %gather_fusion.4 = bf16[768,2048]{1,0:T(8,128)(2,1)} fusion(bf16[769,2048]{1,0:T(8,128)(2,1)} %concatenate.43, s32[1024]{0:T(1024)S(1)} %pad_clamp_fusion.3), kind=kCustom, calls=%fused_computation.4 | custom fusion | bytes 6294528 | tf_op jit(solution)/shard_map/gather | solution.py:193
  360.8 8.6 %while.61 = (s32[]{:T(128)}, bf16[768,2048]{1,0:T(8,128)(2,1)}, f32[768,768]{1,0:T(8,128)}, f32[768,768]{1,0:T(8,128)}, s32[]{:T(128)}, /*index=5*/bf16[768,2048...) while((s32[]{:T(128)}, bf16[768,2048]{1,0:T(8,128)(2,1)}, ...), condition=%wide.region_15.17_spmd, body=%wide.region_14.16_spmd.sunk | while | flops 2417623040 | bytes 42469604 | solution.py:117
  360.8 3.3 constant_dynamic-update-slice_fusion.16
  364.1 3.3 constant_dynamic-update-slice_fusion.17
  374.7 8.3 %while.63 = (s32[]{:T(128)}, bf16[768,2048]{1,0:T(8,128)(2,1)}, bf16[768,768]{1,0:T(8,128)(2,1)}, bf16[768,768]{1,0:T(8,128)(2,1)}, bf16[768,768]{1,0:T(8,128)(2...) while((s32[]{:T(128)}, bf16[768,2048]{1,0:T(8,128)(2,1)}, ...), condition=%wide.region_19.21_spmd, body=%wide.region_18.20_spmd.sunk | while | flops 2419916800 | bytes 32638180 | solution.py:152
  374.9 5.0 constant_dynamic-update-slice_fusion.19
  383.0 5.0 fusion.42
  388.0 3.2 pad_maximum_fusion.4
  393.1 4.3 fusion.39
  397.5 2.9 fusion.40
  400.4 3.2 pad_maximum_fusion.3
  404.7 2.1 concatenate.48
  406.9 4.3 gather_fusion.9
  413.3 4.3 gather_fusion.11
  417.6 6.0 pad_maximum_fusion.1
  423.6 55.2 %all-to-all-start.4 = ((bf16[32,2,24,2048]{3,2,1,0:T(8,128)(2,1)}), bf16[32,2,24,2048]{3,2,1,0:T(8,128)(2,1)}, u32[]{:S(2)}, u32[]{:S(2)}) async-start(bf16[32,2,24,2048]{3,2,1,0:T(8,128)(2,1)} %pad_maximum_fusion.1), calls=%async_computation.4 | async-start | bytes 12582912 | tf_op jit(solution)/shard_map/all_to_all | solution.py:249
  479.2 4.3 fusion.37
  483.6 2.9 fusion.38
  486.5 3.2 pad_maximum_fusion.2
  489.8 2.2 concatenate.42
  492.0 4.3 gather_fusion.3
  498.5 4.4 gather_fusion.5
  502.9 6.1 pad_maximum_fusion
  509.0 61.0 %all-to-all-done.4 = bf16[32,2,24,2048]{3,2,1,0:T(8,128)(2,1)} async-done(((bf16[32,2,24,2048]{3,2,1,0:T(8,128)(2,1)}), bf16[32,2,24,2048]{3,2,1,0:T(8,128)(2,1)}, u32[]{:S(2)}, u32[]{:S(2)}) %all-to-all-start.4) | async-done | bytes 6291488 | tf_op jit(solution)/shard_map/all_to_all | solution.py:249
  570.0 7.5 %all-to-all-start.2 = ((bf16[32,2,24,2048]{3,2,1,0:T(8,128)(2,1)}), bf16[32,2,24,2048]{3,2,1,0:T(8,128)(2,1)}, u32[]{:S(2)}, u32[]{:S(2)}) async-start(bf16[32,2,24,2048]{3,2,1,0:T(8,128)(2,1)} %pad_maximum_fusion), calls=%async_computation.2 | async-start | bytes 12582912 | tf_op jit(solution)/shard_map/all_to_all | solution.py:219
  577.6 6.8 concatenate.51
  584.5 12.4 %gather_fusion.12 = bf16[1024,2048]{1,0:T(8,128)(2,1)} fusion(bf16[1537,2048]{1,0:T(8,128)(2,1)} %concatenate.51, s32[1024]{0:T(1024)S(1)} %broadcast_clamp_fusion), kind=kCustom, calls=%fused_computation.12 | custom fusion | bytes 8392704 | tf_op jit(solution)/shard_map/gather | solution.py:187
  596.9 67.5 %all-to-all-done.2 = bf16[32,2,24,2048]{3,2,1,0:T(8,128)(2,1)} async-done(((bf16[32,2,24,2048]{3,2,1,0:T(8,128)(2,1)}), bf16[32,2,24,2048]{3,2,1,0:T(8,128)(2,1)}, u32[]{:S(2)}, u32[]{:S(2)}) %all-to-all-start.2) | async-done | bytes 6291488 | tf_op jit(solution)/shard_map/all_to_all | solution.py:219
  664.4 6.6 concatenate.45
  671.0 12.4 %gather_fusion.6 = bf16[1024,2048]{1,0:T(8,128)(2,1)} fusion(bf16[1537,2048]{1,0:T(8,128)(2,1)} %concatenate.45, s32[1024]{0:T(1024)S(1)} %broadcast_clamp_fusion), kind=kCustom, calls=%fused_computation.6 | custom fusion | bytes 8392704 | tf_op jit(solution)/shard_map/gather | solution.py:187
  683.4 3.6 fusion.35
  688.1 2.7 fusion.33
  691.5 5.9 bitcast_reduce_fusion
  (167 shorter events, 62.7 us)
Async XLA Ops:
  27.9 24.6 %copy-start.20 = (bf16[128,2048]{1,0:T(8,128)(2,1)S(1)}, bf16[128,2048]{1,0:T(8,128)(2,1)}, u32[]{:S(2)}) copy-start(bf16[128,2048]{1,0:T(8,128)(2,1)} %param.19) | copy-start | bytes 1572868
  28.7 5.3 copy-start.23
  44.2 27.1 %all-to-all-start = ((bf16[32,2,24]{2,1,0:T(2,128)(2,1)}), bf16[32,2,24]{2,1,0:T(2,128)(2,1)S(1)}, u32[]{:S(2)}, u32[]{:S(2)}) async-start(bf16[32,2,24]{2,1,0:T(2,128)(2,1)} %reshape.292), calls=%async_computation | async-start | bytes 32768 | tf_op jit(solution)/shard_map/all_to_all | solution.py:200
  71.3 7.6 %copy-start.22 = (bf16[128,2048]{1,0:T(8,128)(2,1)S(1)}, bf16[128,2048]{1,0:T(8,128)(2,1)}, u32[]{:S(2)}) copy-start(bf16[128,2048]{1,0:T(8,128)(2,1)} %param.18) | copy-start | bytes 1572868
  71.3 95.2 %all-to-all-start.3 = ((bf16[32,2,24,2048]{3,2,1,0:T(8,128)(2,1)}), bf16[32,2,24,2048]{3,2,1,0:T(8,128)(2,1)}, u32[]{:S(2)}, u32[]{:S(2)}) async-start(bf16[32,2,24,2048]{3,2,1,0:T(8,128)(2,1)} %bitcast.209), calls=%async_computation.3 | async-start | bytes 12582912 | tf_op jit(solution)/shard_map/all_to_all | solution.py:232
  166.4 92.6 %all-to-all-start.1 = ((bf16[32,2,24,2048]{3,2,1,0:T(8,128)(2,1)}), bf16[32,2,24,2048]{3,2,1,0:T(8,128)(2,1)}, u32[]{:S(2)}, u32[]{:S(2)}) async-start(bf16[32,2,24,2048]{3,2,1,0:T(8,128)(2,1)} %bitcast.208), calls=%async_computation.1 | async-start | bytes 12582912 | tf_op jit(solution)/shard_map/all_to_all | solution.py:199
  171.4 526.0 %reduce-scatter.8.cloned.1.call-start = ((), (), s32[]{:S(2)}) async-start(), calls=%async_computation.10 | async-start | bytes 7864320 | tf_op jit(solution)/shard_map/reduce_scatter | solution.py:263
  188.6 1.7 copy-start.28
  188.6 51.8 %copy-start.26 = (s32[32]{0:T(128)}, s32[32]{0:T(128)S(1)}, u32[]{:S(2)}) copy-start(s32[32]{0:T(128)S(1)} %get-tuple-element.254) | copy-start | bytes 388
  190.2 50.2 %copy-start.16 = (s32[32]{0:T(128)}, s32[32]{0:T(128)S(1)}, u32[]{:S(2)}) copy-start(s32[32]{0:T(128)S(1)} %sub.60) | copy-start | bytes 388
  190.6 49.9 %copy-start.18 = (s32[32]{0:T(128)}, s32[32]{0:T(128)S(1)}, u32[]{:S(2)}) copy-start(s32[32]{0:T(128)S(1)} %sub.64) | copy-start | bytes 388
  281.4 4.2 copy-start.3
  285.6 3.3 copy-start.12
  290.9 4.2 copy-start.3
  295.1 3.3 copy-start.12
  305.8 5.1 copy-start.4
  310.9 1.9 copy-start
  314.8 5.0 copy-start.4
  319.8 1.9 copy-start
  323.8 6.7 copy-start.10
  360.8 3.3 copy-start.1
  364.1 3.3 copy-start.11
  374.9 5.1 copy-start.2
  383.0 5.0 copy-start.13
  391.2 1.9 copy-start.5
  391.3 306.1 %reduce-scatter.6.cloned.1.call-start = ((), (), s32[]{:S(2)}) async-start(), calls=%async_computation.9 | async-start | bytes 7864320 | tf_op jit(solution)/shard_map/reduce_scatter | solution.py:262
  393.1 4.3 copy-start.7
  393.1 4.3 copy-start.15
  403.6 0.7 copy-start.17
  403.6 0.7 copy-start.29
  403.6 0.8 copy-start.19
  403.6 0.8 copy-start.27
  423.6 55.6 %copy-start.6 = (bf16[768,2048]{1,0:T(8,128)(2,1)S(1)}, bf16[768,2048]{1,0:T(8,128)(2,1)}, u32[]{:S(2)}) copy-start(bf16[768,2048]{1,0:T(8,128)(2,1)} %get-tuple-element.920) | copy-start | bytes 9437188
  423.6 146.3 %all-to-all-start.4 = ((bf16[32,2,24,2048]{3,2,1,0:T(8,128)(2,1)}), bf16[32,2,24,2048]{3,2,1,0:T(8,128)(2,1)}, u32[]{:S(2)}, u32[]{:S(2)}) async-start(bf16[32,2,24,2048]{3,2,1,0:T(8,128)(2,1)} %pad_maximum_fusion.1), calls=%async_computation.4 | async-start | bytes 12582912 | tf_op jit(solution)/shard_map/all_to_all | solution.py:249
  478.9 218.5 %reduce-scatter.4.cloned.1.call-start = ((), (), s32[]{:S(2)}) async-start(), calls=%async_computation.8 | async-start | bytes 7864320 | tf_op jit(solution)/shard_map/reduce_scatter | solution.py:261
  479.2 4.4 copy-start.8
  479.2 4.4 copy-start.14
  509.0 68.5 %copy-start.25 = (bf16[128,8]{0,1:T(8,128)(2,1)S(1)}, bf16[128,8]{0,1:T(8,128)(2,1)}, u32[]{:S(2)}) copy-start(bf16[128,8]{0,1:T(8,128)(2,1)} %param.21) | copy-start | bytes 6148
  509.0 68.6 %copy-start.24 = (s32[1024,1]{0,1:T(1,128)S(1)}, s32[1024,1]{0,1:T(1,128)}, u32[]{:S(2)}) copy-start(s32[1024,1]{0,1:T(1,128)} %copy-done.23) | copy-start | bytes 12292
  570.0 94.4 %all-to-all-start.2 = ((bf16[32,2,24,2048]{3,2,1,0:T(8,128)(2,1)}), bf16[32,2,24,2048]{3,2,1,0:T(8,128)(2,1)}, u32[]{:S(2)}, u32[]{:S(2)}) async-start(bf16[32,2,24,2048]{3,2,1,0:T(8,128)(2,1)} %pad_maximum_fusion), calls=%async_computation.2 | async-start | bytes 12582912 | tf_op jit(solution)/shard_map/all_to_all | solution.py:219
  683.4 4.7 copy-start.9
  683.4 4.7 copy-start.21
Sparse Core Ops, SparseCore 0:
  391.4 112.2 reduce-scatter.7
  506.6 63.6 reduce-scatter.5
  573.3 63.6 reduce-scatter.3
where the time goes:
time: 711 us; the launch traced here: 704 us
  waiting for transfers between devices  216 us (30%)
  local copies, waits for them, and re-layouts  211 us (30%)
  other arithmetic  91.5 us (13%)
  matrix products  84.5 us (12%)
  starting transfers between devices  84.3 us (12%)
  between operations  16.7 us (2%)
    all_to_all x1, waiting for transfers between devices, local(): lax.all_to_all(slot_scaled, 'expert', split_axis=0, concat_axis=0, tiled=...  80.4 us
    all_to_all x1, waiting for transfers between devices, local(): lax.all_to_all(jnp.stack(slot_outputs, axis=1), 'expert', split_axis=0, c...  67.5 us
    all_to_all x1, waiting for transfers between devices, local(): lax.all_to_all(jnp.stack(slot_parts, axis=1), 'expert', split_axis=0, con...  61 us
    all_to_all x1, starting transfers between devices, local(): lax.all_to_all(jnp.stack(slot_parts, axis=1), 'expert', split_axis=0, con...  55.2 us
    select_n x2, other arithmetic, pack(): with_blank(arrived_rows.reshape((group_size * capacity,) + arrived_rows.s...  41.3 us
    gather x4, local copies, waits for them, and re-layouts, pack(): with_blank(arrived_rows.reshape((group_size * capacity,) + arrived_rows.s...  37.7 us
    concatenate x12, local copies, waits for them, and re-layouts, with_blank(): jnp.concatenate([values, jnp.zeros((1,) + values.shape[1:], values.dtype)...  34.3 us
    gather x2, local copies, waits for them, and re-layouts, collect(): return flat_rows[target].reshape((tok_dev, per_token) + returned.shape[3:])  24.9 us
  transfers between devices with their start and end apart: 8, of which 4 were waited for; matrix products, arithmetic and copies ran while one was open for 31% of the time, Pallas kernels for 0%

commit v1 on v0

v1 whole, which is shorter than its diff:
```python
import jax
import jax.numpy as jnp
from jax import lax
from jax.sharding import PartitionSpec as P

F32 = jnp.float32
BF16 = jnp.bfloat16
CONTRACT_FIRST = (((0,), (0,)), ((), ()))
CONTRACT_LAST = (((1,), (1,)), ((), ()))


def dot(a, b, dims=(((1,), (0,)), ((), ()))):
    return lax.dot_general(a, b, dims, preferred_element_type=F32)


def silu_parts(pre_gate):
    s = jax.nn.sigmoid(pre_gate)
    return pre_gate * s, s * (1.0 + pre_gate * (1.0 - s))


def slot_masks(expert_ids, gate_weights, live_count, experts_total, capacity):
    tok_dev = expert_ids.shape[0]
    live = lax.broadcasted_iota(jnp.int32, (experts_total, tok_dev), 1) < live_count
    labels = lax.broadcasted_iota(jnp.int32, (experts_total, 1, tok_dev), 0)
    hits = expert_ids.T[None] == labels
    names = jnp.any(hits, axis=1) & live
    gates = jnp.sum(jnp.where(hits, gate_weights.T[None].astype(F32), 0.0), axis=1)
    before = (
        lax.broadcasted_iota(jnp.int32, (tok_dev, tok_dev), 0)
        < lax.broadcasted_iota(jnp.int32, (tok_dev, tok_dev), 1)
    )
    rank = dot(names.astype(BF16), before.astype(BF16)).astype(jnp.int32)
    column = lax.broadcasted_iota(jnp.int32, (1, capacity, 1), 1)
    mask = names[:, None, :] & (rank[:, None, :] == column)
    return mask, gates


def exchange(rows, group):
    rows = rows.reshape(group, -1, rows.shape[-1])
    got = lax.all_to_all(rows, "expert", split_axis=0, concat_axis=0, tiled=True)
    return got.reshape(-1, rows.shape[-1])


def local(tokens, cotangent, expert_ids, gate_weights, token_counts, gate_proj, up_proj, down_proj):
    group = lax.axis_size("expert")
    local_experts, model_dim, hidden_dim = gate_proj.shape
    tok_dev, per_token = expert_ids.shape
    experts_total = group * local_experts
    capacity = 3 * tok_dev * per_token // (2 * experts_total)
    rows = group * capacity

    mask, gates = slot_masks(expert_ids, gate_weights, token_counts[0], experts_total, capacity)
    by_expert = mask.reshape(group, local_experts, capacity, tok_dev)
    gates_by = gates.reshape(group, local_experts, 1, tok_dev)
    places, weights = [], []
    for e in range(local_experts):
        here = by_expert[:, e]
        places.append(here.astype(BF16).reshape(rows, tok_dev))
        weights.append(jnp.where(here, gates_by[:, e], 0.0).astype(BF16).reshape(rows, tok_dev))

    got_tokens, got_scaled = [], []
    for e in range(local_experts):
        got_tokens.append(exchange(dot(places[e], tokens).astype(BF16), group))
        got_scaled.append(exchange(dot(weights[e], cotangent).astype(BF16), group))

    combined = jnp.zeros((tok_dev, model_dim), F32)
    tokens_grad = jnp.zeros((tok_dev, model_dim), F32)
    products = []
    reduced = []
    for e in range(local_experts):
        x, scaled = got_tokens[e], got_scaled[e]
        gate_mat, up_mat, down_mat = gate_proj[e], up_proj[e], down_proj[e]
        pre_gate = dot(x, gate_mat)
        pre_up = dot(x, up_mat)
        activation, derivative = silu_parts(pre_gate)
        hidden = (activation * pre_up).astype(BF16)
        out = exchange(dot(hidden, down_mat).astype(BF16), group)
        grad_hidden = dot(scaled, down_mat, CONTRACT_LAST)
        grad_pregate = (grad_hidden * pre_up * derivative).astype(BF16)
        grad_preup = (grad_hidden * activation).astype(BF16)
        grads = jnp.concatenate(
            [
                dot(scaled, hidden, CONTRACT_FIRST).astype(BF16),
                dot(x, grad_pregate, CONTRACT_FIRST).astype(BF16),
                dot(x, grad_preup, CONTRACT_FIRST).astype(BF16),
            ],
            axis=1,
        )
        reduced.append(lax.psum_scatter(grads, "dp", scatter_dimension=0, tiled=True))
        part = exchange(
            (dot(grad_pregate, gate_mat, CONTRACT_LAST) + dot(grad_preup, up_mat, CONTRACT_LAST)).astype(BF16),
            group,
        )
        combined = combined + dot(weights[e], out, CONTRACT_FIRST)
        tokens_grad = tokens_grad + dot(places[e], part, CONTRACT_FIRST)
        product = dot(out, cotangent, CONTRACT_LAST).reshape(group, capacity, tok_dev)
        products.append(jnp.sum(jnp.where(by_expert[:, e], product, 0.0), axis=1))

    per_expert = jnp.stack(products, axis=1).reshape(experts_total, 1, tok_dev)
    labels = lax.broadcasted_iota(jnp.int32, (experts_total, 1, tok_dev), 0)
    gates_grad = jnp.sum(jnp.where(expert_ids.T[None] == labels, per_expert, 0.0), axis=0).T
    reduced = jnp.stack(reduced)
    return (
        combined.astype(BF16),
        tokens_grad.astype(BF16),
        gates_grad.astype(BF16),
        reduced[:, :, hidden_dim : 2 * hidden_dim],
        reduced[:, :, 2 * hidden_dim :],
        jnp.swapaxes(reduced[:, :, :hidden_dim], 1, 2),
    )


def solution(mesh):
    both = ("dp", "expert")
    return jax.shard_map(
        local,
        mesh=mesh,
        in_specs=(
            P(both, None),
            P(both, None),
            P(both, None),
            P(both, None),
            P(both),
            P("expert", None, None),
            P("expert", None, None),
            P("expert", None, None),
        ),
        out_specs=(
            P(both, None),
            P(both, None),
            P(both, None),
            P("expert", "dp", None),
            P("expert", "dp", None),
            P("expert", None, "dp"),
        ),
        check_vma=False,
    )
```

time: 711 us -> 469 us (0.66)
  local copies, waits for them, and re-layouts: 211 us -> 6.63 us
  blocking collectives: 0 us -> 87.2 us
  other arithmetic: 91.5 us -> 14.5 us
  starting transfers between devices: 84.3 us -> 36 us
  waiting for transfers between devices: 216 us -> 186 us
  matrix products: 84.5 us -> 114 us
    gather x17 -> x0, local copies, waits for them, and re-layouts: 115 us -> none  [the longest x4 37.7 us: pack(): with_blank(arrived_rows.reshape((group_size * capacity,) + arrived_rows.s...]
    all_to_all x0 -> x2, blocking collectives: none -> 87.2 us  [exchange(): lax.all_to_all(rows, 'expert', split_axis=0, concat_axis=0, tiled=True)]
    all_to_all x5 -> x6, starting transfers between devices: 83.5 us -> 36 us  [exchange(): lax.all_to_all(rows, 'expert', split_axis=0, concat_axis=0, tiled=True)]
    select_n x8 -> x0, other arithmetic: 41.5 us -> none  [the longest x2 41.3 us: pack(): with_blank(arrived_rows.reshape((group_size * capacity,) + arrived_rows.s...]
    another operation x12 -> x1, other arithmetic: 40.3 us -> 0.03 us  [local(): per_expert = jnp.stack(products, axis=1).reshape(experts_total, 1, tok_dev)]
    all_to_all x5 -> x6, waiting for transfers between devices: 216 us -> 176 us  [exchange(): lax.all_to_all(rows, 'expert', split_axis=0, concat_axis=0, tiled=True)]
    concatenate x12 -> x0, local copies, waits for them, and re-layouts: 34.3 us -> none  [with_blank(): jnp.concatenate([values, jnp.zeros((1,) + values.shape[1:], values.dtype)...]
    dot_general x26 -> x29, matrix products: 84.5 us -> 114 us  [dot(): return lax.dot_general(a, b, dims, preferred_element_type=F32)]
  transfers between devices with their start and end apart: 8 -> 8, of which waited for: 4 -> 7; matrix products, arithmetic and copies ran while one was open for 31% -> 20% of each run, Pallas kernels for 0% -> 0%
where the time goes in v1:
time: 469 us; the launch traced here: 460 us
  waiting for transfers between devices  186 us (40%)
  matrix products  114 us (24%)
  blocking collectives  87.2 us (19%)
  starting transfers between devices  36 us (8%)
  between operations  15.8 us (3%)
  other arithmetic  14.5 us (3%)
  local copies, waits for them, and re-layouts  6.63 us (1%)
    all_to_all x6, waiting for transfers between devices, exchange(): lax.all_to_all(rows, 'expert', split_axis=0, concat_axis=0, tiled=True)  176 us
    dot_general x29, matrix products, dot(): return lax.dot_general(a, b, dims, preferred_element_type=F32)  114 us
    all_to_all x2, blocking collectives, exchange(): lax.all_to_all(rows, 'expert', split_axis=0, concat_axis=0, tiled=True)  87.2 us
    all_to_all x6, starting transfers between devices, exchange(): lax.all_to_all(rows, 'expert', split_axis=0, concat_axis=0, tiled=True)  36 us
    reduce_scatter x2, waiting for transfers between devices, local(): lax.psum_scatter(grads, 'dp', scatter_dimension=0, tiled=True)  10.3 us
  transfers between devices with their start and end apart: 8, of which 7 were waited for; matrix products, arithmetic and copies ran while one was open for 20% of the time, Pallas kernels for 0%

profile of v1, /device:TPU:32, one launch (start us, length us, event | category | flops | bytes accessed | tf_op | source)
XLA Modules:
  0.0 460.1 jit_solution(18418411784022660046)
XLA Ops:
  7.2 0.0 copy-start
  7.9 0.8 fusion.47
  8.7 0.1 convolution_convert_fusion.12
  8.9 0.2 fusion.42
  9.1 3.7 convolution_convert_fusion.9
  12.8 8.4 %all-to-all-start = ((bf16[32,24,2048]{2,1,0:T(8,128)(2,1)}), bf16[32,24,2048]{2,1,0:T(8,128)(2,1)}, u32[]{:S(2)}, u32[]{:S(2)}) async-start(bf16[32,24,2048]{2,1,0:T(8,128)(2,1)} %bitcast.146), calls=%async_computation | async-start | bytes 6291456 | tf_op jit(solution)/shard_map/all_to_all | solution.py:40
  21.2 2.6 convolution_convert_fusion.7
  23.8 36.9 %all-to-all-done = bf16[32,24,2048]{2,1,0:T(8,128)(2,1)} async-done(((bf16[32,24,2048]{2,1,0:T(8,128)(2,1)}), bf16[32,24,2048]{2,1,0:T(8,128)(2,1)}, u32[]{:S(2)}, u32[]{:S(2)}) %all-to-all-start) | async-done | bytes 3145760 | tf_op jit(solution)/shard_map/all_to_all | solution.py:40
  60.8 5.3 %all-to-all-start.2 = ((bf16[32,24,2048]{2,1,0:T(8,128)(2,1)}), bf16[32,24,2048]{2,1,0:T(8,128)(2,1)}, u32[]{:S(2)}, u32[]{:S(2)}) async-start(bf16[32,24,2048]{2,1,0:T(8,128)(2,1)} %bitcast.145), calls=%async_computation.2 | async-start | bytes 6291456 | tf_op jit(solution)/shard_map/all_to_all | solution.py:40
  66.1 0.0 slice-start
  66.1 5.6 %fusion.18 = f32[768,768]{1,0:T(8,128)S(1)} fusion(bf16[768,2048]{1,0:T(8,128)(2,1)} %bitcast.9, bf16[2,2048,768]{2,1,0:T(8,128)(2,1)} %param.13), kind=kOutput, calls=%fused_computation.38 | convolution fusion | flops 2415919104 | bytes 8650752 | tf_op jit(solution)/shard_map/dot_general | solution.py:13
  71.7 0.0 slice-start.1
  71.7 7.8 %multiply_convert_fusion.5 = (bf16[768,768]{1,0:T(8,128)(2,1)S(1)}, f32[768,768]{1,0:T(8,128)}) fusion(f32[768,768]{1,0:T(8,128)S(1)} %fusion.18, bf16[768,2048]{1,0:T(8,128)(2,1)} %bitcast.9, bf16[2,2048,768]{2,1,0:T(8,128)(2,1)} %param.14), kind=kOutput, calls=%fused_computation.65 | convolution fusion | flops 2419458048 | bytes 12189696 | tf_op jit(solution)/shard_map/dot_general | solution.py:13
  79.5 1.0 copy-done.14
  80.5 4.0 convolution_convert_fusion.8
  84.5 21.1 %all-to-all-done.2 = bf16[32,24,2048]{2,1,0:T(8,128)(2,1)} async-done(((bf16[32,24,2048]{2,1,0:T(8,128)(2,1)}), bf16[32,24,2048]{2,1,0:T(8,128)(2,1)}, u32[]{:S(2)}, u32[]{:S(2)}) %all-to-all-start.2) | async-done | bytes 3145760 | tf_op jit(solution)/shard_map/all_to_all | solution.py:40
  105.6 5.6 %all-to-all-start.1 = ((bf16[32,24,2048]{2,1,0:T(8,128)(2,1)}), bf16[32,24,2048]{2,1,0:T(8,128)(2,1)}, u32[]{:S(2)}, u32[]{:S(2)}) async-start(bf16[32,24,2048]{2,1,0:T(8,128)(2,1)} %bitcast.150), calls=%async_computation.1 | async-start | bytes 6291456 | tf_op jit(solution)/shard_map/all_to_all | solution.py:40
  111.3 5.6 %fusion.8 = f32[768,768]{1,0:T(8,128)S(1)} fusion(bf16[768,2048]{1,0:T(8,128)(2,1)} %bitcast.19, bf16[2,2048,768]{2,1,0:T(8,128)(2,1)} %param.13), kind=kOutput, calls=%fused_computation.28 | convolution fusion | flops 2415919104 | bytes 8650752 | tf_op jit(solution)/shard_map/dot_general | solution.py:13
  116.9 0.0 slice-start.3
  116.9 7.8 %multiply_convert_fusion.4 = (bf16[768,768]{1,0:T(8,128)(2,1)S(1)}, f32[768,768]{1,0:T(8,128)}) fusion(f32[768,768]{1,0:T(8,128)S(1)} %fusion.8, bf16[768,2048]{1,0:T(8,128)(2,1)} %bitcast.19, bf16[2,2048,768]{2,1,0:T(8,128)(2,1)} %param.14), kind=kOutput, calls=%fused_computation.62 | convolution fusion | flops 2419458048 | bytes 12189696 | tf_op jit(solution)/shard_map/dot_general | solution.py:13
  124.8 1.0 copy-done.12
  125.8 4.0 convolution_convert_fusion.6
  129.7 20.9 %all-to-all-done.1 = bf16[32,24,2048]{2,1,0:T(8,128)(2,1)} async-done(((bf16[32,24,2048]{2,1,0:T(8,128)(2,1)}), bf16[32,24,2048]{2,1,0:T(8,128)(2,1)}, u32[]{:S(2)}, u32[]{:S(2)}) %all-to-all-start.1) | async-done | bytes 3145760 | tf_op jit(solution)/shard_map/all_to_all | solution.py:40
  150.6 5.4 %all-to-all-start.3 = ((bf16[32,24,2048]{2,1,0:T(8,128)(2,1)}), bf16[32,24,2048]{2,1,0:T(8,128)(2,1)}, u32[]{:S(2)}, u32[]{:S(2)}) async-start(bf16[32,24,2048]{2,1,0:T(8,128)(2,1)} %bitcast.151), calls=%async_computation.3 | async-start | bytes 6291456 | tf_op jit(solution)/shard_map/all_to_all | solution.py:40
  156.0 0.0 reduce-scatter.3.cloned.1.call-start
  156.1 2.9 fusion.40
  159.0 36.6 %all-to-all-done.3 = bf16[32,24,2048]{2,1,0:T(8,128)(2,1)} async-done(((bf16[32,24,2048]{2,1,0:T(8,128)(2,1)}), bf16[32,24,2048]{2,1,0:T(8,128)(2,1)}, u32[]{:S(2)}, u32[]{:S(2)}) %all-to-all-start.3) | async-done | bytes 3145760 | tf_op jit(solution)/shard_map/all_to_all | solution.py:40
  195.6 2.9 fusion.41
  198.5 0.7 select_reduce_fusion
  199.3 0.1 fusion.45
  199.4 1.0 convolution_convert_fusion.11
  200.4 43.5 %all_to_all.40 = bf16[32,24,2048]{2,1,0:T(8,128)(2,1)S(1)} all-to-all(bf16[32,24,2048]{2,1,0:T(8,128)(2,1)S(1)} %bitcast.147), channel_id=1, replica_groups=mesh['dp'=4,'expert'=32] {'expert'}, dimensions={0} | all-to-all | bytes 6291456 | tf_op jit(solution)/shard_map/all_to_all | solution.py:40
  243.9 3.0 convolution_convert_fusion.5
  247.0 3.3 multiply_convert_fusion.2
  250.3 5.7 %convolution_convert_fusion.3 = bf16[2048,768]{0,1:T(8,128)(2,1)S(1)} fusion(bf16[768,2048]{1,0:T(8,128)(2,1)} %bitcast.9, bf16[768,768]{1,0:T(8,128)(2,1)S(1)} %get-tuple-element.43), kind=kOutput, calls=%fused_computation.11 | convolution fusion | flops 2417491968 | bytes 7471104 | tf_op jit(solution)/shard_map/dot_general | solution.py:13
  256.0 4.8 %convolution_convert_fusion.4 = bf16[2048,768]{0,1:T(8,128)(2,1)S(1)} fusion(bf16[768,2048]{1,0:T(8,128)(2,1)} %bitcast.9, bf16[768,768]{1,0:T(8,128)(2,1)S(1)} %get-tuple-element.44), kind=kOutput, calls=%fused_computation.12 | convolution fusion | flops 2417491968 | bytes 7471104 | tf_op jit(solution)/shard_map/dot_general | solution.py:13
  260.8 4.5 pad_maximum_fusion
  265.4 0.0 reduce-scatter.3.cloned.1.call-update
  265.4 0.0 reduce-scatter.5.cloned.1.call-start
  265.4 1.0 convolution_convert_fusion.10
  266.4 43.6 %all_to_all.41 = bf16[32,24,2048]{2,1,0:T(8,128)(2,1)S(1)} all-to-all(bf16[32,24,2048]{2,1,0:T(8,128)(2,1)S(1)} %bitcast.148), channel_id=1, replica_groups=mesh['dp'=4,'expert'=32] {'expert'}, dimensions={0} | all-to-all | bytes 6291456 | tf_op jit(solution)/shard_map/all_to_all | solution.py:40
  310.1 3.0 convolution_convert_fusion.2
  313.1 0.1 copy-done.20
  313.3 3.3 multiply_convert_fusion
  316.6 5.7 %convolution_convert_fusion = bf16[2048,768]{0,1:T(8,128)(2,1)S(1)} fusion(bf16[768,2048]{1,0:T(8,128)(2,1)} %bitcast.19, bf16[768,768]{1,0:T(8,128)(2,1)S(1)} %get-tuple-element.41), kind=kOutput, calls=%fused_computation.8 | convolution fusion | flops 2417491968 | bytes 7471104 | tf_op jit(solution)/shard_map/dot_general | solution.py:13
  322.3 4.8 %convolution_convert_fusion.1 = bf16[2048,768]{0,1:T(8,128)(2,1)S(1)} fusion(bf16[768,2048]{1,0:T(8,128)(2,1)} %bitcast.19, bf16[768,768]{1,0:T(8,128)(2,1)S(1)} %get-tuple-element.42), kind=kOutput, calls=%fused_computation.9 | convolution fusion | flops 2417491968 | bytes 7471104 | tf_op jit(solution)/shard_map/dot_general | solution.py:13
  327.2 4.4 pad_maximum_fusion.1
  331.6 0.0 reduce-scatter.5.cloned.1.call-update
  331.6 5.0 %fusion.16 = f32[768,2048]{1,0:T(8,128)S(1)} fusion(bf16[768,768]{1,0:T(8,128)(2,1)} %copy-done.6, bf16[2,2048,768]{2,1,0:T(8,128)(2,1)} %param.13), kind=kOutput, calls=%fused_computation.36 | convolution fusion | flops 2415919104 | bytes 10616832 | tf_op jit(solution)/shard_map/dot_general | solution.py:13
  336.7 4.1 add_convert_fusion.1
  340.8 6.0 %all-to-all-start.5 = ((bf16[32,24,2048]{2,1,0:T(8,128)(2,1)}), bf16[32,24,2048]{2,1,0:T(8,128)(2,1)S(1)}, u32[]{:S(2)}, u32[]{:S(2)}) async-start(bf16[32,24,2048]{2,1,0:T(8,128)(2,1)} %bitcast.152), calls=%async_computation.5 | async-start | bytes 6291456 | tf_op jit(solution)/shard_map/all_to_all | solution.py:40
  346.8 5.0 %fusion.6 = f32[768,2048]{1,0:T(8,128)S(1)} fusion(bf16[768,768]{1,0:T(8,128)(2,1)} %copy-done.7, bf16[2,2048,768]{2,1,0:T(8,128)(2,1)} %param.13), kind=kOutput, calls=%fused_computation.26 | convolution fusion | flops 2415919104 | bytes 10616832 | tf_op jit(solution)/shard_map/dot_general | solution.py:13
  351.8 6.0 %add_convert_fusion = bf16[768,2048]{1,0:T(8,128)(2,1)} fusion(f32[768,2048]{1,0:T(8,128)S(1)} %fusion.6, bf16[768,768]{1,0:T(8,128)(2,1)S(1)} %copy-done.19, bf16[2,2048,768]{2,1,0:T(8,128)(2,1)} %param.14), kind=kOutput, calls=%fused_computation.2 | convolution fusion | flops 2419064832 | bytes 13762560 | tf_op jit(solution)/shard_map/dot_general | solution.py:13
  357.8 28.3 %all-to-all-done.5 = bf16[32,24,2048]{2,1,0:T(8,128)(2,1)S(1)} async-done(((bf16[32,24,2048]{2,1,0:T(8,128)(2,1)}), bf16[32,24,2048]{2,1,0:T(8,128)(2,1)S(1)}, u32[]{:S(2)}, u32[]{:S(2)}) %all-to-all-start.5) | async-done | bytes 3145760 | tf_op jit(solution)/shard_map/all_to_all | solution.py:40
  386.1 5.2 %all-to-all-start.7 = ((bf16[32,24,2048]{2,1,0:T(8,128)(2,1)}), bf16[32,24,2048]{2,1,0:T(8,128)(2,1)}, u32[]{:S(2)}, u32[]{:S(2)}) async-start(bf16[32,24,2048]{2,1,0:T(8,128)(2,1)} %bitcast.149), calls=%async_computation.7 | async-start | bytes 6291456 | tf_op jit(solution)/shard_map/all_to_all | solution.py:40
  391.4 2.5 convolution_bitcast_fusion
  393.9 3.3 fusion.34
  397.2 1.6 fusion.60
  398.8 32.1 %all-to-all-done.7 = bf16[32,24,2048]{2,1,0:T(8,128)(2,1)} async-done(((bf16[32,24,2048]{2,1,0:T(8,128)(2,1)}), bf16[32,24,2048]{2,1,0:T(8,128)(2,1)}, u32[]{:S(2)}, u32[]{:S(2)}) %all-to-all-start.7) | async-done | bytes 3145760 | tf_op jit(solution)/shard_map/all_to_all | solution.py:40
  430.9 3.6 fusion.33
  434.5 10.3 %reduce-scatter.5.cloned.1.call-done = bf16[512,2304]{0,1:T(8,128)(2,1)} async-done(((bf16[2048,2304]{0,1:T(8,128)(2,1)}), bf16[512,2304]{0,1:T(8,128)(2,1)}) %reduce-scatter.5.cloned.1.call-update) | async-done | bytes 2359312 | tf_op jit(solution)/shard_map/reduce_scatter | solution.py:89
  444.8 3.7 fusion.39
  448.5 2.6 copy.51
  451.2 1.6 copy.52
  (72 shorter events, 0.3 us)
Async XLA Ops:
  7.2 148.9 %copy-start = (bf16[128,2048]{1,0:T(8,128)(2,1)S(1)}, bf16[128,2048]{1,0:T(8,128)(2,1)}, u32[]{:S(2)}) copy-start(bf16[128,2048]{1,0:T(8,128)(2,1)} %param.9) | copy-start | bytes 1572868
  12.8 8.4 %copy-start.2 = (bf16[128,2048]{1,0:T(8,128)(2,1)S(1)}, bf16[128,2048]{1,0:T(8,128)(2,1)}, u32[]{:S(2)}) copy-start(bf16[128,2048]{1,0:T(8,128)(2,1)} %param.8) | copy-start | bytes 1572868
  12.8 48.0 %all-to-all-start = ((bf16[32,24,2048]{2,1,0:T(8,128)(2,1)}), bf16[32,24,2048]{2,1,0:T(8,128)(2,1)}, u32[]{:S(2)}, u32[]{:S(2)}) async-start(bf16[32,24,2048]{2,1,0:T(8,128)(2,1)} %bitcast.146), calls=%async_computation | async-start | bytes 6291456 | tf_op jit(solution)/shard_map/all_to_all | solution.py:40
  60.8 44.9 %all-to-all-start.2 = ((bf16[32,24,2048]{2,1,0:T(8,128)(2,1)}), bf16[32,24,2048]{2,1,0:T(8,128)(2,1)}, u32[]{:S(2)}, u32[]{:S(2)}) async-start(bf16[32,24,2048]{2,1,0:T(8,128)(2,1)} %bitcast.145), calls=%async_computation.2 | async-start | bytes 6291456 | tf_op jit(solution)/shard_map/all_to_all | solution.py:40
  66.1 14.5 %slice-start = ((s8[6291456]{0:T(1024)(128)(4,1)}), s8[4194304]{0:T(1024)(128)(4,1)S(1)}, s32[]{:S(2)}) async-start(s8[6291456]{0:T(1024)(128)(4,1)} %bitcast.175), calls=%async_computation.12 | async-start | bytes 8388608
  71.7 7.8 %copy-start.10 = (f32[768,768]{1,0:T(8,128)}, f32[768,768]{1,0:T(8,128)S(1)}, u32[]{:S(2)}) copy-start(f32[768,768]{1,0:T(8,128)S(1)} %fusion.18) | copy-start | bytes 7077892
  71.7 8.8 %slice-start.1 = ((s8[6291456]{0:T(1024)(128)(4,1)}), s8[2097152]{0:T(1024)(128)(4,1)S(1)}, s32[]{:S(2)}) async-start(s8[6291456]{0:T(1024)(128)(4,1)} %bitcast.175), calls=%async_computation.13 | async-start | bytes 4194304
  79.5 1.0 copy-start.14
  105.6 45.0 %all-to-all-start.1 = ((bf16[32,24,2048]{2,1,0:T(8,128)(2,1)}), bf16[32,24,2048]{2,1,0:T(8,128)(2,1)}, u32[]{:S(2)}, u32[]{:S(2)}) async-start(bf16[32,24,2048]{2,1,0:T(8,128)(2,1)} %bitcast.150), calls=%async_computation.1 | async-start | bytes 6291456 | tf_op jit(solution)/shard_map/all_to_all | solution.py:40
  111.3 14.5 %slice-start.2 = ((s8[6291456]{0:T(1024)(128)(4,1)}), s8[4194304]{0:T(1024)(128)(4,1)S(1)}, s32[]{:S(2)}) async-start(s8[6291456]{0:T(1024)(128)(4,1)} %bitcast.177), calls=%async_computation.14 | async-start | bytes 8388608
  116.9 7.9 %copy-start.8 = (f32[768,768]{1,0:T(8,128)}, f32[768,768]{1,0:T(8,128)S(1)}, u32[]{:S(2)}) copy-start(f32[768,768]{1,0:T(8,128)S(1)} %fusion.8) | copy-start | bytes 7077892
  116.9 8.9 %slice-start.3 = ((s8[6291456]{0:T(1024)(128)(4,1)}), s8[2097152]{0:T(1024)(128)(4,1)S(1)}, s32[]{:S(2)}) async-start(s8[6291456]{0:T(1024)(128)(4,1)} %bitcast.177), calls=%async_computation.15 | async-start | bytes 4194304
  124.8 1.0 copy-start.12
  150.6 5.4 %copy-start.5 = (bf16[128,8]{0,1:T(8,128)(2,1)S(1)}, bf16[128,8]{0,1:T(8,128)(2,1)}, u32[]{:S(2)}) copy-start(bf16[128,8]{0,1:T(8,128)(2,1)} %param.11) | copy-start | bytes 6148
  150.6 45.0 %all-to-all-start.3 = ((bf16[32,24,2048]{2,1,0:T(8,128)(2,1)}), bf16[32,24,2048]{2,1,0:T(8,128)(2,1)}, u32[]{:S(2)}, u32[]{:S(2)}) async-start(bf16[32,24,2048]{2,1,0:T(8,128)(2,1)} %bitcast.151), calls=%async_computation.3 | async-start | bytes 6291456 | tf_op jit(solution)/shard_map/all_to_all | solution.py:40
  156.0 278.6 %reduce-scatter.3.cloned.1.call-start = ((), (), s32[]{:S(2)}) async-start(), calls=%async_computation.10 | async-start | bytes 11796480 | tf_op jit(solution)/shard_map/reduce_scatter | solution.py:89
  159.0 39.6 %copy-start.4 = (s32[128,8]{0,1:T(8,128)S(1)}, s32[128,8]{0,1:T(8,128)}, u32[]{:S(2)}) copy-start(s32[128,8]{0,1:T(8,128)} %param.10) | copy-start | bytes 12292
  199.3 44.7 %copy-start.3 = (f32[32,1,1,128]{3,1,0,2:T(1,128)}, f32[32,1,1,128]{3,1,0,2:T(1,128)S(1)}, u32[]{:S(2)}) copy-start(f32[32,1,1,128]{3,1,0,2:T(1,128)S(1)} %get-tuple-element.48) | copy-start | bytes 49156
  200.4 43.6 %copy-start.15 = (bf16[768,768]{1,0:T(8,128)(2,1)S(1)}, bf16[768,768]{1,0:T(8,128)(2,1)}, u32[]{:S(2)}) copy-start(bf16[768,768]{1,0:T(8,128)(2,1)} %copy-done.14) | copy-start | bytes 3538948
  200.4 46.6 %slice-start.4 = ((s8[6291456]{0:T(1024)(128)(4,1)}), s8[4194304]{0:T(1024)(128)(4,1)S(1)}, s32[]{:S(2)}) async-start(s8[6291456]{0:T(1024)(128)(4,1)} %bitcast.179), calls=%async_computation.16 | async-start | bytes 8388608
  243.9 3.0 slice-start.5
  243.9 3.0 copy-start.11
  243.9 3.0 copy-start.21
  250.3 5.7 %copy-start.16 = (bf16[768,768]{1,0:T(8,128)(2,1)}, bf16[768,768]{1,0:T(8,128)(2,1)S(1)}, u32[]{:S(2)}) copy-start(bf16[768,768]{1,0:T(8,128)(2,1)S(1)} %get-tuple-element.43) | copy-start | bytes 3538948
  250.3 5.7 %copy-start.6 = (bf16[768,768]{1,0:T(8,128)(2,1)}, bf16[768,768]{1,0:T(8,128)(2,1)S(1)}, u32[]{:S(2)}) copy-start(bf16[768,768]{1,0:T(8,128)(2,1)S(1)} %get-tuple-element.44) | copy-start | bytes 3538948
  265.4 179.4 %reduce-scatter.5.cloned.1.call-start = ((), (), s32[]{:S(2)}) async-start(), calls=%async_computation.11 | async-start | bytes 11796480 | tf_op jit(solution)/shard_map/reduce_scatter | solution.py:89
  266.4 43.7 %copy-start.13 = (bf16[768,768]{1,0:T(8,128)(2,1)S(1)}, bf16[768,768]{1,0:T(8,128)(2,1)}, u32[]{:S(2)}) copy-start(bf16[768,768]{1,0:T(8,128)(2,1)} %copy-done.12) | copy-start | bytes 3538948
  266.4 46.7 %slice-start.6 = ((s8[6291456]{0:T(1024)(128)(4,1)}), s8[4194304]{0:T(1024)(128)(4,1)S(1)}, s32[]{:S(2)}) async-start(s8[6291456]{0:T(1024)(128)(4,1)} %bitcast.181), calls=%async_computation.18 | async-start | bytes 8388608
  310.1 3.0 slice-start.7
  310.1 3.0 copy-start.9
  310.1 3.2 copy-start.20
  316.6 5.7 %copy-start.18 = (bf16[768,768]{1,0:T(8,128)(2,1)}, bf16[768,768]{1,0:T(8,128)(2,1)S(1)}, u32[]{:S(2)}) copy-start(bf16[768,768]{1,0:T(8,128)(2,1)S(1)} %get-tuple-element.41) | copy-start | bytes 3538948
  316.6 5.7 %copy-start.7 = (bf16[768,768]{1,0:T(8,128)(2,1)}, bf16[768,768]{1,0:T(8,128)(2,1)S(1)}, u32[]{:S(2)}) copy-start(bf16[768,768]{1,0:T(8,128)(2,1)S(1)} %get-tuple-element.42) | copy-start | bytes 3538948
  331.6 5.1 %slice-start.8 = ((s8[6291456]{0:T(1024)(128)(4,1)}), s8[2097152]{0:T(1024)(128)(4,1)S(1)}, s32[]{:S(2)}) async-start(s8[6291456]{0:T(1024)(128)(4,1)} %bitcast.183), calls=%async_computation.20 | async-start | bytes 4194304
  331.6 5.1 %slice-start.9 = ((s8[6291456]{0:T(1024)(128)(4,1)}), s8[4194304]{0:T(1024)(128)(4,1)S(1)}, s32[]{:S(2)}) async-start(s8[6291456]{0:T(1024)(128)(4,1)} %bitcast.183), calls=%async_computation.21 | async-start | bytes 8388608
  331.6 5.1 %copy-start.17 = (bf16[768,768]{1,0:T(8,128)(2,1)S(1)}, bf16[768,768]{1,0:T(8,128)(2,1)}, u32[]{:S(2)}) copy-start(bf16[768,768]{1,0:T(8,128)(2,1)} %copy-done.16) | copy-start | bytes 3538948
  340.8 45.4 %all-to-all-start.5 = ((bf16[32,24,2048]{2,1,0:T(8,128)(2,1)}), bf16[32,24,2048]{2,1,0:T(8,128)(2,1)S(1)}, u32[]{:S(2)}, u32[]{:S(2)}) async-start(bf16[32,24,2048]{2,1,0:T(8,128)(2,1)} %bitcast.152), calls=%async_computation.5 | async-start | bytes 6291456 | tf_op jit(solution)/shard_map/all_to_all | solution.py:40
  346.8 5.0 %copy-start.19 = (bf16[768,768]{1,0:T(8,128)(2,1)S(1)}, bf16[768,768]{1,0:T(8,128)(2,1)}, u32[]{:S(2)}) copy-start(bf16[768,768]{1,0:T(8,128)(2,1)} %copy-done.18) | copy-start | bytes 3538948
  386.1 44.8 %all-to-all-start.7 = ((bf16[32,24,2048]{2,1,0:T(8,128)(2,1)}), bf16[32,24,2048]{2,1,0:T(8,128)(2,1)}, u32[]{:S(2)}, u32[]{:S(2)}) async-start(bf16[32,24,2048]{2,1,0:T(8,128)(2,1)} %bitcast.149), calls=%async_computation.7 | async-start | bytes 6291456 | tf_op jit(solution)/shard_map/all_to_all | solution.py:40
  448.5 4.2 copy-start.1
Sparse Core Ops, SparseCore 0:
  265.5 88.0 reduce-scatter.2
  356.1 88.6 reduce-scatter.4

commit v2 on v1

v2 whole, which is shorter than its diff:
```python
import functools

import jax
import jax.numpy as jnp
from jax import lax
from jax.experimental import pallas as pl
from jax.experimental.pallas import tpu as pltpu
from jax.sharding import PartitionSpec as P

F32 = jnp.float32
BF16 = jnp.bfloat16
CONTRACT_FIRST = (((0,), (0,)), ((), ()))
CONTRACT_LAST = (((1,), (1,)), ((), ()))
NOBODY = 255.0
META_ROWS = 16


def dot(a, b, dims=(((1,), (0,)), ((), ()))):
    return lax.dot_general(a, b, dims, preferred_element_type=F32)


def dispatch_kernel(top, capacity, first_ref, block_ref, *out_refs):
    sources, _, model_dim = block_ref.shape
    tok_dev = 128
    experts = len(out_refs) // 2
    before = (
        lax.broadcasted_iota(jnp.int32, (tok_dev, tok_dev), 0)
        < lax.broadcasted_iota(jnp.int32, (tok_dev, tok_dev), 1)
    ).astype(BF16)
    column = lax.broadcasted_iota(jnp.int32, (capacity, tok_dev), 0).astype(F32)
    picked = []
    for j in range(sources):
        meta = block_ref[j, 2 * tok_dev :, :].astype(F32)[0:1]
        places, weights = [], []
        for e in range(experts):
            expert = (first_ref[0] + e).astype(F32)
            name = jnp.zeros((1, tok_dev), F32)
            gate = jnp.zeros((1, tok_dev), F32)
            for k in range(top):
                hit = meta[:, k * tok_dev : (k + 1) * tok_dev] == expert
                name = jnp.where(hit, 1.0, name)
                gate = jnp.where(hit, meta[:, (top + k) * tok_dev : (top + k + 1) * tok_dev], gate)
            rank = dot(jnp.broadcast_to(name, (16, tok_dev)).astype(BF16), before)[0:1]
            here = (rank == column) & (name > 0.0)
            places.append(jnp.where(here, 1.0, 0.0))
            weights.append(jnp.where(here, gate, 0.0))
        rows = dot(jnp.concatenate(places).astype(BF16), block_ref[j, :tok_dev, :])
        scaled = dot(jnp.concatenate(weights).astype(BF16), block_ref[j, tok_dev : 2 * tok_dev, :])
        picked.append((rows, scaled))
    for e in range(experts):
        span = slice(e * capacity, (e + 1) * capacity)
        for which in range(2):
            out_refs[2 * e + which][...] = jnp.concatenate([pair[which][span] for pair in picked]).astype(BF16)


def dispatch(gathered, first_expert, experts, top, capacity):
    group, height, model_dim = gathered.shape
    step = 2
    rows = jax.ShapeDtypeStruct((group * capacity, model_dim), BF16)
    out = pl.BlockSpec((step * capacity, model_dim), lambda s: (s, 0))
    return pl.pallas_call(
        functools.partial(dispatch_kernel, top, capacity),
        grid=(group // step,),
        in_specs=[
            pl.BlockSpec(memory_space=pltpu.SMEM),
            pl.BlockSpec((step, height, model_dim), lambda s: (s, 0, 0)),
        ],
        out_specs=[out] * (2 * experts),
        out_shape=[rows] * (2 * experts),
        compiler_params=pltpu.CompilerParams(vmem_limit_bytes=48 << 20),
        cost_estimate=pl.CostEstimate(
            flops=4 * experts * group * capacity * 128 * model_dim,
            bytes_accessed=gathered.size * 2 + 4 * experts * group * capacity * model_dim,
            transcendentals=0,
        ),
    )(first_expert, gathered)


def expert_kernel(x_ref, scaled_ref, gate_ref, up_ref, down_ref, back_ref, grads_ref, xt, st, acc_out, acc_part):
    tile = pl.program_id(0)
    group = back_ref.shape[0]
    capacity = back_ref.shape[1] // 2
    shards, _, shard_rows, _ = grads_ref.shape

    @pl.when(tile == 0)
    def _():
        xt[...] = x_ref[...].T
        st[...] = scaled_ref[...].T

    pre_gate = dot(x_ref[...], gate_ref[...])
    pre_up = dot(x_ref[...], up_ref[...])
    grad_hidden = dot(scaled_ref[...], down_ref[...], CONTRACT_LAST)
    s = jax.nn.sigmoid(pre_gate)
    activation = pre_gate * s
    hidden = (activation * pre_up).astype(BF16)
    grad_pregate = (grad_hidden * pre_up * (s * (1.0 + pre_gate * (1.0 - s)))).astype(BF16)
    grad_preup = (grad_hidden * activation).astype(BF16)

    for which, (left, right) in enumerate(((xt, grad_pregate), (xt, grad_preup), (st, hidden))):
        for r in range(shards):
            rows = slice(r * shard_rows, (r + 1) * shard_rows)
            grads_ref[r, which] = dot(left[rows, :], right).astype(BF16)

    out = dot(hidden, down_ref[...])
    part = dot(grad_pregate, gate_ref[...], CONTRACT_LAST) + dot(grad_preup, up_ref[...], CONTRACT_LAST)

    @pl.when(tile == 0)
    def _():
        acc_out[...] = out
        acc_part[...] = part

    @pl.when(tile > 0)
    def _():
        acc_out[...] += out
        acc_part[...] += part

    @pl.when(tile == pl.num_programs(0) - 1)
    def _():
        for source in range(group):
            rows = slice(source * capacity, (source + 1) * capacity)
            back_ref[source] = jnp.concatenate([acc_out[rows, :], acc_part[rows, :]]).astype(BF16)


def run_expert(x, scaled, gate_proj, up_proj, down_proj, e, group, shards):
    rows, model_dim = x.shape
    hidden_dim = gate_proj.shape[2]
    capacity = rows // group
    tile = 256
    whole = pl.BlockSpec((rows, model_dim), lambda f: (0, 0), pipeline_mode=pl.Buffered(1))
    return pl.pallas_call(
        expert_kernel,
        grid=(hidden_dim // tile,),
        in_specs=[
            whole,
            whole,
            pl.BlockSpec((None, model_dim, tile), lambda f: (e, 0, f)),
            pl.BlockSpec((None, model_dim, tile), lambda f: (e, 0, f)),
            pl.BlockSpec((None, tile, model_dim), lambda f: (e, f, 0)),
        ],
        out_specs=[
            pl.BlockSpec((group, 2 * capacity, model_dim), lambda f: (0, 0, 0), pipeline_mode=pl.Buffered(1)),
            pl.BlockSpec((shards, 3, model_dim // shards, tile), lambda f: (0, 0, 0, f)),
        ],
        out_shape=[
            jax.ShapeDtypeStruct((group, 2 * capacity, model_dim), BF16),
            jax.ShapeDtypeStruct((shards, 3, model_dim // shards, hidden_dim), BF16),
        ],
        scratch_shapes=[
            pltpu.VMEM((model_dim, rows), BF16),
            pltpu.VMEM((model_dim, rows), BF16),
            pltpu.VMEM((rows, model_dim), F32),
            pltpu.VMEM((rows, model_dim), F32),
        ],
        compiler_params=pltpu.CompilerParams(vmem_limit_bytes=60 << 20),
        cost_estimate=pl.CostEstimate(
            flops=18 * rows * model_dim * hidden_dim,
            bytes_accessed=8 * rows * model_dim + 12 * model_dim * hidden_dim,
            transcendentals=rows * hidden_dim,
        ),
    )(x, scaled, gate_proj, up_proj, down_proj)


def local(tokens, cotangent, expert_ids, gate_weights, token_counts, gate_proj, up_proj, down_proj):
    group = lax.axis_size("expert")
    shards = lax.axis_size("dp")
    local_experts, model_dim, hidden_dim = gate_proj.shape
    tok_dev, top = expert_ids.shape
    experts_total = group * local_experts
    capacity = 3 * tok_dev * top // (2 * experts_total)

    live = lax.broadcasted_iota(jnp.int32, (tok_dev, top), 0) < token_counts[0]
    named = jnp.where(live, expert_ids, int(NOBODY))
    meta = jnp.concatenate([named.T.astype(BF16).reshape(1, -1), gate_weights.T.reshape(1, -1)], axis=1)
    meta = jnp.broadcast_to(meta, (META_ROWS, model_dim))
    mine = jnp.concatenate([tokens, cotangent, meta])
    gathered = lax.all_gather(mine[None], "expert", axis=0, tiled=True)

    labels = lax.broadcasted_iota(jnp.int32, (1, 1, experts_total), 2)
    hits = named[:, :, None] == labels
    names = jnp.any(hits, axis=1)
    gates = jnp.sum(jnp.where(hits, gate_weights.astype(F32)[:, :, None], 0.0), axis=1)
    after = (
        lax.broadcasted_iota(jnp.int32, (tok_dev, tok_dev), 0)
        > lax.broadcasted_iota(jnp.int32, (tok_dev, tok_dev), 1)
    )
    rank = dot(after.astype(BF16), names.astype(BF16)).astype(jnp.int32)
    column = lax.broadcasted_iota(jnp.int32, (1, 1, 2 * capacity), 2)

    first = (lax.axis_index("expert") * local_experts).astype(jnp.int32).reshape(1)
    picked = dispatch(gathered, first, local_experts, top, capacity)

    sums = jnp.zeros((2 * tok_dev, model_dim), F32)
    products = []
    reduced = []
    for e in range(local_experts):
        back, grads = run_expert(
            picked[2 * e], picked[2 * e + 1], gate_proj, up_proj, down_proj, e, group, shards
        )
        reduced.append(lax.psum_scatter(grads, "dp", scatter_dimension=0, tiled=False))
        got = lax.all_to_all(back, "expert", split_axis=0, concat_axis=0, tiled=True)
        got = got.reshape(-1, model_dim)
        names_e, rank_e, gates_e = (
            v.reshape(tok_dev, group, local_experts)[:, :, e, None] for v in (names, rank, gates)
        )
        here_out = names_e & (rank_e == column)
        here_part = names_e & (rank_e + capacity == column)
        picks = jnp.concatenate(
            [
                jnp.where(here_out, gates_e, 0.0).astype(BF16).reshape(tok_dev, -1),
                here_part.astype(BF16).reshape(tok_dev, -1),
            ]
        )
        sums = sums + dot(picks, got)
        product = dot(cotangent, got, CONTRACT_LAST).reshape(tok_dev, group, 2 * capacity)
        products.append(jnp.sum(jnp.where(here_out, product, 0.0), axis=2))

    per_expert = jnp.stack(products, axis=2).reshape(tok_dev, 1, experts_total)
    gates_grad = jnp.sum(jnp.where(hits, per_expert, 0.0), axis=2)
    reduced = jnp.stack(reduced)
    return (
        sums[:tok_dev].astype(BF16),
        sums[tok_dev:].astype(BF16),
        gates_grad.astype(BF16),
        reduced[:, 0],
        reduced[:, 1],
        jnp.swapaxes(reduced[:, 2], 1, 2),
    )


def solution(mesh):
    both = ("dp", "expert")
    return jax.shard_map(
        local,
        mesh=mesh,
        in_specs=(
            P(both, None),
            P(both, None),
            P(both, None),
            P(both, None),
            P(both),
            P("expert", None, None),
            P("expert", None, None),
            P("expert", None, None),
        ),
        out_specs=(
            P(both, None),
            P(both, None),
            P(both, None),
            P("expert", "dp", None),
            P("expert", "dp", None),
            P("expert", None, "dp"),
        ),
        check_vma=False,
    )
```

time: 469 us -> 444 us (0.947); the launches traced: 460 us -> 443 us
  Pallas kernels: 0 us -> 105 us
  matrix products: 114 us -> 16 us
  starting transfers between devices: 36 us -> 6.26 us
  waiting for transfers between devices: 186 us -> 202 us
  other arithmetic: 14.5 us -> 5.09 us
  local copies, waits for them, and re-layouts: 6.63 us -> 16 us
  blocking collectives: 87.2 us -> 78.3 us
    all_gather x0 -> x1, waiting for transfers between devices: none -> 121 us  [local(): gathered = lax.all_gather(mine[None], 'expert', axis=0, tiled=True)]
    pallas_call x0 -> x3, Pallas kernels: none -> 105 us  [the longest x2 82.2 us: run_expert(): pl.pallas_call(expert_kernel, grid=(hidden_dim // tile,), in_specs=[whole...]
    dot_general x29 -> x5, matrix products: 114 us -> 16 us  [dot(): return lax.dot_general(a, b, dims, preferred_element_type=F32)]
    all_to_all x6 -> x1, waiting for transfers between devices: 176 us -> 81.3 us  [local(): lax.all_to_all(back, 'expert', split_axis=0, concat_axis=0, tiled=True)]
    all_to_all x6 -> x1, starting transfers between devices: 36 us -> 6.14 us  [local(): lax.all_to_all(back, 'expert', split_axis=0, concat_axis=0, tiled=True)]
    reduce_scatter x2, waiting for transfers between devices: 10.3 us -> 0.01 us  [local(): lax.psum_scatter(grads, 'dp', scatter_dimension=0, tiled=False)]
    all_to_all x2 -> x1, blocking collectives: 87.2 us -> 78.3 us  [local(): lax.all_to_all(back, 'expert', split_axis=0, concat_axis=0, tiled=True)]
    concatenate x2, other arithmetic: 8.94 us -> 2.34 us  [the longest x1 2.31 us: local(): mine = jnp.concatenate([tokens, cotangent, meta])]
  transfers between devices with their start and end apart: 8 -> 4, of which waited for: 7 -> 2; matrix products, arithmetic and copies ran while one was open for 20% -> 5% of each run, Pallas kernels for 0% -> 9%
where the time goes in v2:
time: 444 us; the launch traced here: 443 us
  waiting for transfers between devices  202 us (45%)
  Pallas kernels  105 us (24%)
  blocking collectives  78.3 us (18%)
  local copies, waits for them, and re-layouts  16 us (4%)
  matrix products  16 us (4%)
  between operations  14.6 us (3%)
  starting transfers between devices  6.26 us (1%)
  other arithmetic  5.09 us (1%)
    all_gather x1, waiting for transfers between devices, local(): gathered = lax.all_gather(mine[None], 'expert', axis=0, tiled=True)  121 us
    pallas_call x2, Pallas kernels, run_expert(): pl.pallas_call(expert_kernel, grid=(hidden_dim // tile,), in_specs=[whole...  82.2 us
    all_to_all x1, waiting for transfers between devices, local(): lax.all_to_all(back, 'expert', split_axis=0, concat_axis=0, tiled=True)  81.3 us
    all_to_all x1, blocking collectives, local(): lax.all_to_all(back, 'expert', split_axis=0, concat_axis=0, tiled=True)  78.3 us
    pallas_call x1, Pallas kernels, dispatch(): pl.pallas_call(functools.partial(dispatch_kernel, top, capacity), grid=(g...  22.6 us
    dot_general x5, matrix products, dot(): return lax.dot_general(a, b, dims, preferred_element_type=F32)  16 us
  transfers between devices with their start and end apart: 4, of which 2 were waited for; matrix products, arithmetic and copies ran while one was open for 5% of the time, Pallas kernels for 9%

profile of v2, /device:TPU:32, one launch (start us, length us, event | category | flops | bytes accessed | tf_op | source)
XLA Modules:
  0.0 443.0 jit_solution(244825921694955140)
XLA Ops:
  7.2 0.0 all-gather.3.cloned.1.call-start
  7.9 0.7 convert_bitcast_fusion
  8.6 0.7 copy_bitcast_fusion.2
  9.3 2.3 pad_maximum_fusion
  11.6 0.0 all-gather.3.cloned.1.call-update
  11.6 0.0 reduce-scatter.3.cloned.1.call-start
  11.7 120.5 %all-gather.3.cloned.1.call-done = bf16[8704,2048]{1,0:T(8,128)(2,1)} async-done(((bf16[272,2048]{1,0:T(8,128)(2,1)}), bf16[8704,2048]{1,0:T(8,128)(2,1)}) %all-gather.3.cloned.1.call-update) | async-done | bytes 35651600 | tf_op jit(solution)/shard_map/all_gather | solution.py:176
  132.2 22.6 %shard_map.127 = (bf16[768,2048]{1,0:T(8,128)(2,1)S(1)}, bf16[768,2048]{1,0:T(8,128)(2,1)}, bf16[768,2048]{1,0:T(8,128)(2,1)}, bf16[768,2048]{1,0:T(8,128)(2,1)}) custom-call(s32[1]{0:T(128)} %bitcast.10.first_ref, bf16[32,272,2048]{2,1,0:T(8,128)(2,1)} %bitcast.105), custom_call_target="tpu_custom_call" | custom-call | flops 1610612736 | bytes 48234496 | tf_op jit(solution)/shard_map/pallas_call | solution.py:61
  154.8 0.0 copy-start
  154.8 1.6 copy-done
  156.5 41.1 %shard_map.128 = (bf16[32,48,2048]{2,1,0:T(8,128)(2,1)}, bf16[4,3,512,768]{3,2,1,0:T(8,128)(2,1)}) custom-call(bf16[768,2048]{1,0:T(8,128)(2,1)} %copy-done, bf16[768,2048]{1,0:T(8,128)(2,1)} %get-tuple-element.15.scaled_ref, bf16[2,2048,768]{2,1,0:T(8,128)(2,1)} %gate_ref.3, bf16[2,2048,768]{2,1,0:T(8,128)(2,1)} %up_ref.3, bf16[2,768,2048]{2,1,0:T(8,128)(2,1)} %down_ref.3), custom_call_target="tpu_custom_call" | custom-call | flops 21743271936 | bytes 31457280 | tf_op jit(solution)/shard_map/pallas_call | solution.py:130
  197.6 0.0 reduce-scatter.3.cloned.1.call-update
  197.6 0.0 reduce-scatter.5.cloned.1.call-start
  197.7 41.1 %shard_map.129 = (bf16[32,48,2048]{2,1,0:T(8,128)(2,1)}, bf16[4,3,512,768]{3,2,1,0:T(8,128)(2,1)}) custom-call(bf16[768,2048]{1,0:T(8,128)(2,1)} %get-tuple-element.17.x_ref, bf16[768,2048]{1,0:T(8,128)(2,1)} %get-tuple-element.18.scaled_ref, bf16[2,2048,768]{2,1,0:T(8,128)(2,1)} %gate_ref.3, bf16[2,2048,768]{2,1,0:T(8,128)(2,1)} %up_ref.3, ...), custom_call_target="tpu_custom_call" | custom-call | flops 21743271936 | bytes 31457280 | tf_op jit(solution)/shard_map/pallas_call | solution.py:130
  238.8 0.0 reduce-scatter.5.cloned.1.call-update
  238.8 78.3 %all_to_all.10 = bf16[32,48,2048]{2,1,0:T(8,128)(2,1)} all-to-all(bf16[32,48,2048]{2,1,0:T(8,128)(2,1)} %get-tuple-element.19), channel_id=1, replica_groups=mesh['dp'=4,'expert'=32] {'expert'}, dimensions={0} | all-to-all | bytes 12582912 | tf_op jit(solution)/shard_map/all_to_all | solution.py:200
  317.1 0.0 copy-start.2
  317.1 0.0 copy-start.1
  317.1 6.1 %all-to-all-start = ((bf16[32,48,2048]{2,1,0:T(8,128)(2,1)}), bf16[32,48,2048]{2,1,0:T(8,128)(2,1)}, u32[]{:S(2)}, u32[]{:S(2)}) async-start(bf16[32,48,2048]{2,1,0:T(8,128)(2,1)} %get-tuple-element.16), calls=%async_computation | async-start | bytes 12582912 | tf_op jit(solution)/shard_map/all_to_all | solution.py:200
  323.2 0.0 copy-done.2
  323.3 0.1 eq.116
  323.5 0.1 convolution_convert_fusion
  323.6 0.1 broadcast_add_fusion
  323.7 0.3 fusion.13
  324.0 0.0 copy-done.1
  324.0 4.7 %fusion.21 = f32[1536,128]{1,0:T(8,128)S(1)} fusion(bf16[1536,2048]{1,0:T(8,128)(2,1)} %bitcast.101, bf16[128,2048]{1,0:T(8,128)(2,1)S(1)} %copy-done.1), kind=kOutput, calls=%fused_computation.58 | convolution fusion | flops 805306368 | bytes 7602176 | tf_op jit(solution)/shard_map/dot_general | solution.py:19
  328.7 0.3 select_reduce_fusion
  329.0 81.3 %all-to-all-done = bf16[32,48,2048]{2,1,0:T(8,128)(2,1)} async-done(((bf16[32,48,2048]{2,1,0:T(8,128)(2,1)}), bf16[32,48,2048]{2,1,0:T(8,128)(2,1)}, u32[]{:S(2)}, u32[]{:S(2)}) %all-to-all-start) | async-done | bytes 6291488 | tf_op jit(solution)/shard_map/all_to_all | solution.py:200
  410.3 4.6 %fusion.20 = f32[1536,128]{1,0:T(8,128)S(1)} fusion(bf16[1536,2048]{1,0:T(8,128)(2,1)} %bitcast.14, bf16[128,2048]{1,0:T(8,128)(2,1)S(1)} %copy-done.1), kind=kOutput, calls=%fused_computation.57 | convolution fusion | flops 805306368 | bytes 7602176 | tf_op jit(solution)/shard_map/dot_general | solution.py:19
  414.9 0.3 select_reduce_fusion.1
  415.2 0.6 select_reduce_fusion.2
  415.9 0.0 slice-start
  415.9 0.4 fusion.8
  416.3 0.0 slice-start.1
  416.3 4.8 %fusion.1 = f32[256,2048]{1,0:T(8,128)S(1)} fusion(bf16[1536,2048]{1,0:T(8,128)(2,1)} %bitcast.14, bf16[128,1536]{0,1:T(8,128)(2,1)S(1)} %get-tuple-element.66, bf16[128,1536]{0,1:T(8,128)(2,1)S(1)} %get-tuple-element.64), kind=kOutput, calls=%fused_computation.11 | convolution fusion | flops 1612185600 | bytes 9175040 | tf_op jit(solution)/shard_map/dot_general | solution.py:19
  421.1 0.0 slice-done
  421.1 0.0 slice-done.1
  421.2 1.8 fusion
  423.0 1.1 fusion.17
  424.1 0.0 reduce-scatter.3.cloned.1.call-done
  424.1 3.2 constant_dynamic-update-slice_fusion.1
  427.3 0.0 reduce-scatter.5.cloned.1.call-done
  427.3 3.2 constant_dynamic-update-slice_fusion
  430.5 4.3 slice_bitcast_fusion
  434.9 1.6 copy.28
  (13 shorter events, 0.2 us)
Async XLA Ops:
  7.2 125.1 %all-gather.3.cloned.1.call-start = ((), (), s32[]{:S(2)}) async-start(), calls=%async_computation.6 | async-start | bytes 36765696 | tf_op jit(solution)/shard_map/all_gather | solution.py:176
  11.6 412.4 %reduce-scatter.3.cloned.1.call-start = ((), (), s32[]{:S(2)}) async-start(), calls=%async_computation.4 | async-start | bytes 11796480 | tf_op jit(solution)/shard_map/reduce_scatter | solution.py:199
  154.8 1.6 copy-start
  197.6 229.7 %reduce-scatter.5.cloned.1.call-start = ((), (), s32[]{:S(2)}) async-start(), calls=%async_computation.5 | async-start | bytes 11796480 | tf_op jit(solution)/shard_map/reduce_scatter | solution.py:199
  317.1 6.2 %copy-start.2 = (bf16[128,8]{0,1:T(8,128)(2,1)S(1)}, bf16[128,8]{0,1:T(8,128)(2,1)}, u32[]{:S(2)}) copy-start(bf16[128,8]{0,1:T(8,128)(2,1)} %param.11) | copy-start | bytes 6148
  317.1 6.9 %copy-start.1 = (bf16[128,2048]{1,0:T(8,128)(2,1)S(1)}, bf16[128,2048]{1,0:T(8,128)(2,1)}, u32[]{:S(2)}) copy-start(bf16[128,2048]{1,0:T(8,128)(2,1)} %param.9) | copy-start | bytes 1572868
  317.1 93.2 %all-to-all-start = ((bf16[32,48,2048]{2,1,0:T(8,128)(2,1)}), bf16[32,48,2048]{2,1,0:T(8,128)(2,1)}, u32[]{:S(2)}, u32[]{:S(2)}) async-start(bf16[32,48,2048]{2,1,0:T(8,128)(2,1)} %get-tuple-element.16), calls=%async_computation | async-start | bytes 12582912 | tf_op jit(solution)/shard_map/all_to_all | solution.py:200
  415.9 5.2 %slice-start = ((s8[6291456]{0:T(1024)(128)(4,1)}), s8[4194304]{0:T(1024)(128)(4,1)S(1)}, s32[]{:S(2)}) async-start(s8[6291456]{0:T(1024)(128)(4,1)} %bitcast.102), calls=%async_computation.7 | async-start | bytes 8388608
  416.3 4.8 %slice-start.1 = ((s8[6291456]{0:T(1024)(128)(4,1)}), s8[2097152]{0:T(1024)(128)(4,1)S(1)}, s32[]{:S(2)}) async-start(s8[6291456]{0:T(1024)(128)(4,1)} %bitcast.102), calls=%async_computation.8 | async-start | bytes 4194304
Sparse Core Ops, SparseCore 0:
  11.8 120.4 all-gather.2
  197.7 89.1 reduce-scatter.2
  289.4 88.6 reduce-scatter.4

commit v3 on v1

v3 whole, which is shorter than its diff:
```python
import functools

import jax
import jax.numpy as jnp
from jax import lax
from jax.experimental import pallas as pl
from jax.experimental.pallas import tpu as pltpu
from jax.sharding import PartitionSpec as P

F32 = jnp.float32
BF16 = jnp.bfloat16
CONTRACT_FIRST = (((0,), (0,)), ((), ()))
CONTRACT_LAST = (((1,), (1,)), ((), ()))
NOBODY = -1


def dot(a, b, dims=(((1,), (0,)), ((), ()))):
    return lax.dot_general(a, b, dims, preferred_element_type=F32)


def grads_kernel(rows_ref, gate_ref, up_ref, down_ref, grads_ref, hidden_ref, pregate_ref, preup_ref, x, xt, sc, st):
    shards, _, shard_rows, _ = grads_ref.shape
    group, height, _ = rows_ref.shape
    capacity = height // 2

    @pl.when(pl.program_id(0) == 0)
    def _():
        for pair in range(0, group, 2):
            blocks = [rows_ref[pair + j].astype(F32) for j in range(2)]
            span = slice(pair * capacity, (pair + 2) * capacity)
            sc[span, :] = jnp.concatenate([block[:capacity] for block in blocks]).astype(BF16)
            x[span, :] = jnp.concatenate([block[capacity:] for block in blocks]).astype(BF16)
        xt[...] = x[...].T
        st[...] = sc[...].T

    pre_gate = dot(x[...], gate_ref[...])
    pre_up = dot(x[...], up_ref[...])
    grad_hidden = dot(sc[...], down_ref[...], CONTRACT_LAST)
    s = jax.nn.sigmoid(pre_gate)
    activation = pre_gate * s
    hidden = (activation * pre_up).astype(BF16)
    grad_pregate = (grad_hidden * pre_up * (s * (1.0 + pre_gate * (1.0 - s)))).astype(BF16)
    grad_preup = (grad_hidden * activation).astype(BF16)
    hidden_ref[...] = hidden
    pregate_ref[...] = grad_pregate
    preup_ref[...] = grad_preup
    for which, (left, right) in enumerate(((xt, grad_pregate), (xt, grad_preup), (st, hidden))):
        for r in range(shards):
            rows = slice(r * shard_rows, (r + 1) * shard_rows)
            grads_ref[r, which] = dot(left[rows, :], right).astype(BF16)


def expert_grads(got, gate_proj, up_proj, down_proj, e, shards):
    group, height, model_dim = got.shape
    rows = group * height // 2
    hidden_dim = gate_proj.shape[2]
    tile = 256
    narrow = pl.BlockSpec((rows, tile), lambda f: (0, f))
    return pl.pallas_call(
        grads_kernel,
        grid=(hidden_dim // tile,),
        in_specs=[
            pl.BlockSpec(got.shape, lambda f: (0, 0, 0), pipeline_mode=pl.Buffered(1)),
            pl.BlockSpec((None, model_dim, tile), lambda f: (e, 0, f)),
            pl.BlockSpec((None, model_dim, tile), lambda f: (e, 0, f)),
            pl.BlockSpec((None, tile, model_dim), lambda f: (e, f, 0)),
        ],
        out_specs=[
            pl.BlockSpec((shards, 3, model_dim // shards, tile), lambda f: (0, 0, 0, f)),
            narrow,
            narrow,
            narrow,
        ],
        out_shape=[jax.ShapeDtypeStruct((shards, 3, model_dim // shards, hidden_dim), BF16)]
        + [jax.ShapeDtypeStruct((rows, hidden_dim), BF16)] * 3,
        scratch_shapes=[pltpu.VMEM((rows, model_dim), BF16), pltpu.VMEM((model_dim, rows), BF16)] * 2,
        compiler_params=pltpu.CompilerParams(vmem_limit_bytes=56 << 20),
        cost_estimate=pl.CostEstimate(
            flops=12 * rows * model_dim * hidden_dim,
            bytes_accessed=4 * rows * model_dim + 12 * model_dim * hidden_dim + 6 * rows * hidden_dim,
            transcendentals=rows * hidden_dim,
        ),
    )(got, gate_proj, up_proj, down_proj)


def returns_kernel(hidden_ref, pregate_ref, preup_ref, gate_ref, up_ref, down_ref, back_ref):
    group, height, _ = back_ref.shape
    capacity = height // 2
    out = dot(hidden_ref[...], down_ref[...])
    part = dot(pregate_ref[...], gate_ref[...], CONTRACT_LAST) + dot(preup_ref[...], up_ref[...], CONTRACT_LAST)
    for source in range(group):
        rows = slice(source * capacity, (source + 1) * capacity)
        back_ref[source] = jnp.concatenate([out[rows], part[rows]]).astype(BF16)


def expert_returns(hidden, pregate, preup, gate_proj, up_proj, down_proj, e, group):
    rows, hidden_dim = hidden.shape
    model_dim = gate_proj.shape[1]
    capacity = rows // group
    tile = 512
    whole = pl.BlockSpec((rows, hidden_dim), lambda d: (0, 0), pipeline_mode=pl.Buffered(1))
    return pl.pallas_call(
        returns_kernel,
        grid=(model_dim // tile,),
        in_specs=[
            whole,
            whole,
            whole,
            pl.BlockSpec((None, tile, hidden_dim), lambda d: (e, d, 0)),
            pl.BlockSpec((None, tile, hidden_dim), lambda d: (e, d, 0)),
            pl.BlockSpec((None, hidden_dim, tile), lambda d: (e, 0, d)),
        ],
        out_specs=pl.BlockSpec((group, 2 * capacity, tile), lambda d: (0, 0, d)),
        out_shape=jax.ShapeDtypeStruct((group, 2 * capacity, model_dim), BF16),
        compiler_params=pltpu.CompilerParams(vmem_limit_bytes=48 << 20),
        cost_estimate=pl.CostEstimate(
            flops=600 * rows * model_dim * hidden_dim,
            bytes_accessed=4 * rows * model_dim + 6 * model_dim * hidden_dim + 6 * rows * hidden_dim,
            transcendentals=0,
        ),
    )(hidden, pregate, preup, gate_proj, up_proj, down_proj)


def place_kernel(*refs):
    *reduced, gate_ref, up_ref, down_ref = refs
    for e, ref in enumerate(reduced):
        gate_ref[e] = ref[0]
        up_ref[e] = ref[1]
        down_ref[e] = ref[2].T


def place_grads(reduced):
    experts = len(reduced)
    _, shard_rows, hidden_dim = reduced[0].shape
    tile = 256
    straight = pl.BlockSpec((experts, shard_rows, tile), lambda f: (0, 0, f))
    return pl.pallas_call(
        place_kernel,
        grid=(hidden_dim // tile,),
        in_specs=[pl.BlockSpec((3, shard_rows, tile), lambda f: (0, 0, f))] * experts,
        out_specs=[straight, straight, pl.BlockSpec((experts, tile, shard_rows), lambda f: (0, f, 0))],
        out_shape=[
            jax.ShapeDtypeStruct((experts, shard_rows, hidden_dim), BF16),
            jax.ShapeDtypeStruct((experts, shard_rows, hidden_dim), BF16),
            jax.ShapeDtypeStruct((experts, hidden_dim, shard_rows), BF16),
        ],
        compiler_params=pltpu.CompilerParams(vmem_limit_bytes=32 << 20),
        cost_estimate=pl.CostEstimate(
            flops=0, bytes_accessed=12 * experts * shard_rows * hidden_dim, transcendentals=0
        ),
    )(*reduced)


def exchange(rows):
    return lax.all_to_all(rows, "expert", split_axis=0, concat_axis=0, tiled=True)


def local(tokens, cotangent, expert_ids, gate_weights, token_counts, gate_proj, up_proj, down_proj):
    group = lax.axis_size("expert")
    shards = lax.axis_size("dp")
    local_experts, model_dim, hidden_dim = gate_proj.shape
    tok_dev, top = expert_ids.shape
    experts_total = group * local_experts
    capacity = 3 * tok_dev * top // (2 * experts_total)

    live = lax.broadcasted_iota(jnp.int32, (tok_dev, top), 0) < token_counts[0]
    named = jnp.where(live, expert_ids, NOBODY)
    labels = lax.broadcasted_iota(jnp.int32, (experts_total, 1, 1), 0)
    hits = named.T[None] == labels
    names = jnp.any(hits, axis=1)
    gates = jnp.sum(jnp.where(hits, gate_weights.T[None].astype(F32), 0.0), axis=1)
    before = (
        lax.broadcasted_iota(jnp.int32, (tok_dev, tok_dev), 0)
        < lax.broadcasted_iota(jnp.int32, (tok_dev, tok_dev), 1)
    )
    rank = dot(names.astype(BF16), before.astype(BF16)).astype(jnp.int32)
    names, gates, rank = (v.reshape(group, local_experts, 1, tok_dev) for v in (names, gates, rank))
    column = lax.broadcasted_iota(jnp.int32, (1, 2 * capacity, 1), 1)
    stacked = jnp.concatenate([cotangent, tokens])

    masks, picks = [], []
    for e in range(local_experts):
        masks.append(names[:, e] & (rank[:, e] == column))
        second = names[:, e] & (rank[:, e] + capacity == column)
        picks.append(
            jnp.concatenate([jnp.where(masks[e], gates[:, e], 0.0).astype(BF16), second.astype(BF16)], axis=2)
            .reshape(-1, 2 * tok_dev)
        )
    sent = [dot(picks[e], stacked).astype(BF16).reshape(group, 2 * capacity, model_dim) for e in range(local_experts)]

    got = exchange(sent[0])
    returned, reduced = [], []
    back = None
    for e in range(local_experts):
        arriving = exchange(sent[e + 1] if e + 1 < local_experts else back)
        grads, hidden, pregate, preup = expert_grads(got, gate_proj, up_proj, down_proj, e, shards)
        reduced.append(lax.psum_scatter(grads, "dp", scatter_dimension=0, tiled=False))
        if e + 1 < local_experts:
            got = arriving
        else:
            returned.append(arriving)
        back = expert_returns(hidden, pregate, preup, gate_proj, up_proj, down_proj, e, group)
    returned.append(exchange(back))

    sums = jnp.zeros((2 * tok_dev, model_dim), F32)
    products = []
    for e, rows in enumerate(returned):
        rows = rows.reshape(-1, model_dim)
        sums = sums + dot(picks[e], rows, CONTRACT_FIRST)
        product = dot(rows, cotangent, CONTRACT_LAST).reshape(group, 2 * capacity, tok_dev)
        products.append(jnp.sum(jnp.where(masks[e], product, 0.0), axis=1))

    per_expert = jnp.stack(products, axis=1).reshape(experts_total, 1, tok_dev)
    gates_grad = jnp.sum(jnp.where(hits, per_expert, 0.0), axis=0).T
    return (
        sums[:tok_dev].astype(BF16),
        sums[tok_dev:].astype(BF16),
        gates_grad.astype(BF16),
        *place_grads(reduced),
    )


def solution(mesh):
    both = ("dp", "expert")
    return jax.shard_map(
        local,
        mesh=mesh,
        in_specs=(
            P(both, None),
            P(both, None),
            P(both, None),
            P(both, None),
            P(both),
            P("expert", None, None),
            P("expert", None, None),
            P("expert", None, None),
        ),
        out_specs=(
            P(both, None),
            P(both, None),
            P(both, None),
            P("expert", "dp", None),
            P("expert", "dp", None),
            P("expert", None, "dp"),
        ),
        check_vma=False,
    )
```

time: 469 us -> 421 us (0.90); the launches traced: 460 us -> 420 us
  blocking collectives: 87.2 us -> 0 us
  matrix products: 114 us -> 27.5 us
  Pallas kernels: 0 us -> 81 us
  waiting for transfers between devices: 186 us -> 258 us
  starting transfers between devices: 36 us -> 23.6 us
  other arithmetic: 14.5 us -> 3.74 us
    all_to_all x2 -> x0, blocking collectives: 87.2 us -> none  [exchange(): lax.all_to_all(rows, 'expert', split_axis=0, concat_axis=0, tiled=True)]
    dot_general x29 -> x7, matrix products: 114 us -> 27.5 us  [dot(): return lax.dot_general(a, b, dims, preferred_element_type=F32)]
    all_to_all x6 -> x4, waiting for transfers between devices: 176 us -> 258 us  [exchange(): lax.all_to_all(rows, 'expert', split_axis=0, concat_axis=0, tiled=True)]
    pallas_call x0 -> x5, Pallas kernels: none -> 81 us  [the longest x2 56.1 us: expert_grads(): pl.pallas_call(grads_kernel, grid=(hidden_dim // tile,), in_specs=[pl.Blo...]
    all_to_all x6 -> x4, starting transfers between devices: 36 us -> 23.2 us  [exchange(): lax.all_to_all(rows, 'expert', split_axis=0, concat_axis=0, tiled=True)]
    reduce_scatter x2, waiting for transfers between devices: 10.3 us -> 0.01 us  [local(): lax.psum_scatter(grads, 'dp', scatter_dimension=0, tiled=False)]
    concatenate x2 -> x0, other arithmetic: 8.94 us -> none  [local(): jnp.concatenate([dot(scaled, hidden, CONTRACT_FIRST).astype(BF16), dot(x,...]
  transfers between devices with their start and end apart: 8 -> 6, of which waited for: 7 -> 4; matrix products, arithmetic and copies ran while one was open for 20% -> 6% of each run, Pallas kernels for 0% -> 19%
where the time goes in v3:
time: 421 us; the launch traced here: 420 us
  waiting for transfers between devices  258 us (61%)
  Pallas kernels  81 us (19%)
  matrix products  27.5 us (7%)
  starting transfers between devices  23.6 us (6%)
  between operations  15.2 us (4%)
  local copies, waits for them, and re-layouts  10.7 us (3%)
    all_to_all x4, waiting for transfers between devices, exchange(): lax.all_to_all(rows, 'expert', split_axis=0, concat_axis=0, tiled=True)  258 us
    pallas_call x2, Pallas kernels, expert_grads(): pl.pallas_call(grads_kernel, grid=(hidden_dim // tile,), in_specs=[pl.Blo...  56.1 us
    dot_general x7, matrix products, dot(): return lax.dot_general(a, b, dims, preferred_element_type=F32)  27.5 us
    all_to_all x4, starting transfers between devices, exchange(): lax.all_to_all(rows, 'expert', split_axis=0, concat_axis=0, tiled=True)  23.2 us
    pallas_call x2, Pallas kernels, expert_returns(): pl.pallas_call(returns_kernel, grid=(model_dim // tile,), in_specs=[whole...  22.1 us
  transfers between devices with their start and end apart: 6, of which 4 were waited for; matrix products, arithmetic and copies ran while one was open for 6% of the time, Pallas kernels for 19%

profile of v3, /device:TPU:32, one launch (start us, length us, event | category | flops | bytes accessed | tf_op | source)
XLA Modules:
  0.0 419.7 jit_solution(11402379394592531528)
XLA Ops:
  7.8 0.7 select_bitcast_fusion
  8.5 0.1 fusion.28
  8.6 0.1 convolution_convert_fusion.2
  8.8 0.7 convert_bitcast_fusion
  9.5 0.1 eq.125
  9.6 0.0 copy-start.9
  9.6 0.0 copy-start.11
  9.6 0.1 select_reduce_fusion.1
  9.7 0.0 copy-done.25
  9.8 0.0 copy-start.19
  9.8 1.1 constant_dynamic-update-slice_fusion.1
  10.9 0.0 copy-start.13
  10.9 0.0 copy-start.15
  10.9 0.4 fusion.17
  11.3 0.3 fusion.24
  11.7 1.1 constant_dynamic-update-slice_fusion
  12.9 4.4 %convolution_convert_fusion.1 = bf16[1536,2048]{1,0:T(8,128)(2,1)} fusion(bf16[256,2048]{1,0:T(8,128)(2,1)S(1)} %constant_dynamic-update-slice_fusion, bf16[1536,128]{1,0:T(8,128)(2,1)S(1)} %get-tuple-element.38, bf16[1536,128]{1,0:T(8,128)(2,1)S(1)} %get-tuple-element.36), kind=kOutput, calls=%fused_computation.1 | convolution fusion | flops 1615331328 | bytes 8126464 | tf_op jit(solution)/shard_map/dot_general | solution.py:18
  17.3 8.3 %all-to-all-start = ((bf16[32,48,2048]{2,1,0:T(8,128)(2,1)}), bf16[32,48,2048]{2,1,0:T(8,128)(2,1)}, u32[]{:S(2)}, u32[]{:S(2)}) async-start(bf16[32,48,2048]{2,1,0:T(8,128)(2,1)} %bitcast.97), calls=%async_computation | async-start | bytes 12582912 | tf_op jit(solution)/shard_map/all_to_all | solution.py:155
  25.6 4.4 %convolution_convert_fusion = bf16[1536,2048]{1,0:T(8,128)(2,1)} fusion(bf16[256,2048]{1,0:T(8,128)(2,1)S(1)} %constant_dynamic-update-slice_fusion, bf16[1536,128]{1,0:T(8,128)(2,1)S(1)} %get-tuple-element.39, bf16[1536,128]{1,0:T(8,128)(2,1)S(1)} %get-tuple-element.37), kind=kOutput, calls=%fused_computation | convolution fusion | flops 1615331328 | bytes 8126464 | tf_op jit(solution)/shard_map/dot_general | solution.py:18
  30.0 83.1 %all-to-all-done.rows_ref = bf16[32,48,2048]{2,1,0:T(8,128)(2,1)} async-done(((bf16[32,48,2048]{2,1,0:T(8,128)(2,1)}), bf16[32,48,2048]{2,1,0:T(8,128)(2,1)}, u32[]{:S(2)}, u32[]{:S(2)}) %all-to-all-start) | async-done | bytes 6291488 | tf_op jit(solution)/shard_map/all_to_all | solution.py:155
  113.1 5.0 %all-to-all-start.2 = ((bf16[32,48,2048]{2,1,0:T(8,128)(2,1)}), bf16[32,48,2048]{2,1,0:T(8,128)(2,1)}, u32[]{:S(2)}, u32[]{:S(2)}) async-start(bf16[32,48,2048]{2,1,0:T(8,128)(2,1)} %bitcast.96), calls=%async_computation.2 | async-start | bytes 12582912 | tf_op jit(solution)/shard_map/all_to_all | solution.py:155
  118.1 0.2 reduce-scatter.3.cloned.1.call-start
  118.3 28.0 %shard_map.127 = (bf16[4,3,512,768]{3,2,1,0:T(8,128)(2,1)}, bf16[768,768]{1,0:T(8,128)(2,1)}, bf16[768,768]{1,0:T(8,128)(2,1)}, bf16[768,768]{1,0:T(8,128)(2,1)}) custom-call(bf16[32,48,2048]{2,1,0:T(8,128)(2,1)} %all-to-all-done.rows_ref, bf16[2,2048,768]{2,1,0:T(8,128)(2,1)} %gate_ref.7, bf16[2,2048,768]{2,1,0:T(8,128)(2,1)} %up_ref.7, ...), custom_call_target="tpu_custom_call" | custom-call | flops 14495514624 | bytes 28704768 | tf_op jit(solution)/shard_map/pallas_call | solution.py:59
  146.3 0.0 copy-start.2
  146.3 0.0 copy-start.3
  146.4 0.0 copy-start.4
  146.4 0.0 reduce-scatter.3.cloned.1.call-update
  146.4 1.2 copy-done.2
  147.6 0.4 copy-done.3
  148.0 0.4 copy-done.4
  148.3 11.0 %shard_map.128 = bf16[32,48,2048]{2,1,0:T(8,128)(2,1)} custom-call(bf16[768,768]{1,0:T(8,128)(2,1)S(1)} %copy-done.2, bf16[768,768]{1,0:T(8,128)(2,1)S(1)} %copy-done.3, bf16[768,768]{1,0:T(8,128)(2,1)S(1)} %copy-done.4, bf16[2,2048,768]{2,1,0:T(8,128)(2,1)} %gate_ref.7, bf16[2,2048,768]{2,1,0:T(8,128)(2,1)} %up_ref.7, bf16[2,768,2048]{2,1,0:T(8,128)(2,1)} %down_ref.7), custom_call_target="tpu_custom_call" | custom-call | flops 724775731200 | bytes 19267584 | tf_op jit(solution)/shard_map/pallas_call | solution.py:102
  159.4 46.3 %all-to-all-done.2.rows_ref = bf16[32,48,2048]{2,1,0:T(8,128)(2,1)} async-done(((bf16[32,48,2048]{2,1,0:T(8,128)(2,1)}), bf16[32,48,2048]{2,1,0:T(8,128)(2,1)}, u32[]{:S(2)}, u32[]{:S(2)}) %all-to-all-start.2) | async-done | bytes 6291488 | tf_op jit(solution)/shard_map/all_to_all | solution.py:155
  205.7 5.0 %all-to-all-start.1 = ((bf16[32,48,2048]{2,1,0:T(8,128)(2,1)}), bf16[32,48,2048]{2,1,0:T(8,128)(2,1)}, u32[]{:S(2)}, u32[]{:S(2)}) async-start(bf16[32,48,2048]{2,1,0:T(8,128)(2,1)} %shard_map.128), calls=%async_computation.1 | async-start | bytes 12582912 | tf_op jit(solution)/shard_map/all_to_all | solution.py:155
  210.7 0.3 reduce-scatter.5.cloned.1.call-start
  210.9 28.1 %shard_map.129 = (bf16[4,3,512,768]{3,2,1,0:T(8,128)(2,1)}, bf16[768,768]{1,0:T(8,128)(2,1)}, bf16[768,768]{1,0:T(8,128)(2,1)}, bf16[768,768]{1,0:T(8,128)(2,1)}) custom-call(bf16[32,48,2048]{2,1,0:T(8,128)(2,1)} %all-to-all-done.2.rows_ref, bf16[2,2048,768]{2,1,0:T(8,128)(2,1)} %gate_ref.7, bf16[2,2048,768]{2,1,0:T(8,128)(2,1)} %up_ref.7, ...), custom_call_target="tpu_custom_call" | custom-call | flops 14495514624 | bytes 28704768 | tf_op jit(solution)/shard_map/pallas_call | solution.py:59
  239.1 0.0 copy-start.5
  239.1 0.0 copy-start.6
  239.1 0.0 copy-start.7
  239.1 0.0 reduce-scatter.5.cloned.1.call-update
  239.1 1.2 copy-done.5
  240.4 0.4 copy-done.6
  240.7 0.4 copy-done.7
  241.1 11.0 %shard_map.130 = bf16[32,48,2048]{2,1,0:T(8,128)(2,1)} custom-call(bf16[768,768]{1,0:T(8,128)(2,1)S(1)} %copy-done.5, bf16[768,768]{1,0:T(8,128)(2,1)S(1)} %copy-done.6, bf16[768,768]{1,0:T(8,128)(2,1)S(1)} %copy-done.7, bf16[2,2048,768]{2,1,0:T(8,128)(2,1)} %gate_ref.7, bf16[2,2048,768]{2,1,0:T(8,128)(2,1)} %up_ref.7, bf16[2,768,2048]{2,1,0:T(8,128)(2,1)} %down_ref.7), custom_call_target="tpu_custom_call" | custom-call | flops 724775731200 | bytes 19267584 | tf_op jit(solution)/shard_map/pallas_call | solution.py:102
  252.1 0.0 copy-start.20
  252.1 0.0 copy-start.12
  252.2 0.0 copy-start.18
  252.2 0.0 copy-start.8
  252.2 46.1 %all-to-all-done.1 = bf16[32,48,2048]{2,1,0:T(8,128)(2,1)} async-done(((bf16[32,48,2048]{2,1,0:T(8,128)(2,1)}), bf16[32,48,2048]{2,1,0:T(8,128)(2,1)}, u32[]{:S(2)}, u32[]{:S(2)}) %all-to-all-start.1) | async-done | bytes 6291488 | tf_op jit(solution)/shard_map/all_to_all | solution.py:155
  298.3 5.0 %all-to-all-start.3 = ((bf16[32,48,2048]{2,1,0:T(8,128)(2,1)}), bf16[32,48,2048]{2,1,0:T(8,128)(2,1)}, u32[]{:S(2)}, u32[]{:S(2)}) async-start(bf16[32,48,2048]{2,1,0:T(8,128)(2,1)} %shard_map.130), calls=%async_computation.3 | async-start | bytes 12582912 | tf_op jit(solution)/shard_map/all_to_all | solution.py:155
  303.3 0.2 fusion.23
  303.5 0.2 fusion.20
  303.7 0.2 select_convert_fusion
  303.9 0.2 select_convert_fusion.1
  304.1 4.6 %fusion.2 = f32[32,128]{1,0:T(8,128)S(1)} fusion(bf16[32,48,2048]{2,1,0:T(8,128)(2,1)} %all-to-all-done.1, bf16[128,2048]{1,0:T(8,128)(2,1)S(1)} %copy-done.8, s32[32,128]{1,0:T(8,128)S(1)} %bitcast.105, pred[32,128]{1,0:T(8,128)(4,1)S(1)} %copy-done.24), kind=kOutput, calls=%fused_computation.8 | convolution fusion | flops 806088704 | bytes 6852608 | tf_op jit(solution)/shard_map/dot_general | solution.py:18
  308.8 0.0 copy-start.26
  308.8 82.4 %all-to-all-done.3 = bf16[32,48,2048]{2,1,0:T(8,128)(2,1)} async-done(((bf16[32,48,2048]{2,1,0:T(8,128)(2,1)}), bf16[32,48,2048]{2,1,0:T(8,128)(2,1)}, u32[]{:S(2)}, u32[]{:S(2)}) %all-to-all-start.3) | async-done | bytes 6291488 | tf_op jit(solution)/shard_map/all_to_all | solution.py:155
  391.2 4.6 %fusion.3 = f32[32,128]{1,0:T(8,128)S(1)} fusion(bf16[32,48,2048]{2,1,0:T(8,128)(2,1)} %all-to-all-done.3, bf16[128,2048]{1,0:T(8,128)(2,1)S(1)} %copy-done.8, s32[32,128]{1,0:T(8,128)S(1)} %bitcast.101, pred[32,128]{1,0:T(8,128)(4,1)S(1)} %copy-done.22), kind=kOutput, calls=%fused_computation.9 | convolution fusion | flops 806088704 | bytes 6852608 | tf_op jit(solution)/shard_map/dot_general | solution.py:18
  395.8 0.6 select_reduce_fusion
  396.5 4.6 %convolution_bitcast_fusion = f32[256,2048]{1,0:T(8,128)S(1)} fusion(bf16[32,48,2048]{2,1,0:T(8,128)(2,1)} %all-to-all-done.3, bf16[32,48,128]{2,1,0:T(8,128)(2,1)S(1)} %fusion.23, bf16[32,48,128]{2,1,0:T(8,128)(2,1)S(1)} %select_convert_fusion), kind=kOutput, calls=%fused_computation.2 | convolution fusion | flops 1612185600 | bytes 9175040 | tf_op jit(solution)/shard_map/dot_general | solution.py:18
  401.1 4.6 %fusion.1 = bf16[256,2048]{1,0:T(8,128)(2,1)S(1)} fusion(f32[256,2048]{1,0:T(8,128)S(1)} %convolution_bitcast_fusion, bf16[32,48,2048]{2,1,0:T(8,128)(2,1)} %all-to-all-done.1, bf16[32,48,128]{2,1,0:T(8,128)(2,1)S(1)} %fusion.20, bf16[32,48,128]{2,1,0:T(8,128)(2,1)S(1)} %select_convert_fusion.1), kind=kOutput, calls=%fused_computation.5 | convolution fusion | flops 1613234176 | bytes 10223616 | tf_op jit(solution)/shard_map/dot_general | solution.py:18
  405.7 1.1 fusion.33
  406.8 1.7 copy-done
  408.4 1.7 copy-done.1
  410.1 2.8 shard_map.131
  (40 shorter events, 0.2 us)
Async XLA Ops:
  8.5 1.2 copy-start.25
  9.6 3.2 copy-start.9
  9.6 3.2 copy-start.11
  9.8 3.0 copy-start.17
  9.8 3.0 copy-start.19
  10.9 1.9 copy-start.21
  10.9 1.9 copy-start.23
  10.9 1.9 copy-start.13
  10.9 1.9 copy-start.15
  17.3 95.9 %all-to-all-start = ((bf16[32,48,2048]{2,1,0:T(8,128)(2,1)}), bf16[32,48,2048]{2,1,0:T(8,128)(2,1)}, u32[]{:S(2)}, u32[]{:S(2)}) async-start(bf16[32,48,2048]{2,1,0:T(8,128)(2,1)} %bitcast.97), calls=%async_computation | async-start | bytes 12582912 | tf_op jit(solution)/shard_map/all_to_all | solution.py:155
  113.1 92.6 %all-to-all-start.2 = ((bf16[32,48,2048]{2,1,0:T(8,128)(2,1)}), bf16[32,48,2048]{2,1,0:T(8,128)(2,1)}, u32[]{:S(2)}, u32[]{:S(2)}) async-start(bf16[32,48,2048]{2,1,0:T(8,128)(2,1)} %bitcast.96), calls=%async_computation.2 | async-start | bytes 12582912 | tf_op jit(solution)/shard_map/all_to_all | solution.py:155
  118.1 288.6 %reduce-scatter.3.cloned.1.call-start = ((), (), s32[]{:S(2)}) async-start(), calls=%async_computation.6 | async-start | bytes 11796480 | tf_op jit(solution)/shard_map/reduce_scatter | solution.py:197
  146.3 1.3 copy-start.2
  146.3 1.6 copy-start.3
  146.4 2.0 copy-start.4
  205.7 92.6 %all-to-all-start.1 = ((bf16[32,48,2048]{2,1,0:T(8,128)(2,1)}), bf16[32,48,2048]{2,1,0:T(8,128)(2,1)}, u32[]{:S(2)}, u32[]{:S(2)}) async-start(bf16[32,48,2048]{2,1,0:T(8,128)(2,1)} %shard_map.128), calls=%async_computation.1 | async-start | bytes 12582912 | tf_op jit(solution)/shard_map/all_to_all | solution.py:155
  210.7 196.1 %reduce-scatter.5.cloned.1.call-start = ((), (), s32[]{:S(2)}) async-start(), calls=%async_computation.7 | async-start | bytes 11796480 | tf_op jit(solution)/shard_map/reduce_scatter | solution.py:197
  239.1 1.3 copy-start.5
  239.1 1.6 copy-start.6
  239.1 2.0 copy-start.7
  252.1 51.1 %copy-start.16 = (s32[32,128]{1,0:T(8,128)S(1)}, s32[32,128]{1,0:T(8,128)}, u32[]{:S(2)}) copy-start(s32[32,128]{1,0:T(8,128)} %copy-done.15) | copy-start | bytes 49156
  252.1 51.2 %copy-start.22 = (pred[32,128]{1,0:T(8,128)(4,1)S(1)}, pred[32,128]{1,0:T(8,128)(4,1)}, u32[]{:S(2)}) copy-start(pred[32,128]{1,0:T(8,128)(4,1)} %copy-done.21) | copy-start | bytes 12292
  252.1 51.3 %copy-start.14 = (s32[32,128]{1,0:T(8,128)S(1)}, s32[32,128]{1,0:T(8,128)}, u32[]{:S(2)}) copy-start(s32[32,128]{1,0:T(8,128)} %copy-done.13) | copy-start | bytes 49156
  252.1 51.4 %copy-start.24 = (pred[32,128]{1,0:T(8,128)(4,1)S(1)}, pred[32,128]{1,0:T(8,128)(4,1)}, u32[]{:S(2)}) copy-start(pred[32,128]{1,0:T(8,128)(4,1)} %copy-done.23) | copy-start | bytes 12292
  252.1 51.5 %copy-start.10 = (s32[32,1,1,128]{3,1,0,2:T(1,128)S(1)}, s32[32,1,1,128]{3,1,0,2:T(1,128)}, u32[]{:S(2)}) copy-start(s32[32,1,1,128]{3,1,0,2:T(1,128)} %copy-done.9) | copy-start | bytes 49156
  252.1 51.5 %copy-start.20 = (f32[32,1,1,128]{3,1,0,2:T(1,128)S(1)}, f32[32,1,1,128]{3,1,0,2:T(1,128)}, u32[]{:S(2)}) copy-start(f32[32,1,1,128]{3,1,0,2:T(1,128)} %copy-done.19) | copy-start | bytes 49156
  252.1 51.7 %copy-start.12 = (s32[32,1,1,128]{3,1,0,2:T(1,128)S(1)}, s32[32,1,1,128]{3,1,0,2:T(1,128)}, u32[]{:S(2)}) copy-start(s32[32,1,1,128]{3,1,0,2:T(1,128)} %copy-done.11) | copy-start | bytes 49156
  252.2 51.7 %copy-start.18 = (f32[32,1,1,128]{3,1,0,2:T(1,128)S(1)}, f32[32,1,1,128]{3,1,0,2:T(1,128)}, u32[]{:S(2)}) copy-start(f32[32,1,1,128]{3,1,0,2:T(1,128)} %copy-done.17) | copy-start | bytes 49156
  252.2 52.0 %copy-start.8 = (bf16[128,2048]{1,0:T(8,128)(2,1)S(1)}, bf16[128,2048]{1,0:T(8,128)(2,1)}, u32[]{:S(2)}) copy-start(bf16[128,2048]{1,0:T(8,128)(2,1)} %param.9) | copy-start | bytes 1572868
  298.3 92.9 %all-to-all-start.3 = ((bf16[32,48,2048]{2,1,0:T(8,128)(2,1)}), bf16[32,48,2048]{2,1,0:T(8,128)(2,1)}, u32[]{:S(2)}, u32[]{:S(2)}) async-start(bf16[32,48,2048]{2,1,0:T(8,128)(2,1)} %shard_map.130), calls=%async_computation.3 | async-start | bytes 12582912 | tf_op jit(solution)/shard_map/all_to_all | solution.py:155
  308.8 87.0 %copy-start.26 = (s32[8,128]{1,0:T(8,128)S(1)}, s32[8,128]{1,0:T(8,128)}, u32[]{:S(2)}) copy-start(s32[8,128]{1,0:T(8,128)} %copy-done.25) | copy-start | bytes 12292
  406.8 1.7 copy-start
  408.4 1.7 copy-start.1
Sparse Core Ops, SparseCore 0:
  146.5 90.1 reduce-scatter.2
  239.3 90.1 reduce-scatter.4

commit v4 on v3

--- a/solution.py
+++ b/solution.py
@@ -18,24 +18,76 @@
     return lax.dot_general(a, b, dims, preferred_element_type=F32)
 
 
-def grads_kernel(rows_ref, gate_ref, up_ref, down_ref, grads_ref, hidden_ref, pregate_ref, preup_ref, x, xt, sc, st):
+def dispatch_kernel(capacity, first_ref, block_ref, *out_refs):
+    sources = block_ref.shape[0]
+    tok_dev = 128
+    experts = len(out_refs) // 2
+    before = (
+        lax.broadcasted_iota(jnp.int32, (tok_dev, tok_dev), 0)
+        < lax.broadcasted_iota(jnp.int32, (tok_dev, tok_dev), 1)
+    ).astype(BF16)
+    column = lax.broadcasted_iota(jnp.int32, (capacity, tok_dev), 0).astype(F32)
+    names, gates = [], []
+    for j in range(sources):
+        routing = block_ref[j, 2 * tok_dev :, :tok_dev].astype(F32)
+        ids, given = routing[:8], routing[8:]
+        for e in range(experts):
+            hit = ids == (first_ref[0] + e).astype(F32)
+            names.append(jnp.max(jnp.where(hit, 1.0, 0.0), axis=0, keepdims=True))
+            gates.append(jnp.sum(jnp.where(hit, given, 0.0), axis=0, keepdims=True))
+    names = jnp.concatenate(names)
+    ranks = dot(names.astype(BF16), before)
+    picked = []
+    for j in range(sources):
+        places, weights = [], []
+        for e in range(experts):
+            row = slice(j * experts + e, j * experts + e + 1)
+            here = (ranks[row] == column) & (names[row] > 0.0)
+            places.append(jnp.where(here, 1.0, 0.0))
+            weights.append(jnp.where(here, gates[j * experts + e], 0.0))
+        rows = dot(jnp.concatenate(places).astype(BF16), block_ref[j, :tok_dev, :])
+        scaled = dot(jnp.concatenate(weights).astype(BF16), block_ref[j, tok_dev : 2 * tok_dev, :])
+        picked.append((rows, scaled))
+    for e in range(experts):
+        span = slice(e * capacity, (e + 1) * capacity)
+        for which in range(2):
+            out_refs[2 * e + which][...] = jnp.concatenate([pair[which][span] for pair in picked]).astype(BF16)
+
+
+def dispatch(gathered, first_expert, experts, capacity):
+    group, height, model_dim = gathered.shape
+    step = 4
+    rows = jax.ShapeDtypeStruct((group * capacity, model_dim), BF16)
+    out = pl.BlockSpec((step * capacity, model_dim), lambda s: (s, 0))
+    return pl.pallas_call(
+        functools.partial(dispatch_kernel, capacity),
+        grid=(group // step,),
+        in_specs=[
+            pl.BlockSpec(memory_space=pltpu.SMEM),
+            pl.BlockSpec((step, height, model_dim), lambda s: (s, 0, 0)),
+        ],
+        out_specs=[out] * (2 * experts),
+        out_shape=[rows] * (2 * experts),
+        compiler_params=pltpu.CompilerParams(vmem_limit_bytes=56 << 20),
+        cost_estimate=pl.CostEstimate(
+            flops=4 * experts * group * capacity * 128 * model_dim,
+            bytes_accessed=gathered.size * 2 + 4 * experts * group * capacity * model_dim,
+            transcendentals=0,
+        ),
+    )(first_expert, gathered)
+
+
+def grads_kernel(x_ref, scaled_ref, gate_ref, up_ref, down_ref, grads_ref, hidden_ref, pregate_ref, preup_ref, xt, st):
     shards, _, shard_rows, _ = grads_ref.shape
-    group, height, _ = rows_ref.shape
-    capacity = height // 2
 
     @pl.when(pl.program_id(0) == 0)
     def _():
-        for pair in range(0, group, 2):
-            blocks = [rows_ref[pair + j].astype(F32) for j in range(2)]
-            span = slice(pair * capacity, (pair + 2) * capacity)
-            sc[span, :] = jnp.concatenate([block[:capacity] for block in blocks]).astype(BF16)
-            x[span, :] = jnp.concatenate([block[capacity:] for block in blocks]).astype(BF16)
-        xt[...] = x[...].T
-        st[...] = sc[...].T
-
-    pre_gate = dot(x[...], gate_ref[...])
-    pre_up = dot(x[...], up_ref[...])
-    grad_hidden = dot(sc[...], down_ref[...], CONTRACT_LAST)
+        xt[...] = x_ref[...].T
+        st[...] = scaled_ref[...].T
+
+    pre_gate = dot(x_ref[...], gate_ref[...])
+    pre_up = dot(x_ref[...], up_ref[...])
+    grad_hidden = dot(scaled_ref[...], down_ref[...], CONTRACT_LAST)
     s = jax.nn.sigmoid(pre_gate)
     activation = pre_gate * s
     hidden = (activation * pre_up).astype(BF16)
@@ -45,22 +97,23 @@
     pregate_ref[...] = grad_pregate
     preup_ref[...] = grad_preup
     for which, (left, right) in enumerate(((xt, grad_pregate), (xt, grad_preup), (st, hidden))):
+        product = dot(left[...], right).astype(BF16)
         for r in range(shards):
-            rows = slice(r * shard_rows, (r + 1) * shard_rows)
-            grads_ref[r, which] = dot(left[rows, :], right).astype(BF16)
-
-
-def expert_grads(got, gate_proj, up_proj, down_proj, e, shards):
-    group, height, model_dim = got.shape
-    rows = group * height // 2
+            grads_ref[r, which] = product[r * shard_rows : (r + 1) * shard_rows]
+
+
+def expert_grads(x, scaled, gate_proj, up_proj, down_proj, e, shards):
+    rows, model_dim = x.shape
     hidden_dim = gate_proj.shape[2]
     tile = 256
+    whole = pl.BlockSpec((rows, model_dim), lambda f: (0, 0), pipeline_mode=pl.Buffered(1))
     narrow = pl.BlockSpec((rows, tile), lambda f: (0, f))
     return pl.pallas_call(
         grads_kernel,
         grid=(hidden_dim // tile,),
         in_specs=[
-            pl.BlockSpec(got.shape, lambda f: (0, 0, 0), pipeline_mode=pl.Buffered(1)),
+            whole,
+            whole,
             pl.BlockSpec((None, model_dim, tile), lambda f: (e, 0, f)),
             pl.BlockSpec((None, model_dim, tile), lambda f: (e, 0, f)),
             pl.BlockSpec((None, tile, model_dim), lambda f: (e, f, 0)),
@@ -73,14 +126,14 @@
         ],
         out_shape=[jax.ShapeDtypeStruct((shards, 3, model_dim // shards, hidden_dim), BF16)]
         + [jax.ShapeDtypeStruct((rows, hidden_dim), BF16)] * 3,
-        scratch_shapes=[pltpu.VMEM((rows, model_dim), BF16), pltpu.VMEM((model_dim, rows), BF16)] * 2,
+        scratch_shapes=[pltpu.VMEM((model_dim, rows), BF16), pltpu.VMEM((model_dim, rows), BF16)],
         compiler_params=pltpu.CompilerParams(vmem_limit_bytes=56 << 20),
         cost_estimate=pl.CostEstimate(
             flops=12 * rows * model_dim * hidden_dim,
             bytes_accessed=4 * rows * model_dim + 12 * model_dim * hidden_dim + 6 * rows * hidden_dim,
             transcendentals=rows * hidden_dim,
         ),
-    )(got, gate_proj, up_proj, down_proj)
+    )(x, scaled, gate_proj, up_proj, down_proj)
 
 
 def returns_kernel(hidden_ref, pregate_ref, preup_ref, gate_ref, up_ref, down_ref, back_ref):
@@ -121,6 +174,63 @@
     )(hidden, pregate, preup, gate_proj, up_proj, down_proj)
 
 
+def combine_kernel(cotangent_ref, *refs):
+    *pairs, combined_ref, tokens_ref, products_ref, total = refs
+    experts = len(pairs) // 2
+    tok_dev = combined_ref.shape[0]
+    devices, height, model_dim = pairs[0].shape
+    step = pl.program_id(0)
+
+    @pl.when(step == 0)
+    def _():
+        total[...] = jnp.zeros_like(total)
+
+    for e in range(experts):
+        rows = pairs[2 * e][...].reshape(devices * height, model_dim)
+        picks = pairs[2 * e + 1][...]
+        total[...] += dot(picks, rows, CONTRACT_FIRST)
+        product = dot(rows, cotangent_ref[...], CONTRACT_LAST)
+        product = jnp.where(picks[:, :tok_dev].astype(F32) > 0.0, product, 0.0)
+        for d in range(devices):
+            products_ref[e, d] = jnp.sum(product[d * height : d * height + height // 2], axis=0, keepdims=True)
+
+    @pl.when(step == pl.num_programs(0) - 1)
+    def _():
+        combined_ref[...] = total[:tok_dev].astype(BF16)
+        tokens_ref[...] = total[tok_dev:].astype(BF16)
+
+
+def combine(cotangent, returned, picks):
+    experts = len(returned)
+    group, height, model_dim = returned[0].shape
+    tok_dev = cotangent.shape[0]
+    step = 4
+    whole = pl.BlockSpec((tok_dev, model_dim), lambda s: (0, 0))
+    return pl.pallas_call(
+        combine_kernel,
+        grid=(group // step,),
+        in_specs=[whole]
+        + [
+            pl.BlockSpec((step, height, model_dim), lambda s: (s, 0, 0)),
+            pl.BlockSpec((step * height, 2 * tok_dev), lambda s: (s, 0)),
+        ]
+        * experts,
+        out_specs=[whole, whole, pl.BlockSpec((experts, step, 1, tok_dev), lambda s: (0, s, 0, 0))],
+        out_shape=[
+            jax.ShapeDtypeStruct((tok_dev, model_dim), BF16),
+            jax.ShapeDtypeStruct((tok_dev, model_dim), BF16),
+            jax.ShapeDtypeStruct((experts, group, 1, tok_dev), F32),
+        ],
+        scratch_shapes=[pltpu.VMEM((2 * tok_dev, model_dim), F32)],
+        compiler_params=pltpu.CompilerParams(vmem_limit_bytes=60 << 20),
+        cost_estimate=pl.CostEstimate(
+            flops=6 * experts * group * height * tok_dev * model_dim,
+            bytes_accessed=2 * experts * group * height * (model_dim + 2 * tok_dev),
+            transcendentals=0,
+        ),
+    )(cotangent, *[v for pair in zip(returned, picks) for v in pair])
+
+
 def place_kernel(*refs):
     *reduced, gate_ref, up_ref, down_ref = refs
     for e, ref in enumerate(reduced):
@@ -144,7 +254,7 @@
             jax.ShapeDtypeStruct((experts, shard_rows, hidden_dim), BF16),
             jax.ShapeDtypeStruct((experts, hidden_dim, shard_rows), BF16),
         ],
-        compiler_params=pltpu.CompilerParams(vmem_limit_bytes=32 << 20),
+        compiler_params=pltpu.CompilerParams(vmem_limit_bytes=60 << 20),
         cost_estimate=pl.CostEstimate(
             flops=0, bytes_accessed=12 * experts * shard_rows * hidden_dim, transcendentals=0
         ),
@@ -165,6 +275,12 @@
 
     live = lax.broadcasted_iota(jnp.int32, (tok_dev, top), 0) < token_counts[0]
     named = jnp.where(live, expert_ids, NOBODY)
+    routing = jnp.concatenate([named.T.astype(BF16), gate_weights.T])
+    routing = jnp.pad(routing, ((0, 0), (0, model_dim - tok_dev)))
+    gathered = lax.all_gather(
+        jnp.concatenate([tokens, cotangent, routing])[None], "expert", axis=0, tiled=True
+    )
+
     labels = lax.broadcasted_iota(jnp.int32, (experts_total, 1, 1), 0)
     hits = named.T[None] == labels
     names = jnp.any(hits, axis=1)
@@ -176,45 +292,34 @@
     rank = dot(names.astype(BF16), before.astype(BF16)).astype(jnp.int32)
     names, gates, rank = (v.reshape(group, local_experts, 1, tok_dev) for v in (names, gates, rank))
     column = lax.broadcasted_iota(jnp.int32, (1, 2 * capacity, 1), 1)
-    stacked = jnp.concatenate([cotangent, tokens])
-
-    masks, picks = [], []
+    picks = []
     for e in range(local_experts):
-        masks.append(names[:, e] & (rank[:, e] == column))
+        place = names[:, e] & (rank[:, e] == column)
         second = names[:, e] & (rank[:, e] + capacity == column)
         picks.append(
-            jnp.concatenate([jnp.where(masks[e], gates[:, e], 0.0).astype(BF16), second.astype(BF16)], axis=2)
+            jnp.concatenate([jnp.where(place, gates[:, e], 0.0).astype(BF16), second.astype(BF16)], axis=2)
             .reshape(-1, 2 * tok_dev)
         )
-    sent = [dot(picks[e], stacked).astype(BF16).reshape(group, 2 * capacity, model_dim) for e in range(local_experts)]
-
-    got = exchange(sent[0])
+
+    gathered, *picks = lax.optimization_barrier((gathered, *picks))
+    first = (lax.axis_index("expert") * local_experts).astype(jnp.int32).reshape(1)
+    picked = dispatch(gathered, first, local_experts, capacity)
+
     returned, reduced = [], []
-    back = None
     for e in range(local_experts):
-        arriving = exchange(sent[e + 1] if e + 1 < local_experts else back)
-        grads, hidden, pregate, preup = expert_grads(got, gate_proj, up_proj, down_proj, e, shards)
+        grads, hidden, pregate, preup = expert_grads(
+            picked[2 * e], picked[2 * e + 1], gate_proj, up_proj, down_proj, e, shards
+        )
         reduced.append(lax.psum_scatter(grads, "dp", scatter_dimension=0, tiled=False))
-        if e + 1 < local_experts:
-            got = arriving
-        else:
-            returned.append(arriving)
         back = expert_returns(hidden, pregate, preup, gate_proj, up_proj, down_proj, e, group)
-    returned.append(exchange(back))
-
-    sums = jnp.zeros((2 * tok_dev, model_dim), F32)
-    products = []
-    for e, rows in enumerate(returned):
-        rows = rows.reshape(-1, model_dim)
-        sums = sums + dot(picks[e], rows, CONTRACT_FIRST)
-        product = dot(rows, cotangent, CONTRACT_LAST).reshape(group, 2 * capacity, tok_dev)
-        products.append(jnp.sum(jnp.where(masks[e], product, 0.0), axis=1))
-
-    per_expert = jnp.stack(products, axis=1).reshape(experts_total, 1, tok_dev)
+        returned.append(exchange(back))
+
+    combined, tokens_grad, products = combine(cotangent, returned, picks)
+    per_expert = products.transpose(1, 0, 2, 3).reshape(experts_total, 1, tok_dev)
     gates_grad = jnp.sum(jnp.where(hits, per_expert, 0.0), axis=0).T
     return (
-        sums[:tok_dev].astype(BF16),
-        sums[tok_dev:].astype(BF16),
+        combined,
+        tokens_grad,
         gates_grad.astype(BF16),
         *place_grads(reduced),
     )

time: 421 us -> 392 us (0.931)
  waiting for transfers between devices: 258 us -> 163 us
  blocking collectives: 0 us -> 76.7 us
  Pallas kernels: 81 us -> 116 us
  matrix products: 27.5 us -> 0.14 us
  starting transfers between devices: 23.6 us -> 6.26 us
  local copies, waits for them, and re-layouts: 10.7 us -> 5.06 us
    all_to_all x4 -> x1, waiting for transfers between devices: 258 us -> 45.8 us  [exchange(): lax.all_to_all(rows, 'expert', split_axis=0, concat_axis=0, tiled=True)]
    all_gather x0 -> x1, waiting for transfers between devices: none -> 117 us  [local(): lax.all_gather(jnp.concatenate([tokens, cotangent, routing])[None], 'expe...]
    all_to_all x0 -> x1, blocking collectives: none -> 76.7 us  [exchange(): lax.all_to_all(rows, 'expert', split_axis=0, concat_axis=0, tiled=True)]
    pallas_call x2 -> x4, Pallas kernels: 56.1 us -> 87.5 us  [the longest x2 56 us: expert_grads(): pl.pallas_call(grads_kernel, grid=(hidden_dim // tile,), in_specs=[whole,...]
    dot_general x7 -> x1, matrix products: 27.5 us -> 0.14 us  [dot(): return lax.dot_general(a, b, dims, preferred_element_type=F32)]
    all_to_all x4 -> x1, starting transfers between devices: 23.2 us -> 5.96 us  [exchange(): lax.all_to_all(rows, 'expert', split_axis=0, concat_axis=0, tiled=True)]
    concatenate x0 -> x4, other arithmetic: none -> 5.04 us  [the longest x1 2.3 us: local(): jnp.concatenate([tokens, cotangent, routing])[None]]
    unnamed x56 -> x19, local copies, waits for them, and re-layouts: 8.38 us -> 4.09 us
  transfers between devices with their start and end apart: 6 -> 4, of which waited for: 4 -> 2; matrix products, arithmetic and copies ran while one was open for 6% -> 1% of each run, Pallas kernels for 19% -> 17%
where the time goes in v4:
time: 392 us; the launch traced here: 389 us
  waiting for transfers between devices  163 us (42%)
  Pallas kernels  116 us (30%)
  blocking collectives  76.7 us (20%)
  between operations  14.6 us (4%)
  other arithmetic  7.29 us (2%)
  starting transfers between devices  6.26 us (2%)
  local copies, waits for them, and re-layouts  5.06 us (1%)
    all_gather x1, waiting for transfers between devices, local(): lax.all_gather(jnp.concatenate([tokens, cotangent, routing])[None], 'expe...  117 us
    all_to_all x1, blocking collectives, exchange(): lax.all_to_all(rows, 'expert', split_axis=0, concat_axis=0, tiled=True)  76.7 us
    pallas_call x2, Pallas kernels, expert_grads(): pl.pallas_call(grads_kernel, grid=(hidden_dim // tile,), in_specs=[whole,...  56 us
    all_to_all x1, waiting for transfers between devices, exchange(): lax.all_to_all(rows, 'expert', split_axis=0, concat_axis=0, tiled=True)  45.8 us
    pallas_call x2, Pallas kernels, expert_returns(): pl.pallas_call(returns_kernel, grid=(model_dim // tile,), in_specs=[whole...  22.7 us
    pallas_call x1, Pallas kernels, dispatch(): pl.pallas_call(functools.partial(dispatch_kernel, capacity), grid=(group...  18.1 us
    pallas_call x1, Pallas kernels, combine(): pl.pallas_call(combine_kernel, grid=(group // step,), in_specs=[whole] +...  13.3 us
  transfers between devices with their start and end apart: 4, of which 2 were waited for; matrix products, arithmetic and copies ran while one was open for 1% of the time, Pallas kernels for 17%

profile of v4, /device:TPU:32, one launch (start us, length us, event | category | flops | bytes accessed | tf_op | source)
XLA Modules:
  0.0 388.7 jit_solution(5561348393101877740)
XLA Ops:
  7.2 0.0 copy-start.8
  7.2 0.0 all-gather.3.cloned.1.call-start
  7.9 0.7 fusion.8
  8.6 0.0 copy-start.6
  8.6 0.7 fusion.7
  9.3 2.3 pad_maximum_fusion
  11.6 0.0 all-gather.3.cloned.1.call-update
  11.6 0.0 reduce-scatter.3.cloned.1.call-start
  11.7 0.1 fusion.4
  11.8 0.1 eq.104
  11.9 0.0 copy-done.8
  11.9 0.1 select_reduce_fusion.1
  12.0 0.1 convolution_convert_fusion
  12.2 0.4 fusion
  12.6 0.0 copy-done.6
  12.6 0.3 fusion.3
  13.0 1.0 pad_maximum_fusion.2.refs_3_
  14.0 1.0 pad_maximum_fusion.1.refs_1_
  15.0 117.2 %all-gather.3.cloned.1.call-done = bf16[8704,2048]{1,0:T(8,128)(2,1)} async-done(((bf16[272,2048]{1,0:T(8,128)(2,1)}), bf16[8704,2048]{1,0:T(8,128)(2,1)}) %all-gather.3.cloned.1.call-update) | async-done | bytes 35651600 | tf_op jit(solution)/shard_map/all_gather | solution.py:280
  132.2 18.1 %shard_map.127 = (bf16[768,2048]{1,0:T(8,128)(2,1)}, bf16[768,2048]{1,0:T(8,128)(2,1)}, bf16[768,2048]{1,0:T(8,128)(2,1)}, bf16[768,2048]{1,0:T(8,128)(2,1)}) custom-call(s32[1]{0:T(128)} %bitcast.first_ref, bf16[32,272,2048]{2,1,0:T(8,128)(2,1)} %bitcast.75), custom_call_target="tpu_custom_call" | custom-call | flops 1610612736 | bytes 48234496 | tf_op jit(solution)/shard_map/pallas_call | solution.py:62
  150.3 27.8 %shard_map.128 = (bf16[4,3,512,768]{3,2,1,0:T(8,128)(2,1)}, bf16[768,768]{1,0:T(8,128)(2,1)}, bf16[768,768]{1,0:T(8,128)(2,1)}, bf16[768,768]{1,0:T(8,128)(2,1)}) custom-call(bf16[768,2048]{1,0:T(8,128)(2,1)} %get-tuple-element.28.x_ref, bf16[768,2048]{1,0:T(8,128)(2,1)} %get-tuple-element.29.scaled_ref, bf16[2,2048,768]{2,1,0:T(8,128)(2,1)} %gate_ref.7, ...), custom_call_target="tpu_custom_call" | custom-call | flops 14495514624 | bytes 28704768 | tf_op jit(solution)/shard_map/pallas_call | solution.py:111
  178.2 0.0 copy-start
  178.2 0.0 copy-start.1
  178.2 0.0 copy-start.2
  178.2 0.0 reduce-scatter.3.cloned.1.call-update
  178.2 1.2 copy-done
  179.4 0.4 copy-done.1
  179.8 0.4 copy-done.2
  180.1 11.5 %shard_map.129 = bf16[32,48,2048]{2,1,0:T(8,128)(2,1)} custom-call(bf16[768,768]{1,0:T(8,128)(2,1)S(1)} %copy-done, bf16[768,768]{1,0:T(8,128)(2,1)S(1)} %copy-done.1, bf16[768,768]{1,0:T(8,128)(2,1)S(1)} %copy-done.2, bf16[2,2048,768]{2,1,0:T(8,128)(2,1)} %gate_ref.7, bf16[2,2048,768]{2,1,0:T(8,128)(2,1)} %up_ref.7, bf16[2,768,2048]{2,1,0:T(8,128)(2,1)} %down_ref.7), custom_call_target="tpu_custom_call" | custom-call | flops 724775731200 | bytes 19267584 | tf_op jit(solution)/shard_map/pallas_call | solution.py:155
  191.6 6.0 %all-to-all-start = ((bf16[32,48,2048]{2,1,0:T(8,128)(2,1)}), bf16[32,48,2048]{2,1,0:T(8,128)(2,1)}, u32[]{:S(2)}, u32[]{:S(2)}) async-start(bf16[32,48,2048]{2,1,0:T(8,128)(2,1)} %shard_map.129), calls=%async_computation | async-start | bytes 12582912 | tf_op jit(solution)/shard_map/all_to_all | solution.py:265
  197.6 0.2 reduce-scatter.5.cloned.1.call-start
  197.8 28.2 %shard_map.130 = (bf16[4,3,512,768]{3,2,1,0:T(8,128)(2,1)}, bf16[768,768]{1,0:T(8,128)(2,1)}, bf16[768,768]{1,0:T(8,128)(2,1)}, bf16[768,768]{1,0:T(8,128)(2,1)}) custom-call(bf16[768,2048]{1,0:T(8,128)(2,1)} %get-tuple-element.34.x_ref, bf16[768,2048]{1,0:T(8,128)(2,1)} %get-tuple-element.35.scaled_ref, bf16[2,2048,768]{2,1,0:T(8,128)(2,1)} %gate_ref.7, ...), custom_call_target="tpu_custom_call" | custom-call | flops 14495514624 | bytes 28704768 | tf_op jit(solution)/shard_map/pallas_call | solution.py:111
  226.1 0.0 copy-start.3
  226.1 0.0 copy-start.4
  226.1 0.0 copy-start.5
  226.1 0.0 reduce-scatter.5.cloned.1.call-update
  226.1 1.3 copy-done.3
  227.5 0.4 copy-done.4
  227.8 0.4 copy-done.5
  228.2 11.2 %shard_map.131 = bf16[32,48,2048]{2,1,0:T(8,128)(2,1)} custom-call(bf16[768,768]{1,0:T(8,128)(2,1)S(1)} %copy-done.3, bf16[768,768]{1,0:T(8,128)(2,1)S(1)} %copy-done.4, bf16[768,768]{1,0:T(8,128)(2,1)S(1)} %copy-done.5, bf16[2,2048,768]{2,1,0:T(8,128)(2,1)} %gate_ref.7, bf16[2,2048,768]{2,1,0:T(8,128)(2,1)} %up_ref.7, bf16[2,768,2048]{2,1,0:T(8,128)(2,1)} %down_ref.7), custom_call_target="tpu_custom_call" | custom-call | flops 724775731200 | bytes 19267584 | tf_op jit(solution)/shard_map/pallas_call | solution.py:155
  239.4 45.8 %all-to-all-done.refs_0_ = bf16[32,48,2048]{2,1,0:T(8,128)(2,1)} async-done(((bf16[32,48,2048]{2,1,0:T(8,128)(2,1)}), bf16[32,48,2048]{2,1,0:T(8,128)(2,1)}, u32[]{:S(2)}, u32[]{:S(2)}) %all-to-all-start) | async-done | bytes 6291488 | tf_op jit(solution)/shard_map/all_to_all | solution.py:265
  285.2 76.7 %all_to_all.10.refs_2_ = bf16[32,48,2048]{2,1,0:T(8,128)(2,1)} all-to-all(bf16[32,48,2048]{2,1,0:T(8,128)(2,1)} %shard_map.131), channel_id=1, replica_groups=mesh['dp'=4,'expert'=32] {'expert'}, dimensions={0} | all-to-all | bytes 12582912 | tf_op jit(solution)/shard_map/all_to_all | solution.py:265
  361.9 0.0 copy-start.7
  361.9 13.3 %shard_map.132 = (bf16[128,2048]{1,0:T(8,128)(2,1)}, bf16[128,2048]{1,0:T(8,128)(2,1)}, f32[2,32,1,128]{3,2,1,0:T(1,128)}) custom-call(bf16[128,2048]{1,0:T(8,128)(2,1)} %cotangent_ref.1, bf16[32,48,2048]{2,1,0:T(8,128)(2,1)} %all-to-all-done.refs_0_, bf16[1536,256]{1,0:T(8,128)(2,1)} %pad_maximum_fusion.1.refs_1_, ...), custom_call_target="tpu_custom_call" | custom-call | flops 4831838208 | bytes 14155776 | tf_op jit(solution)/shard_map/pallas_call | solution.py:209
  375.3 0.8 copy.20
  376.0 0.0 copy-done.7
  376.1 0.6 select_reduce_fusion
  376.7 0.0 reduce-scatter.3.cloned.1.call-done
  376.7 0.0 reduce-scatter.5.cloned.1.call-done
  376.7 5.4 %shard_map.133 = (bf16[2,512,768]{2,1,0:T(8,128)(2,1)}, bf16[2,512,768]{2,1,0:T(8,128)(2,1)}, bf16[2,768,512]{2,1,0:T(8,128)(2,1)}) custom-call(bf16[3,512,768]{2,1,0:T(8,128)(2,1)} %bitcast.76, bf16[3,512,768]{2,1,0:T(8,128)(2,1)} %bitcast.77), custom_call_target="tpu_custom_call" | custom-call | bytes 9437184 | tf_op jit(solution)/shard_map/pallas_call | solution.py:247
  (9 shorter events, 0.1 us)
Async XLA Ops:
  7.2 4.7 %copy-start.8 = (bf16[128,8]{0,1:T(8,128)(2,1)S(1)}, bf16[128,8]{0,1:T(8,128)(2,1)}, u32[]{:S(2)}) copy-start(bf16[128,8]{0,1:T(8,128)(2,1)} %param.11) | copy-start | bytes 6148
  7.2 125.0 %all-gather.3.cloned.1.call-start = ((), (), s32[]{:S(2)}) async-start(), calls=%async_computation.6 | async-start | bytes 36765696 | tf_op jit(solution)/shard_map/all_gather | solution.py:280
  8.6 4.0 %copy-start.6 = (s32[8,128]{1,0:T(8,128)}, s32[8,128]{1,0:T(8,128)S(1)}, u32[]{:S(2)}) copy-start(s32[8,128]{1,0:T(8,128)S(1)} %get-tuple-element.49) | copy-start | bytes 12292
  11.6 365.1 %reduce-scatter.3.cloned.1.call-start = ((), (), s32[]{:S(2)}) async-start(), calls=%async_computation.4 | async-start | bytes 11796480 | tf_op jit(solution)/shard_map/reduce_scatter | solution.py:313
  178.2 1.3 copy-start
  178.2 1.6 copy-start.1
  178.2 2.0 copy-start.2
  191.6 93.6 %all-to-all-start = ((bf16[32,48,2048]{2,1,0:T(8,128)(2,1)}), bf16[32,48,2048]{2,1,0:T(8,128)(2,1)}, u32[]{:S(2)}, u32[]{:S(2)}) async-start(bf16[32,48,2048]{2,1,0:T(8,128)(2,1)} %shard_map.129), calls=%async_computation | async-start | bytes 12582912 | tf_op jit(solution)/shard_map/all_to_all | solution.py:265
  197.6 179.1 %reduce-scatter.5.cloned.1.call-start = ((), (), s32[]{:S(2)}) async-start(), calls=%async_computation.5 | async-start | bytes 11796480 | tf_op jit(solution)/shard_map/reduce_scatter | solution.py:313
  226.1 1.4 copy-start.3
  226.1 1.8 copy-start.4
  226.1 2.2 copy-start.5
  361.9 14.1 %copy-start.7 = (s32[8,128]{1,0:T(8,128)S(1)}, s32[8,128]{1,0:T(8,128)}, u32[]{:S(2)}) copy-start(s32[8,128]{1,0:T(8,128)} %copy-done.6) | copy-start | bytes 12292
Sparse Core Ops, SparseCore 0:
  11.7 120.4 all-gather.2
  178.3 89.1 reduce-scatter.2
  270.0 88.6 reduce-scatter.4

commit v5 on v3

v5 whole, which is shorter than its diff:
```python
import functools

import jax
import jax.numpy as jnp
from jax import lax
from jax.experimental import pallas as pl
from jax.experimental.pallas import tpu as pltpu
from jax.sharding import PartitionSpec as P

F32 = jnp.float32
BF16 = jnp.bfloat16
CONTRACT_FIRST = (((0,), (0,)), ((), ()))
CONTRACT_LAST = (((1,), (1,)), ((), ()))
NOBODY = -1


def dot(a, b, dims=(((1,), (0,)), ((), ()))):
    return lax.dot_general(a, b, dims, preferred_element_type=F32)


def grads_kernel(
    steps,
    first_ref,
    block_ref,
    gate_ref,
    up_ref,
    down_ref,
    grads_ref,
    hidden_ref,
    pregate_ref,
    preup_ref,
    x,
    xt,
    sc,
    st,
):
    step = pl.program_id(0)
    sources = block_ref.shape[0]
    tok_dev = 128
    rows, model_dim = x.shape
    capacity = rows // (steps * sources)
    shards, _, shard_rows, _ = grads_ref.shape

    @pl.when(step < steps)
    def _():
        before = (
            lax.broadcasted_iota(jnp.int32, (tok_dev, tok_dev), 0)
            < lax.broadcasted_iota(jnp.int32, (tok_dev, tok_dev), 1)
        ).astype(BF16)
        column = lax.broadcasted_iota(jnp.int32, (capacity, tok_dev), 0).astype(F32)
        expert = first_ref[0].astype(F32)
        names, gates = [], []
        for j in range(sources):
            routing = block_ref[j, 2 * tok_dev :, :tok_dev].astype(F32)
            hit = routing[:8] == expert
            names.append(jnp.max(jnp.where(hit, 1.0, 0.0), axis=0, keepdims=True))
            gates.append(jnp.sum(jnp.where(hit, routing[8:], 0.0), axis=0, keepdims=True))
        names = jnp.concatenate(names + [jnp.zeros((8 - sources, tok_dev), F32)])
        ranks = dot(names.astype(BF16), before)
        picked = []
        none = jnp.zeros((capacity, tok_dev), F32)
        for j in range(sources):
            here = (ranks[j : j + 1] == column) & (names[j : j + 1] > 0.0)
            place = jnp.concatenate([jnp.where(here, 1.0, 0.0), none], axis=1)
            weight = jnp.concatenate([none, jnp.where(here, gates[j], 0.0)], axis=1)
            picks = jnp.concatenate([place, weight]).astype(BF16)
            picked.append(dot(picks, block_ref[j, : 2 * tok_dev, :]))
        span = pl.ds(pl.multiple_of(step * sources * capacity, sources * capacity), sources * capacity)
        x[span, :] = jnp.concatenate([pair[:capacity] for pair in picked]).astype(BF16)
        sc[span, :] = jnp.concatenate([pair[capacity:] for pair in picked]).astype(BF16)

    for part in range(2):
        span = slice(part * rows // 2, (part + 1) * rows // 2)

        @pl.when(step == (part + 1) * steps // 2 - 1)
        def _():
            xt[:, span] = x[span, :].T
            st[:, span] = sc[span, :].T

    @pl.when(step >= steps)
    def _():
        pre_gate = dot(x[...], gate_ref[...])
        pre_up = dot(x[...], up_ref[...])
        grad_hidden = dot(sc[...], down_ref[...], CONTRACT_LAST)
        s = jax.nn.sigmoid(pre_gate)
        activation = pre_gate * s
        hidden = (activation * pre_up).astype(BF16)
        grad_pregate = (grad_hidden * pre_up * (s * (1.0 + pre_gate * (1.0 - s)))).astype(BF16)
        grad_preup = (grad_hidden * activation).astype(BF16)
        hidden_ref[...] = hidden
        pregate_ref[...] = grad_pregate
        preup_ref[...] = grad_preup
        for which, (left, right) in enumerate(((xt, grad_pregate), (xt, grad_preup), (st, hidden))):
            product = dot(left[...], right).astype(BF16)
            for r in range(shards):
                grads_ref[r, which] = product[r * shard_rows : (r + 1) * shard_rows]


def expert_grads(gathered, expert, gate_proj, up_proj, down_proj, e, capacity, shards):
    group, height, model_dim = gathered.shape
    rows = group * capacity
    hidden_dim = gate_proj.shape[2]
    tile = 256
    sources = 4
    steps = group // sources

    def at(s):
        return jnp.maximum(s - steps, 0)

    narrow = pl.BlockSpec((rows, tile), lambda s: (0, at(s)))
    return pl.pallas_call(
        functools.partial(grads_kernel, steps),
        grid=(steps + hidden_dim // tile,),
        in_specs=[
            pl.BlockSpec(memory_space=pltpu.SMEM),
            pl.BlockSpec((sources, height, model_dim), lambda s: (jnp.minimum(s, steps - 1), 0, 0)),
            pl.BlockSpec((None, model_dim, tile), lambda s: (e, 0, at(s))),
            pl.BlockSpec((None, model_dim, tile), lambda s: (e, 0, at(s))),
            pl.BlockSpec((None, tile, model_dim), lambda s: (e, at(s), 0)),
        ],
        out_specs=[
            pl.BlockSpec((shards, 3, model_dim // shards, tile), lambda s: (0, 0, 0, at(s))),
            narrow,
            narrow,
            narrow,
        ],
        out_shape=[jax.ShapeDtypeStruct((shards, 3, model_dim // shards, hidden_dim), BF16)]
        + [jax.ShapeDtypeStruct((rows, hidden_dim), BF16)] * 3,
        scratch_shapes=[pltpu.VMEM((rows, model_dim), BF16), pltpu.VMEM((model_dim, rows), BF16)] * 2,
        compiler_params=pltpu.CompilerParams(vmem_limit_bytes=60 << 20),
        cost_estimate=pl.CostEstimate(
            flops=12 * rows * model_dim * hidden_dim,
            bytes_accessed=2 * gathered.size + 12 * model_dim * hidden_dim + 6 * rows * hidden_dim,
            transcendentals=rows * hidden_dim,
        ),
    )(expert, gathered, gate_proj, up_proj, down_proj)


def returns_kernel(hidden_ref, pregate_ref, preup_ref, gate_ref, up_ref, down_ref, back_ref):
    group, height, _ = back_ref.shape
    capacity = height // 2
    out = dot(hidden_ref[...], down_ref[...])
    part = dot(pregate_ref[...], gate_ref[...], CONTRACT_LAST) + dot(preup_ref[...], up_ref[...], CONTRACT_LAST)
    for source in range(group):
        rows = slice(source * capacity, (source + 1) * capacity)
        back_ref[source] = jnp.concatenate([out[rows], part[rows]]).astype(BF16)


def expert_returns(hidden, pregate, preup, gate_proj, up_proj, down_proj, e, group):
    rows, hidden_dim = hidden.shape
    model_dim = gate_proj.shape[1]
    capacity = rows // group
    tile = 512
    whole = pl.BlockSpec((rows, hidden_dim), lambda d: (0, 0), pipeline_mode=pl.Buffered(1))
    return pl.pallas_call(
        returns_kernel,
        grid=(model_dim // tile,),
        in_specs=[
            whole,
            whole,
            whole,
            pl.BlockSpec((None, tile, hidden_dim), lambda d: (e, d, 0)),
            pl.BlockSpec((None, tile, hidden_dim), lambda d: (e, d, 0)),
            pl.BlockSpec((None, hidden_dim, tile), lambda d: (e, 0, d)),
        ],
        out_specs=pl.BlockSpec((group, 2 * capacity, tile), lambda d: (0, 0, d)),
        out_shape=jax.ShapeDtypeStruct((group, 2 * capacity, model_dim), BF16),
        compiler_params=pltpu.CompilerParams(vmem_limit_bytes=60 << 20),
        cost_estimate=pl.CostEstimate(
            flops=600 * rows * model_dim * hidden_dim,
            bytes_accessed=4 * rows * model_dim + 6 * model_dim * hidden_dim + 6 * rows * hidden_dim,
            transcendentals=0,
        ),
    )(hidden, pregate, preup, gate_proj, up_proj, down_proj)


def finish_kernel(experts, cotangent_ref, *refs):
    pairs, reduced = refs[: 2 * experts], refs[2 * experts : 3 * experts]
    combined_ref, tokens_ref, products_ref, gate_ref, up_ref, down_ref, total = refs[3 * experts :]
    tok_dev = combined_ref.shape[0]
    devices, height, model_dim = pairs[0].shape
    step = pl.program_id(0)

    for e in range(experts):
        gate_ref[e] = reduced[e][0]
        up_ref[e] = reduced[e][1]
        down_ref[e] = reduced[e][2].T

    sums = None
    for e in range(experts):
        rows = pairs[2 * e][...].reshape(devices * height, model_dim)
        picks = pairs[2 * e + 1][...]
        part = dot(picks, rows, CONTRACT_FIRST)
        sums = part if sums is None else sums + part
        product = dot(rows, cotangent_ref[...], CONTRACT_LAST)
        product = jnp.where(picks[:, :tok_dev].astype(F32) > 0.0, product, 0.0)
        for d in range(devices):
            products_ref[e, d] = jnp.sum(product[d * height : d * height + height // 2], axis=0, keepdims=True)

    @pl.when(step == 0)
    def _():
        total[...] = sums

    @pl.when(step > 0)
    def _():
        total[...] += sums

    @pl.when(step == pl.num_programs(0) - 1)
    def _():
        combined_ref[...] = total[:tok_dev].astype(BF16)
        tokens_ref[...] = total[tok_dev:].astype(BF16)


def finish(cotangent, returned, picks, reduced):
    experts = len(returned)
    group, height, model_dim = returned[0].shape
    tok_dev = cotangent.shape[0]
    _, shard_rows, hidden_dim = reduced[0].shape
    steps = 2
    step, tile = group // steps, hidden_dim // steps
    whole = pl.BlockSpec((tok_dev, model_dim), lambda s: (0, 0))
    straight = pl.BlockSpec((experts, shard_rows, tile), lambda s: (0, 0, s))
    return pl.pallas_call(
        functools.partial(finish_kernel, experts),
        grid=(steps,),
        in_specs=[whole]
        + [
            pl.BlockSpec((step, height, model_dim), lambda s: (s, 0, 0)),
            pl.BlockSpec((step * height, 2 * tok_dev), lambda s: (s, 0)),
        ]
        * experts
        + [pl.BlockSpec((3, shard_rows, tile), lambda s: (0, 0, s))] * experts,
        out_specs=[
            whole,
            whole,
            pl.BlockSpec((experts, step, 1, tok_dev), lambda s: (0, s, 0, 0)),
            straight,
            straight,
            pl.BlockSpec((experts, tile, shard_rows), lambda s: (0, s, 0)),
        ],
        out_shape=[
            jax.ShapeDtypeStruct((tok_dev, model_dim), BF16),
            jax.ShapeDtypeStruct((tok_dev, model_dim), BF16),
            jax.ShapeDtypeStruct((experts, group, 1, tok_dev), F32),
            jax.ShapeDtypeStruct((experts, shard_rows, hidden_dim), BF16),
            jax.ShapeDtypeStruct((experts, shard_rows, hidden_dim), BF16),
            jax.ShapeDtypeStruct((experts, hidden_dim, shard_rows), BF16),
        ],
        scratch_shapes=[pltpu.VMEM((2 * tok_dev, model_dim), F32)],
        compiler_params=pltpu.CompilerParams(vmem_limit_bytes=60 << 20),
        cost_estimate=pl.CostEstimate(
            flops=6 * experts * group * height * tok_dev * model_dim,
            bytes_accessed=2 * experts * (group * height * (model_dim + 2 * tok_dev) + 6 * shard_rows * hidden_dim),
            transcendentals=0,
        ),
    )(cotangent, *[v for pair in zip(returned, picks) for v in pair], *reduced)


def exchange(rows):
    return lax.all_to_all(rows, "expert", split_axis=0, concat_axis=0, tiled=True)


def local(tokens, cotangent, expert_ids, gate_weights, token_counts, gate_proj, up_proj, down_proj):
    group = lax.axis_size("expert")
    shards = lax.axis_size("dp")
    local_experts, model_dim, hidden_dim = gate_proj.shape
    tok_dev, top = expert_ids.shape
    experts_total = group * local_experts
    capacity = 3 * tok_dev * top // (2 * experts_total)

    live = lax.broadcasted_iota(jnp.int32, (tok_dev, top), 0) < token_counts[0]
    named = jnp.where(live, expert_ids, NOBODY)
    routing = jnp.concatenate([named.T.astype(BF16), gate_weights.T])
    routing = jnp.pad(routing, ((0, 0), (0, model_dim - tok_dev)))
    gathered = lax.all_gather(
        jnp.concatenate([tokens, cotangent, routing])[None], "expert", axis=0, tiled=True
    )

    labels = lax.broadcasted_iota(jnp.int32, (experts_total, 1, 1), 0)
    hits = named.T[None] == labels
    names = jnp.any(hits, axis=1)
    gates = jnp.sum(jnp.where(hits, gate_weights.T[None].astype(F32), 0.0), axis=1)
    before = (
        lax.broadcasted_iota(jnp.int32, (tok_dev, tok_dev), 0)
        < lax.broadcasted_iota(jnp.int32, (tok_dev, tok_dev), 1)
    )
    rank = dot(names.astype(BF16), before.astype(BF16)).astype(jnp.int32)
    names, gates, rank = (v.reshape(group, local_experts, 1, tok_dev) for v in (names, gates, rank))
    column = lax.broadcasted_iota(jnp.int32, (1, 2 * capacity, 1), 1)
    picks = []
    for e in range(local_experts):
        place = names[:, e] & (rank[:, e] == column)
        second = names[:, e] & (rank[:, e] + capacity == column)
        picks.append(
            jnp.concatenate([jnp.where(place, gates[:, e], 0.0).astype(BF16), second.astype(BF16)], axis=2)
            .reshape(-1, 2 * tok_dev)
        )

    gathered, *picks = lax.optimization_barrier((gathered, *picks))
    first = (lax.axis_index("expert") * local_experts).astype(jnp.int32).reshape(1)

    returned, reduced = [], []
    for e in range(local_experts):
        grads, hidden, pregate, preup = expert_grads(
            gathered, first + e, gate_proj, up_proj, down_proj, e, capacity, shards
        )
        reduced.append(lax.psum_scatter(grads, "dp", scatter_dimension=0, tiled=False))
        back = expert_returns(hidden, pregate, preup, gate_proj, up_proj, down_proj, e, group)
        returned.append(exchange(back))

    combined, tokens_grad, products, *weight_grads = finish(cotangent, returned, picks, reduced)
    per_expert = products.transpose(1, 0, 2, 3).reshape(experts_total, 1, tok_dev)
    gates_grad = jnp.sum(jnp.where(hits, per_expert, 0.0), axis=0).T
    return (
        combined,
        tokens_grad,
        gates_grad.astype(BF16),
        *weight_grads,
    )


def solution(mesh):
    both = ("dp", "expert")
    return jax.shard_map(
        local,
        mesh=mesh,
        in_specs=(
            P(both, None),
            P(both, None),
            P(both, None),
            P(both, None),
            P(both),
            P("expert", None, None),
            P("expert", None, None),
            P("expert", None, None),
        ),
        out_specs=(
            P(both, None),
            P(both, None),
            P(both, None),
            P("expert", "dp", None),
            P("expert", "dp", None),
            P("expert", None, "dp"),
        ),
        check_vma=False,
    )
```

time: 421 us -> 380 us (0.903)
  waiting for transfers between devices: 258 us -> 151 us
  blocking collectives: 0 us -> 75.8 us
  Pallas kernels: 81 us -> 119 us
  matrix products: 27.5 us -> 0.14 us
  starting transfers between devices: 23.6 us -> 6.66 us
  local copies, waits for them, and re-layouts: 10.7 us -> 1 us
    all_to_all x4 -> x1, waiting for transfers between devices: 258 us -> 34.1 us  [exchange(): lax.all_to_all(rows, 'expert', split_axis=0, concat_axis=0, tiled=True)]
    all_gather x0 -> x1, waiting for transfers between devices: none -> 117 us  [local(): lax.all_gather(jnp.concatenate([tokens, cotangent, routing])[None], 'expe...]
    all_to_all x0 -> x1, blocking collectives: none -> 75.8 us  [exchange(): lax.all_to_all(rows, 'expert', split_axis=0, concat_axis=0, tiled=True)]
    pallas_call x3, Pallas kernels: 58.9 us -> 94.2 us  [the longest x2 79.9 us: expert_grads(): pl.pallas_call(functools.partial(grads_kernel, steps), grid=(steps + hidd...]
    dot_general x7 -> x1, matrix products: 27.5 us -> 0.14 us  [dot(): return lax.dot_general(a, b, dims, preferred_element_type=F32)]
    all_to_all x4 -> x1, starting transfers between devices: 23.2 us -> 6.36 us  [exchange(): lax.all_to_all(rows, 'expert', split_axis=0, concat_axis=0, tiled=True)]
    unnamed x56 -> x7, local copies, waits for them, and re-layouts: 8.38 us -> 0.02 us
    concatenate x0 -> x4, other arithmetic: none -> 4.96 us  [the longest x1 2.32 us: local(): jnp.concatenate([tokens, cotangent, routing])[None]]
  transfers between devices with their start and end apart: 6 -> 4, of which waited for: 4 -> 2; matrix products, arithmetic and copies ran while one was open for 6% -> 1% of each run, Pallas kernels for 19% -> 17%
where the time goes in v5:
time: 380 us; the launch traced here: 376 us
  waiting for transfers between devices  151 us (40%)
  Pallas kernels  119 us (31%)
  blocking collectives  75.8 us (20%)
  between operations  14.5 us (4%)
  other arithmetic  7.22 us (2%)
  starting transfers between devices  6.66 us (2%)
    all_gather x1, waiting for transfers between devices, local(): lax.all_gather(jnp.concatenate([tokens, cotangent, routing])[None], 'expe...  117 us
    pallas_call x2, Pallas kernels, expert_grads(): pl.pallas_call(functools.partial(grads_kernel, steps), grid=(steps + hidd...  79.9 us
    all_to_all x1, blocking collectives, exchange(): lax.all_to_all(rows, 'expert', split_axis=0, concat_axis=0, tiled=True)  75.8 us
    all_to_all x1, waiting for transfers between devices, exchange(): lax.all_to_all(rows, 'expert', split_axis=0, concat_axis=0, tiled=True)  34.1 us
    pallas_call x2, Pallas kernels, expert_returns(): pl.pallas_call(returns_kernel, grid=(model_dim // tile,), in_specs=[whole...  25.1 us
    pallas_call x1, Pallas kernels, finish(): pl.pallas_call(functools.partial(finish_kernel, experts), grid=(steps,),...  14.3 us
  transfers between devices with their start and end apart: 4, of which 2 were waited for; matrix products, arithmetic and copies ran while one was open for 1% of the time, Pallas kernels for 17%

profile of v5, /device:TPU:32, one launch (start us, length us, event | category | flops | bytes accessed | tf_op | source)
XLA Modules:
  0.0 376.1 jit_solution(17078667199337228585)
XLA Ops:
  7.2 0.0 all-gather.3.cloned.1.call-start
  7.9 0.7 fusion.8
  8.6 0.0 copy-start
  8.6 0.7 fusion.7
  9.3 0.0 copy-start.2
  9.3 2.3 pad_maximum_fusion
  11.6 0.0 all-gather.3.cloned.1.call-update
  11.6 0.0 reduce-scatter.5.cloned.1.call-start
  11.7 0.1 fusion.4
  11.8 0.1 eq.104
  11.9 0.0 copy-done.2
  11.9 0.0 copy-done
  11.9 0.1 select_reduce_fusion.1
  12.0 0.1 convolution_convert_fusion
  12.2 0.4 fusion
  12.6 0.3 fusion.3
  13.0 1.0 pad_maximum_fusion.2.refs_3_
  14.0 1.0 pad_maximum_fusion.1.refs_1_
  14.9 117.3 %all-gather.3.cloned.1.call-done = bf16[8704,2048]{1,0:T(8,128)(2,1)} async-done(((bf16[272,2048]{1,0:T(8,128)(2,1)}), bf16[8704,2048]{1,0:T(8,128)(2,1)}) %all-gather.3.cloned.1.call-update) | async-done | bytes 35651600 | tf_op jit(solution)/shard_map/all_gather | solution.py:275
  132.2 39.8 %shard_map.129 = (bf16[4,3,512,768]{3,2,1,0:T(8,128)(2,1)}, bf16[768,768]{1,0:T(8,128)(2,1)}, bf16[768,768]{1,0:T(8,128)(2,1)}, bf16[768,768]{1,0:T(8,128)(2,1)}) custom-call(s32[1]{0:T(128)S(6)} %add.27.first_ref, bf16[32,272,2048]{2,1,0:T(8,128)(2,1)} %bitcast.75, bf16[2,2048,768]{2,1,0:T(8,128)(2,1)} %gate_ref.7, bf16[2,2048,768]{2,1,0:T(8,128)(2,1)} %up_ref.7, ...), custom_call_target="tpu_custom_call" | custom-call | flops 14495514624 | bytes 58064896 | tf_op jit(solution)/shard_map/pallas_call | solution.py:111
  172.0 0.0 reduce-scatter.5.cloned.1.call-update
  172.1 12.5 %shard_map.130 = bf16[32,48,2048]{2,1,0:T(8,128)(2,1)} custom-call(bf16[768,768]{1,0:T(8,128)(2,1)} %get-tuple-element.28.hidden_ref, bf16[768,768]{1,0:T(8,128)(2,1)} %get-tuple-element.29.pregate_ref, bf16[768,768]{1,0:T(8,128)(2,1)} %get-tuple-element.30.preup_ref, bf16[2,2048,768]{2,1,0:T(8,128)(2,1)} %gate_ref.7, bf16[2,2048,768]{2,1,0:T(8,128)(2,1)} %up_ref.7, ...), custom_call_target="tpu_custom_call" | custom-call | flops 724775731200 | bytes 19267584 | tf_op jit(solution)/shard_map/pallas_call | solution.py:155
  184.6 6.4 %all-to-all-start.1 = ((bf16[32,48,2048]{2,1,0:T(8,128)(2,1)}), bf16[32,48,2048]{2,1,0:T(8,128)(2,1)}, u32[]{:S(2)}, u32[]{:S(2)}) async-start(bf16[32,48,2048]{2,1,0:T(8,128)(2,1)} %shard_map.130), calls=%async_computation.1 | async-start | bytes 12582912 | tf_op jit(solution)/shard_map/all_to_all | solution.py:260
  190.9 0.2 reduce-scatter.3.cloned.1.call-start
  191.2 40.1 %shard_map.127 = (bf16[4,3,512,768]{3,2,1,0:T(8,128)(2,1)}, bf16[768,768]{1,0:T(8,128)(2,1)}, bf16[768,768]{1,0:T(8,128)(2,1)}, bf16[768,768]{1,0:T(8,128)(2,1)}) custom-call(s32[1]{0:T(128)} %bitcast.first_ref, bf16[32,272,2048]{2,1,0:T(8,128)(2,1)} %bitcast.76, bf16[2,2048,768]{2,1,0:T(8,128)(2,1)} %gate_ref.7, bf16[2,2048,768]{2,1,0:T(8,128)(2,1)} %up_ref.7, ...), custom_call_target="tpu_custom_call" | custom-call | flops 14495514624 | bytes 58064896 | tf_op jit(solution)/shard_map/pallas_call | solution.py:111
  231.3 0.0 reduce-scatter.3.cloned.1.call-update
  231.3 12.5 %shard_map.128 = bf16[32,48,2048]{2,1,0:T(8,128)(2,1)} custom-call(bf16[768,768]{1,0:T(8,128)(2,1)} %get-tuple-element.24.hidden_ref, bf16[768,768]{1,0:T(8,128)(2,1)} %get-tuple-element.25.pregate_ref, bf16[768,768]{1,0:T(8,128)(2,1)} %get-tuple-element.26.preup_ref, bf16[2,2048,768]{2,1,0:T(8,128)(2,1)} %gate_ref.7, bf16[2,2048,768]{2,1,0:T(8,128)(2,1)} %up_ref.7, ...), custom_call_target="tpu_custom_call" | custom-call | flops 724775731200 | bytes 19267584 | tf_op jit(solution)/shard_map/pallas_call | solution.py:155
  243.9 34.1 %all-to-all-done.1.refs_2_ = bf16[32,48,2048]{2,1,0:T(8,128)(2,1)} async-done(((bf16[32,48,2048]{2,1,0:T(8,128)(2,1)}), bf16[32,48,2048]{2,1,0:T(8,128)(2,1)}, u32[]{:S(2)}, u32[]{:S(2)}) %all-to-all-start.1) | async-done | bytes 6291488 | tf_op jit(solution)/shard_map/all_to_all | solution.py:260
  278.0 75.8 %all_to_all.10.refs_0_ = bf16[32,48,2048]{2,1,0:T(8,128)(2,1)} all-to-all(bf16[32,48,2048]{2,1,0:T(8,128)(2,1)} %shard_map.128), channel_id=1, replica_groups=mesh['dp'=4,'expert'=32] {'expert'}, dimensions={0} | all-to-all | bytes 12582912 | tf_op jit(solution)/shard_map/all_to_all | solution.py:260
  353.8 0.0 reduce-scatter.5.cloned.1.call-done
  353.8 0.0 reduce-scatter.3.cloned.1.call-done
  353.8 0.0 copy-start.1
  353.8 14.3 %shard_map.131 = (bf16[128,2048]{1,0:T(8,128)(2,1)}, bf16[128,2048]{1,0:T(8,128)(2,1)}, f32[2,32,1,128]{3,2,1,0:T(1,128)}, bf16[2,512,768]{2,1,0:T(8,128)(2,1)},...) custom-call(bf16[128,2048]{1,0:T(8,128)(2,1)} %cotangent_ref.1, bf16[32,48,2048]{2,1,0:T(8,128)(2,1)} %all_to_all.10.refs_0_, ...), custom_call_target="tpu_custom_call" | custom-call | flops 4831838208 | bytes 23592960 | tf_op jit(solution)/shard_map/pallas_call | solution.py:223
  368.1 0.8 copy.20
  368.9 0.0 copy-done.1
  368.9 0.6 select_reduce_fusion
  (9 shorter events, 0.1 us)
Async XLA Ops:
  7.2 125.0 %all-gather.3.cloned.1.call-start = ((), (), s32[]{:S(2)}) async-start(), calls=%async_computation.6 | async-start | bytes 36765696 | tf_op jit(solution)/shard_map/all_gather | solution.py:275
  8.6 3.3 copy-start
  9.3 2.6 copy-start.2
  11.6 342.2 %reduce-scatter.5.cloned.1.call-start = ((), (), s32[]{:S(2)}) async-start(), calls=%async_computation.5 | async-start | bytes 11796480 | tf_op jit(solution)/shard_map/reduce_scatter | solution.py:307
  184.6 93.4 %all-to-all-start.1 = ((bf16[32,48,2048]{2,1,0:T(8,128)(2,1)}), bf16[32,48,2048]{2,1,0:T(8,128)(2,1)}, u32[]{:S(2)}, u32[]{:S(2)}) async-start(bf16[32,48,2048]{2,1,0:T(8,128)(2,1)} %shard_map.130), calls=%async_computation.1 | async-start | bytes 12582912 | tf_op jit(solution)/shard_map/all_to_all | solution.py:260
  190.9 162.9 %reduce-scatter.3.cloned.1.call-start = ((), (), s32[]{:S(2)}) async-start(), calls=%async_computation.4 | async-start | bytes 11796480 | tf_op jit(solution)/shard_map/reduce_scatter | solution.py:307
  353.8 15.1 %copy-start.1 = (s32[8,128]{1,0:T(8,128)S(1)}, s32[8,128]{1,0:T(8,128)}, u32[]{:S(2)}) copy-start(s32[8,128]{1,0:T(8,128)} %copy-done) | copy-start | bytes 12292
Sparse Core Ops, SparseCore 0:
  11.7 120.4 all-gather.2
  172.2 89.1 reduce-scatter.4
  263.8 88.6 reduce-scatter.2

commit v6 on v5

--- a/solution.py
+++ b/solution.py
@@ -18,53 +18,26 @@
     return lax.dot_general(a, b, dims, preferred_element_type=F32)
 
 
-def grads_kernel(
-    steps,
-    first_ref,
-    block_ref,
-    gate_ref,
-    up_ref,
-    down_ref,
-    grads_ref,
-    hidden_ref,
-    pregate_ref,
-    preup_ref,
-    x,
-    xt,
-    sc,
-    st,
-):
+def grads_kernel(steps, sources, e, plan_ref, *refs):
+    blocks, (gate_ref, up_ref, down_ref) = refs[:sources], refs[sources : sources + 3]
+    grads_ref, hidden_ref, pregate_ref, preup_ref, x, xt, sc, st = refs[sources + 3 :]
     step = pl.program_id(0)
-    sources = block_ref.shape[0]
-    tok_dev = 128
+    tok_dev = plan_ref.shape[2]
     rows, model_dim = x.shape
     capacity = rows // (steps * sources)
     shards, _, shard_rows, _ = grads_ref.shape
 
     @pl.when(step < steps)
     def _():
-        before = (
-            lax.broadcasted_iota(jnp.int32, (tok_dev, tok_dev), 0)
-            < lax.broadcasted_iota(jnp.int32, (tok_dev, tok_dev), 1)
-        ).astype(BF16)
         column = lax.broadcasted_iota(jnp.int32, (capacity, tok_dev), 0).astype(F32)
-        expert = first_ref[0].astype(F32)
-        names, gates = [], []
+        none = jnp.zeros((capacity, tok_dev), F32)
+        picked = []
         for j in range(sources):
-            routing = block_ref[j, 2 * tok_dev :, :tok_dev].astype(F32)
-            hit = routing[:8] == expert
-            names.append(jnp.max(jnp.where(hit, 1.0, 0.0), axis=0, keepdims=True))
-            gates.append(jnp.sum(jnp.where(hit, routing[8:], 0.0), axis=0, keepdims=True))
-        names = jnp.concatenate(names + [jnp.zeros((8 - sources, tok_dev), F32)])
-        ranks = dot(names.astype(BF16), before)
-        picked = []
-        none = jnp.zeros((capacity, tok_dev), F32)
-        for j in range(sources):
-            here = (ranks[j : j + 1] == column) & (names[j : j + 1] > 0.0)
+            here = plan_ref[j, 2 * e : 2 * e + 1, :] == column
             place = jnp.concatenate([jnp.where(here, 1.0, 0.0), none], axis=1)
-            weight = jnp.concatenate([none, jnp.where(here, gates[j], 0.0)], axis=1)
+            weight = jnp.concatenate([none, jnp.where(here, plan_ref[j, 2 * e + 1 : 2 * e + 2, :], 0.0)], axis=1)
             picks = jnp.concatenate([place, weight]).astype(BF16)
-            picked.append(dot(picks, block_ref[j, : 2 * tok_dev, :]))
+            picked.append(dot(picks, blocks[j][...]))
         span = pl.ds(pl.multiple_of(step * sources * capacity, sources * capacity), sources * capacity)
         x[span, :] = jnp.concatenate([pair[:capacity] for pair in picked]).astype(BF16)
         sc[span, :] = jnp.concatenate([pair[capacity:] for pair in picked]).astype(BF16)
@@ -96,7 +69,7 @@
                 grads_ref[r, which] = product[r * shard_rows : (r + 1) * shard_rows]
 
 
-def expert_grads(gathered, expert, gate_proj, up_proj, down_proj, e, capacity, shards):
+def expert_grads(gathered, plan, gate_proj, up_proj, down_proj, e, capacity, shards):
     group, height, model_dim = gathered.shape
     rows = group * capacity
     hidden_dim = gate_proj.shape[2]
@@ -107,13 +80,16 @@
     def at(s):
         return jnp.maximum(s - steps, 0)
 
+    def source(j):
+        return lambda s: (jnp.minimum(s, steps - 1) * sources + j, 0, 0)
+
     narrow = pl.BlockSpec((rows, tile), lambda s: (0, at(s)))
     return pl.pallas_call(
-        functools.partial(grads_kernel, steps),
+        functools.partial(grads_kernel, steps, sources, e),
         grid=(steps + hidden_dim // tile,),
         in_specs=[
-            pl.BlockSpec(memory_space=pltpu.SMEM),
-            pl.BlockSpec((sources, height, model_dim), lambda s: (jnp.minimum(s, steps - 1), 0, 0)),
+            pl.BlockSpec((sources, *plan.shape[1:]), lambda s: (jnp.minimum(s, steps - 1), 0, 0)),
+            *[pl.BlockSpec((None, height, model_dim), source(j)) for j in range(sources)],
             pl.BlockSpec((None, model_dim, tile), lambda s: (e, 0, at(s))),
             pl.BlockSpec((None, model_dim, tile), lambda s: (e, 0, at(s))),
             pl.BlockSpec((None, tile, model_dim), lambda s: (e, at(s), 0)),
@@ -133,7 +109,7 @@
             bytes_accessed=2 * gathered.size + 12 * model_dim * hidden_dim + 6 * rows * hidden_dim,
             transcendentals=rows * hidden_dim,
         ),
-    )(expert, gathered, gate_proj, up_proj, down_proj)
+    )(plan, *[gathered] * sources, gate_proj, up_proj, down_proj)
 
 
 def returns_kernel(hidden_ref, pregate_ref, preup_ref, gate_ref, up_ref, down_ref, back_ref):
@@ -270,11 +246,7 @@
 
     live = lax.broadcasted_iota(jnp.int32, (tok_dev, top), 0) < token_counts[0]
     named = jnp.where(live, expert_ids, NOBODY)
-    routing = jnp.concatenate([named.T.astype(BF16), gate_weights.T])
-    routing = jnp.pad(routing, ((0, 0), (0, model_dim - tok_dev)))
-    gathered = lax.all_gather(
-        jnp.concatenate([tokens, cotangent, routing])[None], "expert", axis=0, tiled=True
-    )
+    gathered = lax.all_gather(jnp.concatenate([tokens, cotangent])[None], "expert", axis=0, tiled=True)
 
     labels = lax.broadcasted_iota(jnp.int32, (experts_total, 1, 1), 0)
     hits = named.T[None] == labels
@@ -296,13 +268,15 @@
             .reshape(-1, 2 * tok_dev)
         )
 
-    gathered, *picks = lax.optimization_barrier((gathered, *picks))
-    first = (lax.axis_index("expert") * local_experts).astype(jnp.int32).reshape(1)
+    slots = jnp.where(names, rank.astype(F32), -1.0)
+    plan = jnp.concatenate([slots, gates], axis=2).reshape(group, 2 * local_experts, tok_dev)
+    plan = exchange(jnp.pad(plan, ((0, 0), (0, 8 - 2 * local_experts), (0, 0))))
+    gathered, plan, *picks = lax.optimization_barrier((gathered, plan, *picks))
 
     returned, reduced = [], []
     for e in range(local_experts):
         grads, hidden, pregate, preup = expert_grads(
-            gathered, first + e, gate_proj, up_proj, down_proj, e, capacity, shards
+            gathered, plan, gate_proj, up_proj, down_proj, e, capacity, shards
         )
         reduced.append(lax.psum_scatter(grads, "dp", scatter_dimension=0, tiled=False))
         back = expert_returns(hidden, pregate, preup, gate_proj, up_proj, down_proj, e, group)

time: 380 us -> 373 us (0.982)
  waiting for transfers between devices: 151 us -> 138 us
  starting transfers between devices: 6.66 us -> 14.7 us
    all_gather x1, waiting for transfers between devices: 117 us -> 99.7 us  [local(): lax.all_gather(jnp.concatenate([tokens, cotangent])[None], 'expert', axis...]
    all_to_all x1 -> x2, starting transfers between devices: 6.36 us -> 14.4 us  [exchange(): lax.all_to_all(rows, 'expert', split_axis=0, concat_axis=0, tiled=True)]
    all_to_all x1 -> x2, waiting for transfers between devices: 34.1 us -> 38.4 us  [exchange(): lax.all_to_all(rows, 'expert', split_axis=0, concat_axis=0, tiled=True)]
  transfers between devices with their start and end apart: 4 -> 5, of which waited for: 2 -> 3; matrix products, arithmetic and copies ran while one was open for 1% -> 1% of each run, Pallas kernels for 17% -> 18%
where the time goes in v6:
time: 373 us; the launch traced here: 369 us
  waiting for transfers between devices  138 us (37%)
  Pallas kernels  118 us (32%)
  blocking collectives  75.8 us (20%)
  starting transfers between devices  14.7 us (4%)
  between operations  14.6 us (4%)
  other arithmetic  5.89 us (2%)
    all_gather x1, waiting for transfers between devices, local(): lax.all_gather(jnp.concatenate([tokens, cotangent])[None], 'expert', axis...  99.7 us
    pallas_call x2, Pallas kernels, expert_grads(): pl.pallas_call(functools.partial(grads_kernel, steps, sources, e), grid=(...  78.6 us
    all_to_all x1, blocking collectives, exchange(): lax.all_to_all(rows, 'expert', split_axis=0, concat_axis=0, tiled=True)  75.8 us
    all_to_all x2, waiting for transfers between devices, exchange(): lax.all_to_all(rows, 'expert', split_axis=0, concat_axis=0, tiled=True)  38.4 us
    pallas_call x2, Pallas kernels, expert_returns(): pl.pallas_call(returns_kernel, grid=(model_dim // tile,), in_specs=[whole...  25.3 us
    all_to_all x2, starting transfers between devices, exchange(): lax.all_to_all(rows, 'expert', split_axis=0, concat_axis=0, tiled=True)  14.4 us
    pallas_call x1, Pallas kernels, finish(): pl.pallas_call(functools.partial(finish_kernel, experts), grid=(steps,),...  14.3 us
  transfers between devices with their start and end apart: 5, of which 3 were waited for; matrix products, arithmetic and copies ran while one was open for 1% of the time, Pallas kernels for 18%

profile of v6, /device:TPU:32, one launch (start us, length us, event | category | flops | bytes accessed | tf_op | source)
XLA Modules:
  0.0 369.2 jit_solution(7450982607533212724)
XLA Ops:
  7.2 0.0 copy-start.3
  7.2 0.0 copy-start.4
  7.2 0.0 all-gather.3.cloned.1.call-start
  7.2 2.3 pad_maximum_fusion
  9.5 0.0 all-gather.3.cloned.1.call-update
  10.2 0.0 copy-done.3
  10.2 0.0 copy-start.1
  10.2 0.1 fusion.4
  10.3 0.0 copy-done.4
  10.4 0.1 select_reduce_fusion.1
  10.5 0.1 convolution_convert_fusion
  10.7 0.1 copy.19
  10.7 0.7 pad.4
  11.4 0.0 copy-done.1
  11.4 8.2 %all-to-all-start = ((f32[32,8,128]{2,1,0:T(8,128)}), f32[32,8,128]{2,1,0:T(8,128)S(1)}, u32[]{:S(2)}, u32[]{:S(2)}) async-start(f32[32,8,128]{2,1,0:T(8,128)} %pad.4), calls=%async_computation | async-start | bytes 262144 | tf_op jit(solution)/shard_map/all_to_all | solution.py:236
  19.6 0.0 reduce-scatter.5.cloned.1.call-start
  19.7 0.1 eq.104
  19.9 0.4 fusion
  20.3 0.3 fusion.3
  20.6 1.0 pad_maximum_fusion.2.refs_3_
  21.7 1.0 pad_maximum_fusion.1.refs_1_
  22.6 3.6 all-to-all-done.plan_ref
  26.2 0.0 copy-start
  26.2 99.7 %all-gather.3.cloned.1.call-done = bf16[8192,2048]{1,0:T(8,128)(2,1)} async-done(((bf16[256,2048]{1,0:T(8,128)(2,1)}), bf16[8192,2048]{1,0:T(8,128)(2,1)}) %all-gather.3.cloned.1.call-update) | async-done | bytes 33554448 | tf_op jit(solution)/shard_map/all_gather | solution.py:249
  125.9 0.0 copy-done
  125.9 39.1 %shard_map.129 = (bf16[4,3,512,768]{3,2,1,0:T(8,128)(2,1)}, bf16[768,768]{1,0:T(8,128)(2,1)}, bf16[768,768]{1,0:T(8,128)(2,1)}, bf16[768,768]{1,0:T(8,128)(2,1)}) custom-call(f32[32,8,128]{2,1,0:T(8,128)} %copy-done, bf16[32,256,2048]{2,1,0:T(8,128)(2,1)} %bitcast.74, bf16[32,256,2048]{2,1,0:T(8,128)(2,1)} %bitcast.75, bf16[32,256,2048]{2,1,0:T(8,128)(2,1)} %bitcast.76, ...), custom_call_target="tpu_custom_call" | custom-call | flops 14495514624 | bytes 55967744 | tf_op jit(solution)/shard_map/pallas_call | solution.py:87
  165.1 0.0 reduce-scatter.5.cloned.1.call-update
  165.1 12.8 %shard_map.130 = bf16[32,48,2048]{2,1,0:T(8,128)(2,1)} custom-call(bf16[768,768]{1,0:T(8,128)(2,1)} %get-tuple-element.30.hidden_ref, bf16[768,768]{1,0:T(8,128)(2,1)} %get-tuple-element.31.pregate_ref, bf16[768,768]{1,0:T(8,128)(2,1)} %get-tuple-element.32.preup_ref, bf16[2,2048,768]{2,1,0:T(8,128)(2,1)} %gate_ref.3, bf16[2,2048,768]{2,1,0:T(8,128)(2,1)} %up_ref.3, ...), custom_call_target="tpu_custom_call" | custom-call | flops 724775731200 | bytes 19267584 | tf_op jit(solution)/shard_map/pallas_call | solution.py:131
  177.8 6.2 %all-to-all-start.2 = ((bf16[32,48,2048]{2,1,0:T(8,128)(2,1)}), bf16[32,48,2048]{2,1,0:T(8,128)(2,1)}, u32[]{:S(2)}, u32[]{:S(2)}) async-start(bf16[32,48,2048]{2,1,0:T(8,128)(2,1)} %shard_map.130), calls=%async_computation.2 | async-start | bytes 12582912 | tf_op jit(solution)/shard_map/all_to_all | solution.py:236
  184.1 0.2 reduce-scatter.3.cloned.1.call-start
  184.3 39.5 %shard_map.127 = (bf16[4,3,512,768]{3,2,1,0:T(8,128)(2,1)}, bf16[768,768]{1,0:T(8,128)(2,1)}, bf16[768,768]{1,0:T(8,128)(2,1)}, bf16[768,768]{1,0:T(8,128)(2,1)}) custom-call(f32[32,8,128]{2,1,0:T(8,128)} %copy-done, bf16[32,256,2048]{2,1,0:T(8,128)(2,1)} %bitcast.78, bf16[32,256,2048]{2,1,0:T(8,128)(2,1)} %bitcast.79, bf16[32,256,2048]{2,1,0:T(8,128)(2,1)} %bitcast.80, ...), custom_call_target="tpu_custom_call" | custom-call | flops 14495514624 | bytes 55967744 | tf_op jit(solution)/shard_map/pallas_call | solution.py:87
  223.8 0.0 reduce-scatter.3.cloned.1.call-update
  223.8 12.5 %shard_map.128 = bf16[32,48,2048]{2,1,0:T(8,128)(2,1)} custom-call(bf16[768,768]{1,0:T(8,128)(2,1)} %get-tuple-element.26.hidden_ref, bf16[768,768]{1,0:T(8,128)(2,1)} %get-tuple-element.27.pregate_ref, bf16[768,768]{1,0:T(8,128)(2,1)} %get-tuple-element.28.preup_ref, bf16[2,2048,768]{2,1,0:T(8,128)(2,1)} %gate_ref.3, bf16[2,2048,768]{2,1,0:T(8,128)(2,1)} %up_ref.3, ...), custom_call_target="tpu_custom_call" | custom-call | flops 724775731200 | bytes 19267584 | tf_op jit(solution)/shard_map/pallas_call | solution.py:131
  236.3 34.8 %all-to-all-done.2.refs_2_ = bf16[32,48,2048]{2,1,0:T(8,128)(2,1)} async-done(((bf16[32,48,2048]{2,1,0:T(8,128)(2,1)}), bf16[32,48,2048]{2,1,0:T(8,128)(2,1)}, u32[]{:S(2)}, u32[]{:S(2)}) %all-to-all-start.2) | async-done | bytes 6291488 | tf_op jit(solution)/shard_map/all_to_all | solution.py:236
  271.1 75.8 %all_to_all.15.refs_0_ = bf16[32,48,2048]{2,1,0:T(8,128)(2,1)} all-to-all(bf16[32,48,2048]{2,1,0:T(8,128)(2,1)} %shard_map.128), channel_id=1, replica_groups=mesh['dp'=4,'expert'=32] {'expert'}, dimensions={0} | all-to-all | bytes 12582912 | tf_op jit(solution)/shard_map/all_to_all | solution.py:236
  346.9 0.0 reduce-scatter.5.cloned.1.call-done
  346.9 0.0 reduce-scatter.3.cloned.1.call-done
  347.0 0.0 copy-start.2
  347.0 14.3 %shard_map.131 = (bf16[128,2048]{1,0:T(8,128)(2,1)}, bf16[128,2048]{1,0:T(8,128)(2,1)}, f32[2,32,1,128]{3,2,1,0:T(1,128)}, bf16[2,512,768]{2,1,0:T(8,128)(2,1)},...) custom-call(bf16[128,2048]{1,0:T(8,128)(2,1)} %cotangent_ref.1, bf16[32,48,2048]{2,1,0:T(8,128)(2,1)} %all_to_all.15.refs_0_, ...), custom_call_target="tpu_custom_call" | custom-call | flops 4831838208 | bytes 23592960 | tf_op jit(solution)/shard_map/pallas_call | solution.py:199
  361.2 0.8 copy.21
  362.0 0.0 copy-done.2
  362.0 0.6 select_reduce_fusion
  (12 shorter events, 0.2 us)
Async XLA Ops:
  7.2 3.0 copy-start.3
  7.2 3.2 copy-start.4
  7.2 118.7 %all-gather.3.cloned.1.call-start = ((), (), s32[]{:S(2)}) async-start(), calls=%async_computation.7 | async-start | bytes 34603008 | tf_op jit(solution)/shard_map/all_gather | solution.py:249
  10.2 1.2 copy-start.1
  11.4 14.8 %all-to-all-start = ((f32[32,8,128]{2,1,0:T(8,128)}), f32[32,8,128]{2,1,0:T(8,128)S(1)}, u32[]{:S(2)}, u32[]{:S(2)}) async-start(f32[32,8,128]{2,1,0:T(8,128)} %pad.4), calls=%async_computation | async-start | bytes 262144 | tf_op jit(solution)/shard_map/all_to_all | solution.py:236
  19.6 327.3 %reduce-scatter.5.cloned.1.call-start = ((), (), s32[]{:S(2)}) async-start(), calls=%async_computation.6 | async-start | bytes 11796480 | tf_op jit(solution)/shard_map/reduce_scatter | solution.py:281
  26.2 99.7 %copy-start = (f32[32,8,128]{2,1,0:T(8,128)}, f32[32,8,128]{2,1,0:T(8,128)S(1)}, u32[]{:S(2)}) copy-start(f32[32,8,128]{2,1,0:T(8,128)S(1)} %all-to-all-done.plan_ref) | copy-start | bytes 393220
  177.8 93.3 %all-to-all-start.2 = ((bf16[32,48,2048]{2,1,0:T(8,128)(2,1)}), bf16[32,48,2048]{2,1,0:T(8,128)(2,1)}, u32[]{:S(2)}, u32[]{:S(2)}) async-start(bf16[32,48,2048]{2,1,0:T(8,128)(2,1)} %shard_map.130), calls=%async_computation.2 | async-start | bytes 12582912 | tf_op jit(solution)/shard_map/all_to_all | solution.py:236
  184.1 162.9 %reduce-scatter.3.cloned.1.call-start = ((), (), s32[]{:S(2)}) async-start(), calls=%async_computation.5 | async-start | bytes 11796480 | tf_op jit(solution)/shard_map/reduce_scatter | solution.py:281
  347.0 15.1 %copy-start.2 = (s32[8,128]{1,0:T(8,128)S(1)}, s32[8,128]{1,0:T(8,128)}, u32[]{:S(2)}) copy-start(s32[8,128]{1,0:T(8,128)} %copy-done.1) | copy-start | bytes 12292
Sparse Core Ops, SparseCore 0:
  10.9 115.0 all-gather.2
  165.2 89.1 reduce-scatter.4
  256.8 88.6 reduce-scatter.2

commit v7 on v6

--- a/solution.py
+++ b/solution.py
@@ -18,9 +18,13 @@
     return lax.dot_general(a, b, dims, preferred_element_type=F32)
 
 
-def grads_kernel(steps, sources, e, plan_ref, *refs):
-    blocks, (gate_ref, up_ref, down_ref) = refs[:sources], refs[sources : sources + 3]
-    grads_ref, hidden_ref, pregate_ref, preup_ref, x, xt, sc, st = refs[sources + 3 :]
+def grads_kernel(steps, sources, e, last, plan_ref, *refs):
+    blocks, (gate_ref, up_ref, down_ref), refs = refs[:sources], refs[sources : sources + 3], refs[sources + 3 :]
+    if last:
+        old_hidden_ref, old_scaled_ref, grads_ref, hidden_ref, pregate_ref, preup_ref, x, xt, sc, st, old_st = refs
+    else:
+        grads_ref, hidden_ref, pregate_ref, preup_ref, scaled_ref, x, xt, sc, sem = refs
+        keep = pltpu.make_async_copy(sc, scaled_ref, sem)
     step = pl.program_id(0)
     tok_dev = plan_ref.shape[2]
     rows, model_dim = x.shape
@@ -48,7 +52,15 @@
         @pl.when(step == (part + 1) * steps // 2 - 1)
         def _():
             xt[:, span] = x[span, :].T
-            st[:, span] = sc[span, :].T
+            if last:
+                st[:, span] = sc[span, :].T
+                old_st[:, span] = old_scaled_ref[span, :].T
+
+    if not last:
+
+        @pl.when(step == steps)
+        def _():
+            keep.start()
 
     @pl.when(step >= steps)
     def _():
@@ -63,13 +75,22 @@
         hidden_ref[...] = hidden
         pregate_ref[...] = grad_pregate
         preup_ref[...] = grad_preup
-        for which, (left, right) in enumerate(((xt, grad_pregate), (xt, grad_preup), (st, hidden))):
+        pairs = [(xt, grad_pregate), (xt, grad_preup)]
+        if last:
+            pairs += [(st, hidden), (old_st, old_hidden_ref[...])]
+        for which, (left, right) in enumerate(pairs):
             product = dot(left[...], right).astype(BF16)
             for r in range(shards):
                 grads_ref[r, which] = product[r * shard_rows : (r + 1) * shard_rows]
 
-
-def expert_grads(gathered, plan, gate_proj, up_proj, down_proj, e, capacity, shards):
+    if not last:
+
+        @pl.when(step == pl.num_programs(0) - 1)
+        def _():
+            keep.wait()
+
+
+def expert_grads(gathered, plan, gate_proj, up_proj, down_proj, e, capacity, shards, old):
     group, height, model_dim = gathered.shape
     rows = group * capacity
     hidden_dim = gate_proj.shape[2]
@@ -84,8 +105,12 @@
         return lambda s: (jnp.minimum(s, steps - 1) * sources + j, 0, 0)
 
     narrow = pl.BlockSpec((rows, tile), lambda s: (0, at(s)))
+    last = old is not None
+    matrices = 4 if last else 2
+    wide = pltpu.VMEM((rows, model_dim), BF16)
+    tall = pltpu.VMEM((model_dim, rows), BF16)
     return pl.pallas_call(
-        functools.partial(grads_kernel, steps, sources, e),
+        functools.partial(grads_kernel, steps, sources, e, last),
         grid=(steps + hidden_dim // tile,),
         in_specs=[
             pl.BlockSpec((sources, *plan.shape[1:]), lambda s: (jnp.minimum(s, steps - 1), 0, 0)),
@@ -93,23 +118,26 @@
             pl.BlockSpec((None, model_dim, tile), lambda s: (e, 0, at(s))),
             pl.BlockSpec((None, model_dim, tile), lambda s: (e, 0, at(s))),
             pl.BlockSpec((None, tile, model_dim), lambda s: (e, at(s), 0)),
-        ],
+        ]
+        + [narrow, pl.BlockSpec((rows, model_dim), lambda s: (0, 0), pipeline_mode=pl.Buffered(1))] * last,
         out_specs=[
-            pl.BlockSpec((shards, 3, model_dim // shards, tile), lambda s: (0, 0, 0, at(s))),
+            pl.BlockSpec((shards, matrices, model_dim // shards, tile), lambda s: (0, 0, 0, at(s))),
             narrow,
             narrow,
             narrow,
-        ],
-        out_shape=[jax.ShapeDtypeStruct((shards, 3, model_dim // shards, hidden_dim), BF16)]
-        + [jax.ShapeDtypeStruct((rows, hidden_dim), BF16)] * 3,
-        scratch_shapes=[pltpu.VMEM((rows, model_dim), BF16), pltpu.VMEM((model_dim, rows), BF16)] * 2,
-        compiler_params=pltpu.CompilerParams(vmem_limit_bytes=60 << 20),
+        ]
+        + [pl.BlockSpec(memory_space=pl.ANY)] * (not last),
+        out_shape=[jax.ShapeDtypeStruct((shards, matrices, model_dim // shards, hidden_dim), BF16)]
+        + [jax.ShapeDtypeStruct((rows, hidden_dim), BF16)] * 3
+        + [jax.ShapeDtypeStruct((rows, model_dim), BF16)] * (not last),
+        scratch_shapes=[wide, tall, wide] + ([tall, tall] if last else [pltpu.SemaphoreType.DMA]),
+        compiler_params=pltpu.CompilerParams(vmem_limit_bytes=61 << 20),
         cost_estimate=pl.CostEstimate(
             flops=12 * rows * model_dim * hidden_dim,
             bytes_accessed=2 * gathered.size + 12 * model_dim * hidden_dim + 6 * rows * hidden_dim,
             transcendentals=rows * hidden_dim,
         ),
-    )(plan, *[gathered] * sources, gate_proj, up_proj, down_proj)
+    )(plan, *[gathered] * sources, gate_proj, up_proj, down_proj, *(old if last else ()))
 
 
 def returns_kernel(hidden_ref, pregate_ref, preup_ref, gate_ref, up_ref, down_ref, back_ref):
@@ -160,7 +188,8 @@
     for e in range(experts):
         gate_ref[e] = reduced[e][0]
         up_ref[e] = reduced[e][1]
-        down_ref[e] = reduced[e][2].T
+    down_ref[0] = reduced[1][3].T
+    down_ref[1] = reduced[1][2].T
 
     sums = None
     for e in range(experts):
@@ -205,7 +234,7 @@
             pl.BlockSpec((step * height, 2 * tok_dev), lambda s: (s, 0)),
         ]
         * experts
-        + [pl.BlockSpec((3, shard_rows, tile), lambda s: (0, 0, s))] * experts,
+        + [pl.BlockSpec((v.shape[0], shard_rows, tile), lambda s: (0, 0, s)) for v in reduced],
         out_specs=[
             whole,
             whole,
@@ -272,12 +301,14 @@
     plan = jnp.concatenate([slots, gates], axis=2).reshape(group, 2 * local_experts, tok_dev)
     plan = exchange(jnp.pad(plan, ((0, 0), (0, 8 - 2 * local_experts), (0, 0))))
     gathered, plan, *picks = lax.optimization_barrier((gathered, plan, *picks))
+    old = None
 
     returned, reduced = [], []
     for e in range(local_experts):
-        grads, hidden, pregate, preup = expert_grads(
-            gathered, plan, gate_proj, up_proj, down_proj, e, capacity, shards
+        grads, hidden, pregate, preup, *scaled = expert_grads(
+            gathered, plan, gate_proj, up_proj, down_proj, e, capacity, shards, old
         )
+        old = (hidden, *scaled)
         reduced.append(lax.psum_scatter(grads, "dp", scatter_dimension=0, tiled=False))
         back = expert_returns(hidden, pregate, preup, gate_proj, up_proj, down_proj, e, group)
         returned.append(exchange(back))

time: 373 us -> 368 us (0.987)
  waiting for transfers between devices: 138 us -> 132 us
    all_to_all x2, waiting for transfers between devices: 38.4 us -> 33 us  [exchange(): lax.all_to_all(rows, 'expert', split_axis=0, concat_axis=0, tiled=True)]
  transfers between devices with their start and end apart: 5 -> 5, of which waited for: 3 -> 3; matrix products, arithmetic and copies ran while one was open for 1% -> 1% of each run, Pallas kernels for 18% -> 19%
where the time goes in v7:
time: 368 us; the launch traced here: 364 us
  waiting for transfers between devices  132 us (36%)
  Pallas kernels  119 us (32%)
  blocking collectives  75.3 us (20%)
  starting transfers between devices  14.8 us (4%)
  between operations  14.6 us (4%)
  other arithmetic  5.84 us (2%)
    all_gather x1, waiting for transfers between devices, local(): lax.all_gather(jnp.concatenate([tokens, cotangent])[None], 'expert', axis...  99.3 us
    pallas_call x2, Pallas kernels, expert_grads(): pl.pallas_call(functools.partial(grads_kernel, steps, sources, e, last),...  80.6 us
    all_to_all x1, blocking collectives, exchange(): lax.all_to_all(rows, 'expert', split_axis=0, concat_axis=0, tiled=True)  75.3 us
    all_to_all x2, waiting for transfers between devices, exchange(): lax.all_to_all(rows, 'expert', split_axis=0, concat_axis=0, tiled=True)  33 us
    pallas_call x2, Pallas kernels, expert_returns(): pl.pallas_call(returns_kernel, grid=(model_dim // tile,), in_specs=[whole...  25 us
    all_to_all x2, starting transfers between devices, exchange(): lax.all_to_all(rows, 'expert', split_axis=0, concat_axis=0, tiled=True)  14.5 us
    pallas_call x1, Pallas kernels, finish(): pl.pallas_call(functools.partial(finish_kernel, experts), grid=(steps,),...  13.5 us
  transfers between devices with their start and end apart: 5, of which 3 were waited for; matrix products, arithmetic and copies ran while one was open for 1% of the time, Pallas kernels for 19%

profile of v7, /device:TPU:32, one launch (start us, length us, event | category | flops | bytes accessed | tf_op | source)
XLA Modules:
  0.0 364.3 jit_solution(5512639268209781273)
XLA Ops:
  7.2 0.0 copy-start.3
  7.2 0.0 copy-start.4
  7.2 0.0 all-gather.3.cloned.1.call-start
  7.2 2.3 pad_maximum_fusion
  9.5 0.0 all-gather.3.cloned.1.call-update
  10.2 0.0 copy-done.3
  10.2 0.0 copy-start.1
  10.2 0.1 fusion.4
  10.3 0.0 copy-done.4
  10.4 0.4 copy-done.1
  10.8 0.1 select_reduce_fusion.1
  10.9 0.1 convolution_convert_fusion
  11.1 0.1 copy.19
  11.2 0.7 pad.4
  11.8 8.2 %all-to-all-start = ((f32[32,8,128]{2,1,0:T(8,128)}), f32[32,8,128]{2,1,0:T(8,128)S(1)}, u32[]{:S(2)}, u32[]{:S(2)}) async-start(f32[32,8,128]{2,1,0:T(8,128)} %pad.4), calls=%async_computation | async-start | bytes 262144 | tf_op jit(solution)/shard_map/all_to_all | solution.py:265
  20.1 0.0 reduce-scatter.3.cloned.1.call-start
  20.1 0.1 eq.104
  20.3 0.4 fusion
  20.7 0.3 fusion.3
  21.1 1.0 pad_maximum_fusion.2.refs_3_
  22.0 1.0 pad_maximum_fusion.1.refs_1_
  23.0 3.6 %all-to-all-done.plan_ref = f32[32,8,128]{2,1,0:T(8,128)S(1)} async-done(((f32[32,8,128]{2,1,0:T(8,128)}), f32[32,8,128]{2,1,0:T(8,128)S(1)}, u32[]{:S(2)}, u32[]{:S(2)}) %all-to-all-start) | async-done | bytes 131104 | tf_op jit(solution)/shard_map/all_to_all | solution.py:265
  26.7 0.0 copy-start
  26.7 99.3 %all-gather.3.cloned.1.call-done = bf16[8192,2048]{1,0:T(8,128)(2,1)} async-done(((bf16[256,2048]{1,0:T(8,128)(2,1)}), bf16[8192,2048]{1,0:T(8,128)(2,1)}) %all-gather.3.cloned.1.call-update) | async-done | bytes 33554448 | tf_op jit(solution)/shard_map/all_gather | solution.py:278
  125.9 0.0 copy-done
  125.9 35.6 %shard_map.127 = (bf16[4,2,512,768]{3,2,1,0:T(8,128)(2,1)}, bf16[768,768]{1,0:T(8,128)(2,1)}, bf16[768,768]{1,0:T(8,128)(2,1)}, bf16[768,768]{1,0:T(8,128)(2,1)}, bf16[768,2048]{1,0:T(8,128)(2,1)}) custom-call(f32[32,8,128]{2,1,0:T(8,128)} %copy-done, bf16[32,256,2048]{2,1,0:T(8,128)(2,1)} %bitcast.74, bf16[32,256,2048]{2,1,0:T(8,128)(2,1)} %bitcast.75, ...), custom_call_target="tpu_custom_call" | custom-call | flops 14495514624 | bytes 55967744 | tf_op jit(solution)/shard_map/pallas_call | solution.py:112
  161.5 0.0 reduce-scatter.3.cloned.1.call-update
  161.5 12.6 %shard_map.128 = bf16[32,48,2048]{2,1,0:T(8,128)(2,1)} custom-call(bf16[768,768]{1,0:T(8,128)(2,1)} %get-tuple-element.27.hidden_ref.refs_7_, bf16[768,768]{1,0:T(8,128)(2,1)} %get-tuple-element.28.pregate_ref, bf16[768,768]{1,0:T(8,128)(2,1)} %get-tuple-element.29.preup_ref, bf16[2,2048,768]{2,1,0:T(8,128)(2,1)} %gate_ref.3, bf16[2,2048,768]{2,1,0:T(8,128)(2,1)} %up_ref.3, ...), custom_call_target="tpu_custom_call" | custom-call | flops 724775731200 | bytes 19267584 | tf_op jit(solution)/shard_map/pallas_call | solution.py:159
  174.1 6.3 %all-to-all-start.1 = ((bf16[32,48,2048]{2,1,0:T(8,128)(2,1)}), bf16[32,48,2048]{2,1,0:T(8,128)(2,1)}, u32[]{:S(2)}, u32[]{:S(2)}) async-start(bf16[32,48,2048]{2,1,0:T(8,128)(2,1)} %shard_map.128), calls=%async_computation.1 | async-start | bytes 12582912 | tf_op jit(solution)/shard_map/all_to_all | solution.py:265
  180.4 0.2 reduce-scatter.5.cloned.1.call-start
  180.7 45.0 %shard_map.129 = (bf16[4,4,512,768]{3,2,1,0:T(8,128)(2,1)}, bf16[768,768]{1,0:T(8,128)(2,1)}, bf16[768,768]{1,0:T(8,128)(2,1)}, bf16[768,768]{1,0:T(8,128)(2,1)}) custom-call(f32[32,8,128]{2,1,0:T(8,128)} %copy-done, bf16[32,256,2048]{2,1,0:T(8,128)(2,1)} %bitcast.78, bf16[32,256,2048]{2,1,0:T(8,128)(2,1)} %bitcast.79, bf16[32,256,2048]{2,1,0:T(8,128)(2,1)} %bitcast.80, ...), custom_call_target="tpu_custom_call" | custom-call | flops 14495514624 | bytes 55967744 | tf_op jit(solution)/shard_map/pallas_call | solution.py:112
  225.7 0.0 reduce-scatter.5.cloned.1.call-update
  225.7 12.4 %shard_map.130 = bf16[32,48,2048]{2,1,0:T(8,128)(2,1)} custom-call(bf16[768,768]{1,0:T(8,128)(2,1)} %get-tuple-element.32.hidden_ref, bf16[768,768]{1,0:T(8,128)(2,1)} %get-tuple-element.33.pregate_ref, bf16[768,768]{1,0:T(8,128)(2,1)} %get-tuple-element.34.preup_ref, bf16[2,2048,768]{2,1,0:T(8,128)(2,1)} %gate_ref.3, bf16[2,2048,768]{2,1,0:T(8,128)(2,1)} %up_ref.3, ...), custom_call_target="tpu_custom_call" | custom-call | flops 724775731200 | bytes 19267584 | tf_op jit(solution)/shard_map/pallas_call | solution.py:159
  238.1 29.4 %all-to-all-done.1.refs_0_ = bf16[32,48,2048]{2,1,0:T(8,128)(2,1)} async-done(((bf16[32,48,2048]{2,1,0:T(8,128)(2,1)}), bf16[32,48,2048]{2,1,0:T(8,128)(2,1)}, u32[]{:S(2)}, u32[]{:S(2)}) %all-to-all-start.1) | async-done | bytes 6291488 | tf_op jit(solution)/shard_map/all_to_all | solution.py:265
  267.5 75.3 %all_to_all.15.refs_2_ = bf16[32,48,2048]{2,1,0:T(8,128)(2,1)} all-to-all(bf16[32,48,2048]{2,1,0:T(8,128)(2,1)} %shard_map.130), channel_id=1, replica_groups=mesh['dp'=4,'expert'=32] {'expert'}, dimensions={0} | all-to-all | bytes 12582912 | tf_op jit(solution)/shard_map/all_to_all | solution.py:265
  342.8 0.0 reduce-scatter.3.cloned.1.call-done
  342.8 0.0 reduce-scatter.5.cloned.1.call-done
  342.8 0.0 copy-start.2
  342.8 13.5 %shard_map.131 = (bf16[128,2048]{1,0:T(8,128)(2,1)}, bf16[128,2048]{1,0:T(8,128)(2,1)}, f32[2,32,1,128]{3,2,1,0:T(1,128)}, bf16[2,512,768]{2,1,0:T(8,128)(2,1)},...) custom-call(bf16[128,2048]{1,0:T(8,128)(2,1)} %cotangent_ref.1, ...), custom_call_target="tpu_custom_call" | custom-call | flops 4831838208 | bytes 23592960 | tf_op jit(solution)/shard_map/pallas_call | solution.py:228
  356.3 0.8 copy.21
  357.1 0.0 copy-done.2
  357.1 0.6 select_reduce_fusion
  (12 shorter events, 0.2 us)
Async XLA Ops:
  7.2 3.0 copy-start.3
  7.2 3.2 copy-start.4
  7.2 118.7 %all-gather.3.cloned.1.call-start = ((), (), s32[]{:S(2)}) async-start(), calls=%async_computation.7 | async-start | bytes 34603008 | tf_op jit(solution)/shard_map/all_gather | solution.py:278
  10.2 0.6 copy-start.1
  11.8 14.8 %all-to-all-start = ((f32[32,8,128]{2,1,0:T(8,128)}), f32[32,8,128]{2,1,0:T(8,128)S(1)}, u32[]{:S(2)}, u32[]{:S(2)}) async-start(f32[32,8,128]{2,1,0:T(8,128)} %pad.4), calls=%async_computation | async-start | bytes 262144 | tf_op jit(solution)/shard_map/all_to_all | solution.py:265
  20.1 322.7 %reduce-scatter.3.cloned.1.call-start = ((), (), s32[]{:S(2)}) async-start(), calls=%async_computation.5 | async-start | bytes 7864320 | tf_op jit(solution)/shard_map/reduce_scatter | solution.py:312
  26.7 99.3 %copy-start = (f32[32,8,128]{2,1,0:T(8,128)}, f32[32,8,128]{2,1,0:T(8,128)S(1)}, u32[]{:S(2)}) copy-start(f32[32,8,128]{2,1,0:T(8,128)S(1)} %all-to-all-done.plan_ref) | copy-start | bytes 393220
  174.1 93.4 %all-to-all-start.1 = ((bf16[32,48,2048]{2,1,0:T(8,128)(2,1)}), bf16[32,48,2048]{2,1,0:T(8,128)(2,1)}, u32[]{:S(2)}, u32[]{:S(2)}) async-start(bf16[32,48,2048]{2,1,0:T(8,128)(2,1)} %shard_map.128), calls=%async_computation.1 | async-start | bytes 12582912 | tf_op jit(solution)/shard_map/all_to_all | solution.py:265
  180.4 162.4 %reduce-scatter.5.cloned.1.call-start = ((), (), s32[]{:S(2)}) async-start(), calls=%async_computation.6 | async-start | bytes 15728640 | tf_op jit(solution)/shard_map/reduce_scatter | solution.py:312
  342.8 14.3 %copy-start.2 = (s32[8,128]{1,0:T(8,128)S(1)}, s32[8,128]{1,0:T(8,128)}, u32[]{:S(2)}) copy-start(s32[8,128]{1,0:T(8,128)} %copy-done.1) | copy-start | bytes 12292
Sparse Core Ops, SparseCore 0:
  10.9 115.0 all-gather.2
  161.7 64.0 reduce-scatter.2
  228.2 114.1 reduce-scatter.4

commit v8 on v7

--- a/solution.py
+++ b/solution.py
@@ -147,7 +147,8 @@
     part = dot(pregate_ref[...], gate_ref[...], CONTRACT_LAST) + dot(preup_ref[...], up_ref[...], CONTRACT_LAST)
     for source in range(group):
         rows = slice(source * capacity, (source + 1) * capacity)
-        back_ref[source] = jnp.concatenate([out[rows], part[rows]]).astype(BF16)
+        pieces = [v[rows][span] for span in (slice(0, 16), slice(16, capacity)) for v in (out, part)]
+        back_ref[source] = jnp.concatenate(pieces).astype(BF16)
 
 
 def expert_returns(hidden, pregate, preup, gate_proj, up_proj, down_proj, e, group):
@@ -197,10 +198,15 @@
         picks = pairs[2 * e + 1][...]
         part = dot(picks, rows, CONTRACT_FIRST)
         sums = part if sums is None else sums + part
-        product = dot(rows, cotangent_ref[...], CONTRACT_LAST)
-        product = jnp.where(picks[:, :tok_dev].astype(F32) > 0.0, product, 0.0)
+        gates = picks[:, :tok_dev].reshape(devices, height, tok_dev)
+        by_device = []
+        for span in (slice(0, 16), slice(32, 48)):
+            product = dot(pairs[2 * e][:, span, :].reshape(devices * 16, model_dim), cotangent_ref[...], CONTRACT_LAST)
+            given = gates[:, span, :].reshape(devices * 16, tok_dev).astype(F32)
+            by_device.append(jnp.where(given > 0.0, product, 0.0))
         for d in range(devices):
-            products_ref[e, d] = jnp.sum(product[d * height : d * height + height // 2], axis=0, keepdims=True)
+            rows_d = slice(d * 16, (d + 1) * 16)
+            products_ref[e, d] = jnp.sum(by_device[0][rows_d] + by_device[1][rows_d], axis=0, keepdims=True)
 
     @pl.when(step == 0)
     def _():
@@ -288,10 +294,13 @@
     rank = dot(names.astype(BF16), before.astype(BF16)).astype(jnp.int32)
     names, gates, rank = (v.reshape(group, local_experts, 1, tok_dev) for v in (names, gates, rank))
     column = lax.broadcasted_iota(jnp.int32, (1, 2 * capacity, 1), 1)
+    rest = 32 + capacity - 16
+    out_slot = jnp.where(column < 16, column, jnp.where((column >= 32) & (column < rest), column - 16, -1))
+    part_slot = jnp.where(column >= rest, column - rest + 16, jnp.where((column >= 16) & (column < 32), column - 16, -1))
     picks = []
     for e in range(local_experts):
-        place = names[:, e] & (rank[:, e] == column)
-        second = names[:, e] & (rank[:, e] + capacity == column)
+        place = names[:, e] & (rank[:, e] == out_slot)
+        second = names[:, e] & (rank[:, e] == part_slot)
         picks.append(
             jnp.concatenate([jnp.where(place, gates[:, e], 0.0).astype(BF16), second.astype(BF16)], axis=2)
             .reshape(-1, 2 * tok_dev)

time: 368 us -> 366 us (level)
  no operation moved by 1% of the time
where the time goes in v8:
time: 366 us; the launch traced here: 363 us
  waiting for transfers between devices  132 us (36%)
  Pallas kernels  118 us (32%)
  blocking collectives  75.3 us (21%)
  starting transfers between devices  14.8 us (4%)
  between operations  14.6 us (4%)
  other arithmetic  5.87 us (2%)
    all_gather x1, waiting for transfers between devices, local(): lax.all_gather(jnp.concatenate([tokens, cotangent])[None], 'expert', axis...  99.3 us
    pallas_call x2, Pallas kernels, expert_grads(): pl.pallas_call(functools.partial(grads_kernel, steps, sources, e, last),...  80.6 us
    all_to_all x1, blocking collectives, exchange(): lax.all_to_all(rows, 'expert', split_axis=0, concat_axis=0, tiled=True)  75.3 us
    all_to_all x2, waiting for transfers between devices, exchange(): lax.all_to_all(rows, 'expert', split_axis=0, concat_axis=0, tiled=True)  32.9 us
    pallas_call x2, Pallas kernels, expert_returns(): pl.pallas_call(returns_kernel, grid=(model_dim // tile,), in_specs=[whole...  24.9 us
    all_to_all x2, starting transfers between devices, exchange(): lax.all_to_all(rows, 'expert', split_axis=0, concat_axis=0, tiled=True)  14.5 us
    pallas_call x1, Pallas kernels, finish(): pl.pallas_call(functools.partial(finish_kernel, experts), grid=(steps,),...  12.3 us
  transfers between devices with their start and end apart: 5, of which 3 were waited for; matrix products, arithmetic and copies ran while one was open for 1% of the time, Pallas kernels for 19%

profile of v8, /device:TPU:32, one launch (start us, length us, event | category | flops | bytes accessed | tf_op | source)
XLA Modules:
  0.0 363.0 jit_solution(10151574385999433705)
XLA Ops:
  7.2 0.0 copy-start.3
  7.2 0.0 copy-start.4
  7.2 0.0 all-gather.3.cloned.1.call-start
  7.2 2.3 pad_maximum_fusion
  9.5 0.0 all-gather.3.cloned.1.call-update
  10.2 0.0 copy-done.3
  10.2 0.0 copy-start.1
  10.2 0.1 fusion.4
  10.3 0.0 copy-done.4
  10.4 0.4 copy-done.1
  10.8 0.1 select_reduce_fusion.1
  10.9 0.1 convolution_convert_fusion
  11.1 0.1 copy.17
  11.2 0.7 pad.4
  11.8 8.2 %all-to-all-start = ((f32[32,8,128]{2,1,0:T(8,128)}), f32[32,8,128]{2,1,0:T(8,128)S(1)}, u32[]{:S(2)}, u32[]{:S(2)}) async-start(f32[32,8,128]{2,1,0:T(8,128)} %pad.4), calls=%async_computation | async-start | bytes 262144 | tf_op jit(solution)/shard_map/all_to_all | solution.py:271
  20.1 0.0 reduce-scatter.3.cloned.1.call-start
  20.1 0.1 eq.96
  20.2 0.1 eq.100
  20.4 0.3 fusion.3
  20.8 0.4 fusion
  21.2 1.0 pad_maximum_fusion.2.refs_3_
  22.1 1.0 pad_maximum_fusion.1.refs_1_
  23.1 3.5 all-to-all-done.plan_ref
  26.7 0.0 copy-start
  26.7 99.3 %all-gather.3.cloned.1.call-done = bf16[8192,2048]{1,0:T(8,128)(2,1)} async-done(((bf16[256,2048]{1,0:T(8,128)(2,1)}), bf16[8192,2048]{1,0:T(8,128)(2,1)}) %all-gather.3.cloned.1.call-update) | async-done | bytes 33554448 | tf_op jit(solution)/shard_map/all_gather | solution.py:284
  125.9 0.0 copy-done
  125.9 35.6 %shard_map.127 = (bf16[4,2,512,768]{3,2,1,0:T(8,128)(2,1)}, bf16[768,768]{1,0:T(8,128)(2,1)}, bf16[768,768]{1,0:T(8,128)(2,1)}, bf16[768,768]{1,0:T(8,128)(2,1)}, bf16[768,2048]{1,0:T(8,128)(2,1)}) custom-call(f32[32,8,128]{2,1,0:T(8,128)} %copy-done, bf16[32,256,2048]{2,1,0:T(8,128)(2,1)} %bitcast.62, bf16[32,256,2048]{2,1,0:T(8,128)(2,1)} %bitcast.63, ...), custom_call_target="tpu_custom_call" | custom-call | flops 14495514624 | bytes 55967744 | tf_op jit(solution)/shard_map/pallas_call | solution.py:112
  161.5 0.0 reduce-scatter.3.cloned.1.call-update
  161.5 12.5 %shard_map.128 = bf16[32,48,2048]{2,1,0:T(8,128)(2,1)} custom-call(bf16[768,768]{1,0:T(8,128)(2,1)} %get-tuple-element.27.hidden_ref.refs_7_, bf16[768,768]{1,0:T(8,128)(2,1)} %get-tuple-element.28.pregate_ref, bf16[768,768]{1,0:T(8,128)(2,1)} %get-tuple-element.29.preup_ref, bf16[2,2048,768]{2,1,0:T(8,128)(2,1)} %gate_ref.3, bf16[2,2048,768]{2,1,0:T(8,128)(2,1)} %up_ref.3, ...), custom_call_target="tpu_custom_call" | custom-call | flops 724775731200 | bytes 19267584 | tf_op jit(solution)/shard_map/pallas_call | solution.py:160
  174.1 6.3 %all-to-all-start.1 = ((bf16[32,48,2048]{2,1,0:T(8,128)(2,1)}), bf16[32,48,2048]{2,1,0:T(8,128)(2,1)}, u32[]{:S(2)}, u32[]{:S(2)}) async-start(bf16[32,48,2048]{2,1,0:T(8,128)(2,1)} %shard_map.128), calls=%async_computation.1 | async-start | bytes 12582912 | tf_op jit(solution)/shard_map/all_to_all | solution.py:271
  180.4 0.2 reduce-scatter.5.cloned.1.call-start
  180.6 45.0 %shard_map.129 = (bf16[4,4,512,768]{3,2,1,0:T(8,128)(2,1)}, bf16[768,768]{1,0:T(8,128)(2,1)}, bf16[768,768]{1,0:T(8,128)(2,1)}, bf16[768,768]{1,0:T(8,128)(2,1)}) custom-call(f32[32,8,128]{2,1,0:T(8,128)} %copy-done, bf16[32,256,2048]{2,1,0:T(8,128)(2,1)} %bitcast.66, bf16[32,256,2048]{2,1,0:T(8,128)(2,1)} %bitcast.67, bf16[32,256,2048]{2,1,0:T(8,128)(2,1)} %bitcast.68, ...), custom_call_target="tpu_custom_call" | custom-call | flops 14495514624 | bytes 55967744 | tf_op jit(solution)/shard_map/pallas_call | solution.py:112
  225.6 0.0 reduce-scatter.5.cloned.1.call-update
  225.6 12.4 %shard_map.130 = bf16[32,48,2048]{2,1,0:T(8,128)(2,1)} custom-call(bf16[768,768]{1,0:T(8,128)(2,1)} %get-tuple-element.32.hidden_ref, bf16[768,768]{1,0:T(8,128)(2,1)} %get-tuple-element.33.pregate_ref, bf16[768,768]{1,0:T(8,128)(2,1)} %get-tuple-element.34.preup_ref, bf16[2,2048,768]{2,1,0:T(8,128)(2,1)} %gate_ref.3, bf16[2,2048,768]{2,1,0:T(8,128)(2,1)} %up_ref.3, ...), custom_call_target="tpu_custom_call" | custom-call | flops 724775731200 | bytes 19267584 | tf_op jit(solution)/shard_map/pallas_call | solution.py:160
  238.0 29.4 %all-to-all-done.1.refs_0_ = bf16[32,48,2048]{2,1,0:T(8,128)(2,1)} async-done(((bf16[32,48,2048]{2,1,0:T(8,128)(2,1)}), bf16[32,48,2048]{2,1,0:T(8,128)(2,1)}, u32[]{:S(2)}, u32[]{:S(2)}) %all-to-all-start.1) | async-done | bytes 6291488 | tf_op jit(solution)/shard_map/all_to_all | solution.py:271
  267.4 75.3 %all_to_all.15.refs_2_ = bf16[32,48,2048]{2,1,0:T(8,128)(2,1)} all-to-all(bf16[32,48,2048]{2,1,0:T(8,128)(2,1)} %shard_map.130), channel_id=1, replica_groups=mesh['dp'=4,'expert'=32] {'expert'}, dimensions={0} | all-to-all | bytes 12582912 | tf_op jit(solution)/shard_map/all_to_all | solution.py:271
  342.7 0.0 reduce-scatter.3.cloned.1.call-done
  342.7 0.0 reduce-scatter.5.cloned.1.call-done
  342.7 0.0 copy-start.2
  342.7 12.3 %shard_map.131 = (bf16[128,2048]{1,0:T(8,128)(2,1)}, bf16[128,2048]{1,0:T(8,128)(2,1)}, f32[2,32,1,128]{3,2,1,0:T(1,128)}, bf16[2,512,768]{2,1,0:T(8,128)(2,1)},...) custom-call(bf16[128,2048]{1,0:T(8,128)(2,1)} %cotangent_ref.1, ...), custom_call_target="tpu_custom_call" | custom-call | flops 4831838208 | bytes 23592960 | tf_op jit(solution)/shard_map/pallas_call | solution.py:234
  355.1 0.8 copy.18
  355.8 0.0 copy-done.2
  355.9 0.6 select_reduce_fusion
  (14 shorter events, 0.2 us)
Async XLA Ops:
  7.2 3.0 copy-start.3
  7.2 3.2 copy-start.4
  7.2 118.7 %all-gather.3.cloned.1.call-start = ((), (), s32[]{:S(2)}) async-start(), calls=%async_computation.7 | async-start | bytes 34603008 | tf_op jit(solution)/shard_map/all_gather | solution.py:284
  10.2 0.6 copy-start.1
  11.8 14.8 %all-to-all-start = ((f32[32,8,128]{2,1,0:T(8,128)}), f32[32,8,128]{2,1,0:T(8,128)S(1)}, u32[]{:S(2)}, u32[]{:S(2)}) async-start(f32[32,8,128]{2,1,0:T(8,128)} %pad.4), calls=%async_computation | async-start | bytes 262144 | tf_op jit(solution)/shard_map/all_to_all | solution.py:271
  20.1 322.7 %reduce-scatter.3.cloned.1.call-start = ((), (), s32[]{:S(2)}) async-start(), calls=%async_computation.5 | async-start | bytes 7864320 | tf_op jit(solution)/shard_map/reduce_scatter | solution.py:321
  26.7 99.3 %copy-start = (f32[32,8,128]{2,1,0:T(8,128)}, f32[32,8,128]{2,1,0:T(8,128)S(1)}, u32[]{:S(2)}) copy-start(f32[32,8,128]{2,1,0:T(8,128)S(1)} %all-to-all-done.plan_ref) | copy-start | bytes 393220
  174.1 93.4 %all-to-all-start.1 = ((bf16[32,48,2048]{2,1,0:T(8,128)(2,1)}), bf16[32,48,2048]{2,1,0:T(8,128)(2,1)}, u32[]{:S(2)}, u32[]{:S(2)}) async-start(bf16[32,48,2048]{2,1,0:T(8,128)(2,1)} %shard_map.128), calls=%async_computation.1 | async-start | bytes 12582912 | tf_op jit(solution)/shard_map/all_to_all | solution.py:271
  180.4 162.4 %reduce-scatter.5.cloned.1.call-start = ((), (), s32[]{:S(2)}) async-start(), calls=%async_computation.6 | async-start | bytes 15728640 | tf_op jit(solution)/shard_map/reduce_scatter | solution.py:321
  342.7 13.1 %copy-start.2 = (s32[8,128]{1,0:T(8,128)S(1)}, s32[8,128]{1,0:T(8,128)}, u32[]{:S(2)}) copy-start(s32[8,128]{1,0:T(8,128)} %copy-done.1) | copy-start | bytes 12292
Sparse Core Ops, SparseCore 0:
  10.9 115.0 all-gather.2
  161.7 64.0 reduce-scatter.2
  228.2 114.1 reduce-scatter.4

commit v9 on v8

--- a/solution.py
+++ b/solution.py
@@ -155,7 +155,7 @@
     rows, hidden_dim = hidden.shape
     model_dim = gate_proj.shape[1]
     capacity = rows // group
-    tile = 512
+    tile = 256
     whole = pl.BlockSpec((rows, hidden_dim), lambda d: (0, 0), pipeline_mode=pl.Buffered(1))
     return pl.pallas_call(
         returns_kernel,

time: 366 us -> 370 us (1.011)
  transfers between devices with their start and end apart: 5 -> 5, of which waited for: 3 -> 3; matrix products, arithmetic and copies ran while one was open for 1% -> 1% of each run, Pallas kernels for 19% -> 20%
where the time goes in v9:
time: 370 us; the launch traced here: 367 us
  waiting for transfers between devices  131 us (35%)
  Pallas kernels  121 us (33%)
  blocking collectives  76.7 us (21%)
  starting transfers between devices  15.1 us (4%)
  between operations  14.6 us (4%)
  other arithmetic  5.87 us (2%)
    all_gather x1, waiting for transfers between devices, local(): lax.all_gather(jnp.concatenate([tokens, cotangent])[None], 'expert', axis...  99.3 us
    pallas_call x2, Pallas kernels, expert_grads(): pl.pallas_call(functools.partial(grads_kernel, steps, sources, e, last),...  80.3 us
    all_to_all x1, blocking collectives, exchange(): lax.all_to_all(rows, 'expert', split_axis=0, concat_axis=0, tiled=True)  76.7 us
    all_to_all x2, waiting for transfers between devices, exchange(): lax.all_to_all(rows, 'expert', split_axis=0, concat_axis=0, tiled=True)  32.1 us
    pallas_call x2, Pallas kernels, expert_returns(): pl.pallas_call(returns_kernel, grid=(model_dim // tile,), in_specs=[whole...  27.9 us
    all_to_all x2, starting transfers between devices, exchange(): lax.all_to_all(rows, 'expert', split_axis=0, concat_axis=0, tiled=True)  14.8 us
    pallas_call x1, Pallas kernels, finish(): pl.pallas_call(functools.partial(finish_kernel, experts), grid=(steps,),...  12.3 us
  transfers between devices with their start and end apart: 5, of which 3 were waited for; matrix products, arithmetic and copies ran while one was open for 1% of the time, Pallas kernels for 20%

profile of v9, /device:TPU:32, one launch (start us, length us, event | category | flops | bytes accessed | tf_op | source)
XLA Modules:
  0.0 366.7 jit_solution(18346865355265644015)
XLA Ops:
  7.2 0.0 copy-start.3
  7.2 0.0 copy-start.4
  7.2 0.0 all-gather.3.cloned.1.call-start
  7.2 2.3 pad_maximum_fusion
  9.5 0.0 all-gather.3.cloned.1.call-update
  10.2 0.0 copy-done.3
  10.2 0.0 copy-start.1
  10.2 0.1 fusion.4
  10.3 0.0 copy-done.4
  10.4 0.4 copy-done.1
  10.8 0.1 select_reduce_fusion.1
  10.9 0.1 convolution_convert_fusion
  11.1 0.1 copy.17
  11.2 0.7 pad.4
  11.8 8.2 %all-to-all-start = ((f32[32,8,128]{2,1,0:T(8,128)}), f32[32,8,128]{2,1,0:T(8,128)S(1)}, u32[]{:S(2)}, u32[]{:S(2)}) async-start(f32[32,8,128]{2,1,0:T(8,128)} %pad.4), calls=%async_computation | async-start | bytes 262144 | tf_op jit(solution)/shard_map/all_to_all | solution.py:271
  20.1 0.0 reduce-scatter.3.cloned.1.call-start
  20.1 0.1 eq.96
  20.2 0.1 eq.100
  20.4 0.3 fusion.3
  20.8 0.4 fusion
  21.2 1.0 pad_maximum_fusion.2.refs_3_
  22.1 1.0 pad_maximum_fusion.1.refs_1_
  23.1 3.5 all-to-all-done.plan_ref
  26.7 0.0 copy-start
  26.7 99.3 %all-gather.3.cloned.1.call-done = bf16[8192,2048]{1,0:T(8,128)(2,1)} async-done(((bf16[256,2048]{1,0:T(8,128)(2,1)}), bf16[8192,2048]{1,0:T(8,128)(2,1)}) %all-gather.3.cloned.1.call-update) | async-done | bytes 33554448 | tf_op jit(solution)/shard_map/all_gather | solution.py:284
  125.9 0.0 copy-done
  125.9 35.6 %shard_map.127 = (bf16[4,2,512,768]{3,2,1,0:T(8,128)(2,1)}, bf16[768,768]{1,0:T(8,128)(2,1)}, bf16[768,768]{1,0:T(8,128)(2,1)}, bf16[768,768]{1,0:T(8,128)(2,1)}, bf16[768,2048]{1,0:T(8,128)(2,1)}) custom-call(f32[32,8,128]{2,1,0:T(8,128)} %copy-done, bf16[32,256,2048]{2,1,0:T(8,128)(2,1)} %bitcast.62, bf16[32,256,2048]{2,1,0:T(8,128)(2,1)} %bitcast.63, ...), custom_call_target="tpu_custom_call" | custom-call | flops 14495514624 | bytes 55967744 | tf_op jit(solution)/shard_map/pallas_call | solution.py:112
  161.5 0.0 reduce-scatter.3.cloned.1.call-update
  161.5 13.9 %shard_map.128 = bf16[32,48,2048]{2,1,0:T(8,128)(2,1)} custom-call(bf16[768,768]{1,0:T(8,128)(2,1)} %get-tuple-element.27.hidden_ref.refs_7_, bf16[768,768]{1,0:T(8,128)(2,1)} %get-tuple-element.28.pregate_ref, bf16[768,768]{1,0:T(8,128)(2,1)} %get-tuple-element.29.preup_ref, bf16[2,2048,768]{2,1,0:T(8,128)(2,1)} %gate_ref.3, bf16[2,2048,768]{2,1,0:T(8,128)(2,1)} %up_ref.3, ...), custom_call_target="tpu_custom_call" | custom-call | flops 724775731200 | bytes 19267584 | tf_op jit(solution)/shard_map/pallas_call | solution.py:160
  175.4 6.6 %all-to-all-start.1 = ((bf16[32,48,2048]{2,1,0:T(8,128)(2,1)}), bf16[32,48,2048]{2,1,0:T(8,128)(2,1)}, u32[]{:S(2)}, u32[]{:S(2)}) async-start(bf16[32,48,2048]{2,1,0:T(8,128)(2,1)} %shard_map.128), calls=%async_computation.1 | async-start | bytes 12582912 | tf_op jit(solution)/shard_map/all_to_all | solution.py:271
  182.0 0.2 reduce-scatter.5.cloned.1.call-start
  182.2 44.7 %shard_map.129 = (bf16[4,4,512,768]{3,2,1,0:T(8,128)(2,1)}, bf16[768,768]{1,0:T(8,128)(2,1)}, bf16[768,768]{1,0:T(8,128)(2,1)}, bf16[768,768]{1,0:T(8,128)(2,1)}) custom-call(f32[32,8,128]{2,1,0:T(8,128)} %copy-done, bf16[32,256,2048]{2,1,0:T(8,128)(2,1)} %bitcast.66, bf16[32,256,2048]{2,1,0:T(8,128)(2,1)} %bitcast.67, bf16[32,256,2048]{2,1,0:T(8,128)(2,1)} %bitcast.68, ...), custom_call_target="tpu_custom_call" | custom-call | flops 14495514624 | bytes 55967744 | tf_op jit(solution)/shard_map/pallas_call | solution.py:112
  227.0 0.0 reduce-scatter.5.cloned.1.call-update
  227.0 14.0 %shard_map.130 = bf16[32,48,2048]{2,1,0:T(8,128)(2,1)} custom-call(bf16[768,768]{1,0:T(8,128)(2,1)} %get-tuple-element.32.hidden_ref, bf16[768,768]{1,0:T(8,128)(2,1)} %get-tuple-element.33.pregate_ref, bf16[768,768]{1,0:T(8,128)(2,1)} %get-tuple-element.34.preup_ref, bf16[2,2048,768]{2,1,0:T(8,128)(2,1)} %gate_ref.3, bf16[2,2048,768]{2,1,0:T(8,128)(2,1)} %up_ref.3, ...), custom_call_target="tpu_custom_call" | custom-call | flops 724775731200 | bytes 19267584 | tf_op jit(solution)/shard_map/pallas_call | solution.py:160
  241.0 28.6 %all-to-all-done.1.refs_0_ = bf16[32,48,2048]{2,1,0:T(8,128)(2,1)} async-done(((bf16[32,48,2048]{2,1,0:T(8,128)(2,1)}), bf16[32,48,2048]{2,1,0:T(8,128)(2,1)}, u32[]{:S(2)}, u32[]{:S(2)}) %all-to-all-start.1) | async-done | bytes 6291488 | tf_op jit(solution)/shard_map/all_to_all | solution.py:271
  269.6 76.7 %all_to_all.15.refs_2_ = bf16[32,48,2048]{2,1,0:T(8,128)(2,1)} all-to-all(bf16[32,48,2048]{2,1,0:T(8,128)(2,1)} %shard_map.130), channel_id=1, replica_groups=mesh['dp'=4,'expert'=32] {'expert'}, dimensions={0} | all-to-all | bytes 12582912 | tf_op jit(solution)/shard_map/all_to_all | solution.py:271
  346.3 0.0 reduce-scatter.3.cloned.1.call-done
  346.3 0.0 reduce-scatter.5.cloned.1.call-done
  346.3 0.0 copy-start.2
  346.3 12.3 %shard_map.131 = (bf16[128,2048]{1,0:T(8,128)(2,1)}, bf16[128,2048]{1,0:T(8,128)(2,1)}, f32[2,32,1,128]{3,2,1,0:T(1,128)}, bf16[2,512,768]{2,1,0:T(8,128)(2,1)},...) custom-call(bf16[128,2048]{1,0:T(8,128)(2,1)} %cotangent_ref.1, ...), custom_call_target="tpu_custom_call" | custom-call | flops 4831838208 | bytes 23592960 | tf_op jit(solution)/shard_map/pallas_call | solution.py:234
  358.7 0.8 copy.18
  359.5 0.0 copy-done.2
  359.5 0.6 select_reduce_fusion
  (14 shorter events, 0.2 us)
Async XLA Ops:
  7.2 3.0 copy-start.3
  7.2 3.2 copy-start.4
  7.2 118.7 %all-gather.3.cloned.1.call-start = ((), (), s32[]{:S(2)}) async-start(), calls=%async_computation.7 | async-start | bytes 34603008 | tf_op jit(solution)/shard_map/all_gather | solution.py:284
  10.2 0.6 copy-start.1
  11.8 14.8 %all-to-all-start = ((f32[32,8,128]{2,1,0:T(8,128)}), f32[32,8,128]{2,1,0:T(8,128)S(1)}, u32[]{:S(2)}, u32[]{:S(2)}) async-start(f32[32,8,128]{2,1,0:T(8,128)} %pad.4), calls=%async_computation | async-start | bytes 262144 | tf_op jit(solution)/shard_map/all_to_all | solution.py:271
  20.1 326.3 %reduce-scatter.3.cloned.1.call-start = ((), (), s32[]{:S(2)}) async-start(), calls=%async_computation.5 | async-start | bytes 7864320 | tf_op jit(solution)/shard_map/reduce_scatter | solution.py:321
  26.7 99.3 %copy-start = (f32[32,8,128]{2,1,0:T(8,128)}, f32[32,8,128]{2,1,0:T(8,128)S(1)}, u32[]{:S(2)}) copy-start(f32[32,8,128]{2,1,0:T(8,128)S(1)} %all-to-all-done.plan_ref) | copy-start | bytes 393220
  175.4 94.2 %all-to-all-start.1 = ((bf16[32,48,2048]{2,1,0:T(8,128)(2,1)}), bf16[32,48,2048]{2,1,0:T(8,128)(2,1)}, u32[]{:S(2)}, u32[]{:S(2)}) async-start(bf16[32,48,2048]{2,1,0:T(8,128)(2,1)} %shard_map.128), calls=%async_computation.1 | async-start | bytes 12582912 | tf_op jit(solution)/shard_map/all_to_all | solution.py:271
  182.0 164.3 %reduce-scatter.5.cloned.1.call-start = ((), (), s32[]{:S(2)}) async-start(), calls=%async_computation.6 | async-start | bytes 15728640 | tf_op jit(solution)/shard_map/reduce_scatter | solution.py:321
  346.3 13.1 %copy-start.2 = (s32[8,128]{1,0:T(8,128)S(1)}, s32[8,128]{1,0:T(8,128)}, u32[]{:S(2)}) copy-start(s32[8,128]{1,0:T(8,128)} %copy-done.1) | copy-start | bytes 12292
Sparse Core Ops, SparseCore 0:
  10.9 115.0 all-gather.2
  161.7 64.0 reduce-scatter.2
  228.2 114.4 reduce-scatter.4
